TPU v7x, 32 devices: a whole 2x2x4 slice. The times are simulated.
32 devices in a mesh: grp: 2 (over y), gx: 4 (over z), gy: 2 (over x), sa: 2 (over core).
Axes of the slice: x: 2, y: 2, z: 4, core: 2. Of those that a mesh axis runs over, the one named last changes fastest.
Arguments:
- initial: float32 [6, 16, 64, 512], P('grp', None, 'gx', ('gy', 'sa')), parts along dimension 0, may hold values from 0 to 1
- logk: float32 [32, 64, 512], P('grp', 'gx', ('gy', 'sa')), parts along dimension 0, may hold values from -1 to 1
- direction: float32 [32, 64, 512], P('grp', 'gx', ('gy', 'sa')), parts along dimension 0, may hold values from -4 to 4
- face_speed: float32 [4, 16, 64, 512], P('grp', None, 'gx', ('gy', 'sa')), parts along dimension 0, may hold values from 0.04 to 0.16
- face_flags: int32 [4, 16, 64, 512], P('grp', None, 'gx', ('gy', 'sa')), parts along dimension 0, may hold values 0 or 1
- retard: float32 [3], replicated, may hold values from 1 to 3
- decay: float32 [3], replicated, may hold values from 0.05 to 0.7
- screen_cells: int32 [768, 32], P('grp'), parts along dimension 0, may hold values from 0 to 524287, as said below
- screen_count: int32 [768], P('grp'), parts along dimension 0, may hold values from 1 to 32, as said below
- well_weight: float32 [6, 384], P('grp'), parts along dimension 0, may hold values from 2000 to 32000
Outputs:
- hessian: float32 [32, 64, 512], P('grp', 'gx', ('gy', 'sa')), parts along dimension 0
There are 2 independent parts, one for each index of `grp`. A program takes and returns all parts, laid end to end along the dimension named above; an argument that names none is the same for every part. Nothing has to cross between parts.
Inputs may be any that keep to these rules, and one draw needn't show every extreme that they name: `screen_cells`: each well's 32 entries are cells in a row along x at one z and one y, flat index z * 64 * 512 + x * 512 + y; only the first screen_count entries of a well are used. `screen_count`: some well uses all 32 entries.
All inputs are finite; a program needn't handle non-finite values. No bound on the sum of `face_flags` on one device may be relied on, other than what follows from the above.
Results may differ from a plain program's by a relative error of at most 0.00002.
Values sent between devices are 32-bit elements; how exact they have to be, the bound alone decides.
No kernel may reach another device: no remote copies, remote signals or barrier semaphores. Data moves between devices by JAX's collectives and lax.ppermute only.
A program may use at most 128 MiB of HBM per device.

v0:
```python
import functools

import jax
import jax.numpy as jnp
from jax import lax
from jax.experimental import pallas as pl
from jax.experimental.pallas import tpu as pltpu
from jax.sharding import PartitionSpec as P

STEPS = 4
HALO = STEPS
RATE = 0.02
HALF_DT = 0.025
LANES = 128
GROUP = 16
RIGHT = 64
Y = ("gy", "sa")
VMEM_LIMIT = 40 * 1024 * 1024


def lane_of(shape):
    return lax.broadcasted_iota(jnp.int32, shape, len(shape) - 1)


def roll(value, shift, axis):
    return pltpu.roll(value, shift % value.shape[axis], axis)


def pack_edges(fields):
    lane = lane_of(fields[0].shape)
    packed = jnp.zeros_like(fields[0])
    for f, field in enumerate(fields):
        packed = jnp.where(lane // GROUP == f, roll(field, 8 + GROUP * f, 1), packed)
    return packed


def y_neighbours(value, strip, s):
    lane = lane_of(value.shape)
    after = jnp.where(lane == LANES - 1, roll(strip, 127 - (RIGHT + GROUP * s + 8), 1), roll(value, 127, 1))
    before = jnp.where(lane == 0, roll(strip, -(GROUP * s + 7), 1), roll(value, 1, 1))
    return after, before


def y_before(value, strip):
    return jnp.where(lane_of(value.shape) == 0, roll(strip, -7, 1), roll(value, 1, 1))


def y_after(value, strip, s):
    lane = lane_of(value.shape)
    return jnp.where(lane == LANES - 1, roll(strip, 127 - (RIGHT + GROUP * s + 8), 1), roll(value, 127, 1))


def z_pair(value):
    layers = value.shape[0]
    depth = lax.broadcasted_iota(jnp.int32, value.shape, 0)
    above = jnp.where(depth == layers - 1, value, roll(value, layers - 1, 0))
    below = jnp.where(depth == 0, value, roll(value, 1, 0))
    return above + below


def strip_retard(retard_ref, shape):
    place = lane_of(shape) % RIGHT // GROUP
    return jnp.where(place == 0, retard_ref[0], jnp.where(place == 1, retard_ref[1], retard_ref[2]))


def pack_kernel(initial_ref, logk_ref, direction_ref, speed_ref, flags_ref, f7_ref, e_ref, xa_ref, xb_ref, *, layers, width, species):
    plane = layers * width
    even = lax.rem(lax.axis_index("gx"), 2) == 0
    top, bottom = width - HALO, 0

    def row(x, carry):
        def take(ref, index):
            return ref[pl.ds(index * plane + x, layers, stride=width), :]

        fields = [take(initial_ref, s) for s in range(species)]
        conductance = jnp.exp(take(logk_ref, 0))
        fields += [conductance, conductance * take(direction_ref, 0)]
        for axis in range(2):
            speed = take(speed_ref, axis)
            fields.append(jnp.where(take(flags_ref, axis) == 1, speed, -speed))
        for f, field in enumerate(fields):
            f7_ref[x, f] = field
        e_ref[x] = pack_edges(fields)
        return carry

    lax.fori_loop(0, width, row, 0)
    count = species + 4
    start_a = jnp.where(even, top, bottom)
    start_b = jnp.where(even, bottom, top)
    for r in range(HALO):
        xa_ref[r, 0:count] = f7_ref[start_a + r]
        xb_ref[r, 0:count] = f7_ref[start_b + r]


def pack(initial, logk, direction, face_speed, face_flags):
    species, layers, width, _ = initial.shape
    flat = lambda a: a.reshape(-1, LANES)
    f32 = jnp.float32
    return pl.pallas_call(
        functools.partial(pack_kernel, layers=layers, width=width, species=species),
        out_shape=(
            jax.ShapeDtypeStruct((width, species + 4, layers, LANES), f32),
            jax.ShapeDtypeStruct((width, layers, LANES), f32),
            jax.ShapeDtypeStruct((HALO, species + 5, layers, LANES), f32),
            jax.ShapeDtypeStruct((HALO, species + 5, layers, LANES), f32),
        ),
        in_specs=[pl.BlockSpec(memory_space=pltpu.VMEM)] * 5,
        out_specs=[pl.BlockSpec(memory_space=pltpu.VMEM)] * 4,
        name="pack",
    )(flat(initial), flat(logk), flat(direction), flat(face_speed), flat(face_flags))


def strips_kernel(ea_ref, eb_ref, xa_in, xb_in, xa_ref, xb_ref, buf_a, buf_b, sem_a, sem_b, *, width, count):
    even_x = lax.rem(lax.axis_index("gx"), 2) == 0
    even_y = lax.rem(lax.axis_index(Y), 2) == 0
    start_a = jnp.where(even_x, width - HALO, 0)
    start_b = jnp.where(even_x, 0, width - HALO)
    for r in range(HALO):
        for start, buf in ((start_a, buf_a), (start_b, buf_b)):
            one, two = ea_ref[start + r], eb_ref[start + r]
            from_left = lane_of(one.shape) % GROUP < 8
            buf[r] = jnp.where(from_left == even_y, two, one)
    copies = [
        pltpu.make_async_copy(buf_a, xa_ref.at[:, count], sem_a),
        pltpu.make_async_copy(buf_b, xb_ref.at[:, count], sem_b),
    ]
    for copy in copies:
        copy.start()
    for copy in copies:
        copy.wait()


def add_strips(ea, eb, xa, xb):
    width, layers, _ = ea.shape
    buffer = pltpu.VMEM((HALO, layers, LANES), jnp.float32)
    return pl.pallas_call(
        functools.partial(strips_kernel, width=width, count=xa.shape[1] - 1),
        out_shape=(jax.ShapeDtypeStruct(xa.shape, xa.dtype), jax.ShapeDtypeStruct(xb.shape, xb.dtype)),
        in_specs=[pl.BlockSpec(memory_space=pltpu.VMEM)] * 2 + [pl.BlockSpec(memory_space=pl.ANY)] * 2,
        out_specs=[pl.BlockSpec(memory_space=pl.ANY)] * 2,
        input_output_aliases={2: 0, 3: 1},
        scratch_shapes=[buffer, buffer, pltpu.SemaphoreType.DMA, pltpu.SemaphoreType.DMA],
        name="corner_strips",
    )(ea, eb, xa, xb)


def well_rows(meta_ref):
    return [meta_ref[i : i + 1, :] for i in range(4)]


def forward_kernel(
    retard_ref, f7_ref, e_ref, ea_ref, eb_ref, xa_ref, xb_ref, meta_ref,
    partial_ref, px_ref, qx_ref, py_ref, qym_ref, d_ref, c_ref, jy_ref,
    k_ref, kd_ref, ux_ref, uy_ref, qy_ref, pym_ref, bx_ref, by_ref, bym_ref, t_ref, wide_ref,
    *, layers, width, species,
):
    f32 = jnp.float32
    rows = width + 2 * HALO
    shape = (layers, LANES)
    lane = lane_of(shape)
    gx, gy = lax.axis_index("gx"), lax.axis_index(Y)
    even_x, even_y = lax.rem(gx, 2) == 0, lax.rem(gy, 2) == 0
    total_x = width * lax.axis_size("gx")
    first_y, last_y = gy == 0, gy == lax.axis_size(Y) - 1
    column = lane % GROUP
    near = column < 8
    left = lane < RIGHT
    count = species + 4

    def place(r, fields, own_edges, outer_edges):
        left_strip = jnp.where(near, outer_edges, own_edges)
        right_strip = jnp.where(near, own_edges, outer_edges)
        for s in range(species):
            c_ref[0, r, s] = fields[s]
        c_ref[0, r, species] = jnp.where(left, left_strip, roll(right_strip, RIGHT, 1))
        for f, ref in enumerate((k_ref, kd_ref, ux_ref, uy_ref), species):
            ref[r, 0] = fields[f]
            index = GROUP * f + column
            ref[r, 1] = jnp.where(
                left,
                jnp.take_along_axis(left_strip, index, 1, mode="promise_in_bounds"),
                jnp.take_along_axis(right_strip, index, 1, mode="promise_in_bounds"),
            )

    def own_row(x, carry):
        one, two = ea_ref[x], eb_ref[x]
        outer = jnp.where(near == even_y, two, one)
        place(x + HALO, [f7_ref[x, f] for f in range(count)], e_ref[x], outer)
        return carry

    lax.fori_loop(0, width, own_row, 0)

    def halo_row(r, carry):
        for low in (True, False):
            from_a = even_x != low
            both = [jnp.where(from_a, xa_ref[r, f], xb_ref[r, f]) for f in range(count + 1)]
            place(r if low else r + HALO + width, both[:count], pack_edges(both[:count]), both[count])
        return carry

    lax.fori_loop(0, HALO, halo_row, 0)

    strip_mask = jnp.where(
        left, jnp.where(first_y & near, 0.0, 1.0), jnp.where(last_y & (column >= 7), 0.0, 1.0)
    ).astype(f32)
    main_mask = jnp.where(last_y & (lane == LANES - 1), 0.0, 1.0).astype(f32)

    def y_faces(r, carry):
        k4, kd4, u4 = k_ref[r, 1], kd_ref[r, 1], uy_ref[r, 1]
        half4 = HALF_DT * (k4 + roll(k4, 127, 1))
        p4 = (half4 + jnp.maximum(u4, 0.0)) * strip_mask
        q4 = (half4 - jnp.minimum(u4, 0.0)) * strip_mask
        b4 = HALF_DT * (kd4 + roll(kd4, 127, 1)) * strip_mask
        k, kd, u = k_ref[r, 0], kd_ref[r, 0], uy_ref[r, 0]
        half = HALF_DT * (k + y_after(k, k4, 0))
        p = (half + jnp.maximum(u, 0.0)) * main_mask
        q = (half - jnp.minimum(u, 0.0)) * main_mask
        b = HALF_DT * (kd + y_after(kd, kd4, 0)) * main_mask
        py_ref[r, 0], py_ref[r, 1] = p, p4
        qy_ref[r, 0], qy_ref[r, 1] = q, q4
        by_ref[r, 0], by_ref[r, 1] = b, b4
        qm, qm4 = y_before(q, q4), roll(q4, 1, 1)
        pym_ref[r, 0], pym_ref[r, 1] = y_before(p, p4), roll(p4, 1, 1)
        qym_ref[r, 0], qym_ref[r, 1] = qm, qm4
        bym_ref[r, 0], bym_ref[r, 1] = y_before(b, b4), roll(b4, 1, 1)
        d_ref[r, 0], d_ref[r, 1] = p + qm + 2 * RATE, p4 + qm4 + 2 * RATE
        return carry

    lax.fori_loop(0, rows, y_faces, 0)

    def x_faces(r, carry):
        x = gx * width + r - HALO
        mask = jnp.where((x >= 0) & (x + 1 < total_x), 1.0, 0.0).astype(f32)
        for i in range(2):
            u = ux_ref[r, i]
            half = HALF_DT * (k_ref[r, i] + k_ref[r + 1, i])
            p = (half + jnp.maximum(u, 0.0)) * mask
            q = (half - jnp.minimum(u, 0.0)) * mask
            px_ref[r, i] = p
            qx_ref[r, i] = q
            bx_ref[r, i] = HALF_DT * (kd_ref[r, i] + kd_ref[r + 1, i]) * mask
            d_ref[r, i] = d_ref[r, i] + p
            d_ref[r + 1, i] = d_ref[r + 1, i] + q
        return carry

    lax.fori_loop(0, rows - 1, x_faces, 0)

    strip_rate = strip_retard(retard_ref, shape)
    for m in range(STEPS):
        now, later = m % 2, (m + 1) % 2

        def step_row(r, carry, m=m, now=now, later=later):
            for s in (species,) + tuple(range(species)):
                i = 1 if s == species else 0
                rate = strip_rate if i else retard_ref[s]
                kept = rate - d_ref[r, i]
                upper, lower = qx_ref[r, i], px_ref[r - 1, i]
                after, before = qy_ref[r, i], pym_ref[r, i]

                def around(ref, slot):
                    value, strip = ref[slot, r, s], ref[slot, r, species]
                    if i:
                        return value, roll(value, 127, 1), roll(value, 1, 1)
                    return (value,) + y_neighbours(value, strip, s)

                def moved(ref, slot, value, yp, ym):
                    return (
                        kept * value
                        + upper * ref[slot, r + 1, s]
                        + lower * ref[slot, r - 1, s]
                        + after * yp
                        + before * ym
                        + RATE * z_pair(value)
                    )

                c, yp, ym = around(c_ref, m)
                jump = yp - c
                source = (
                    bx_ref[r, i] * (c_ref[m, r + 1, s] - c)
                    - bx_ref[r - 1, i] * (c - c_ref[m, r - 1, s])
                    + by_ref[r, i] * jump
                    - bym_ref[r, i] * (c - ym)
                )
                jy_ref[m, r, s] = jump
                if m + 1 < STEPS:
                    c_ref[m + 1, r, s] = moved(c_ref, m, c, yp, ym)
                if m > 0:
                    t, tp, tm = around(t_ref, now)
                    source = source + moved(t_ref, now, t, tp, tm)
                t_ref[later, r, s] = source
            return carry

        lax.fori_loop(m + 1, rows - 1 - m, step_row, 0)

    final = STEPS % 2
    depth, first, last, where_y = well_rows(meta_ref)
    wells = meta_ref.shape[1]
    own = lax.broadcasted_iota(jnp.int32, (LANES, wells), 0)
    own_hot = jnp.where(own == where_y, 1.0, 0.0).astype(jnp.bfloat16)
    strip_place = own % RIGHT // GROUP
    strip_col = own % GROUP + jnp.where(own < RIGHT, -8, 120)
    outside = (strip_col < 0) | (strip_col >= LANES)
    strip_hit = outside & (strip_col == where_y)
    for x in range(width):
        wide_ref[x, 0] = t_ref[final, x + HALO, species]
    layer = lax.broadcasted_iota(jnp.int32, (layers, wells), 0)
    in_layer = layer == depth
    for s in range(species):
        hot = jnp.concatenate(
            [own_hot, jnp.where(strip_hit & (strip_place == s), 1.0, 0.0).astype(jnp.bfloat16)], axis=0
        )
        total = jnp.zeros((layers, wells), f32)
        for part in range(2):
            half = width // 2
            main = t_ref[final, HALO + part * half : HALO + (part + 1) * half, s].reshape(half * layers, LANES)
            side = t_ref[final, HALO + part * half : HALO + (part + 1) * half, species].reshape(half * layers, LANES)
            both = jnp.concatenate([main, side], axis=1)
            picked = jnp.zeros((half * layers, wells), f32)
            for piece in range(3):
                coarse = both.astype(jnp.bfloat16)
                picked = picked + jnp.dot(coarse, hot, preferred_element_type=f32)
                both = both - coarse.astype(f32)
            picked = picked.reshape(half, layers, wells)
            for x in range(half):
                at = x + part * half
                inside = (first <= at) & (last >= at)
                total = total + jnp.where(inside & in_layer, picked[x], 0.0)
        partial_ref[s : s + 1, :] = jnp.sum(total, axis=0, keepdims=True)


def forward(retard, f7, e, ea, eb, xa, xb, meta):
    width, count, layers, _ = f7.shape
    species = count - 4
    rows = width + 2 * HALO
    f32 = jnp.float32
    coef = (rows, 2, layers, LANES)
    state = (rows, species + 1, layers, LANES)
    vmem = pl.BlockSpec(memory_space=pltpu.VMEM)
    return pl.pallas_call(
        functools.partial(forward_kernel, layers=layers, width=width, species=species),
        out_shape=(jax.ShapeDtypeStruct((species, meta.shape[1]), f32),)
        + (jax.ShapeDtypeStruct(coef, f32),) * 5
        + (jax.ShapeDtypeStruct((STEPS,) + state, f32),) * 2,
        in_specs=[pl.BlockSpec(memory_space=pltpu.SMEM)] + [vmem] * 7,
        out_specs=[vmem] * 8,
        scratch_shapes=[pltpu.VMEM(coef, f32)] * 9
        + [pltpu.VMEM((2,) + state, f32), pltpu.VMEM((width, 1, layers, LANES), f32)],
        compiler_params=pltpu.CompilerParams(vmem_limit_bytes=VMEM_LIMIT),
        name="forward_steps",
    )(retard, f7, e, ea, eb, xa, xb, meta)


def adjoint_kernel(
    retard_ref, decay_ref, weight_ref, meta_ref, px_ref, qx_ref, py_ref, qym_ref, d_ref, c_ref, jy_ref, f7_ref,
    partial_ref, *rest, layers, width, species, parts,
):
    others, out_ref, lam_ref, hx_ref, hy_ref, mask_ref = rest[:parts], *rest[parts:]
    f32, bf16 = jnp.float32, jnp.bfloat16
    rows = width + 2 * HALO
    shape = (layers, LANES)
    lane = lane_of(shape)
    gx, gy = lax.axis_index("gx"), lax.axis_index(Y)
    total_x = width * lax.axis_size("gx")
    depth, first, last, where_y = well_rows(meta_ref)
    wells = meta_ref.shape[1]

    layer = lax.broadcasted_iota(jnp.int32, (layers, wells), 0)
    in_layer = layer == depth
    for r in range(rows):
        x = r - HALO
        inside = (first <= x) & (last >= x) & in_layer
        mask_ref[r * layers : (r + 1) * layers, :] = jnp.where(inside, 1.0, 0.0).astype(bf16)

    counts = meta_ref[4:5, :].astype(f32)
    own = lax.broadcasted_iota(jnp.int32, (LANES, wells), 0)
    strip_place = own % RIGHT // GROUP
    strip_col = own % GROUP + jnp.where(own < RIGHT, -8, 120)
    strip_hit = strip_col == where_y
    own_hit = own == where_y
    targets = [own_hit] * species
    residuals = []
    for s in range(species):
        total = partial_ref[s : s + 1, :]
        for other in others:
            total = total + other[s : s + 1, :]
        rate = jnp.full((1, wells), retard_ref[s], f32)
        factor = jnp.exp(jnp.full((1, wells), -decay_ref[s], f32)) / rate
        factor = factor * factor
        factor = factor * factor
        residual = weight_ref[s : s + 1, :] * (total * factor) / counts
        residuals.append(residual / counts * factor)
    lam = jnp.zeros((rows * layers, (species + 1) * LANES), f32)
    for piece in range(3):
        coarse = [r.astype(bf16).astype(f32) for r in residuals]
        residuals = [r - q for r, q in zip(residuals, coarse)]
        blocks = [jnp.where(own_hit, q, 0.0).astype(bf16) for q in coarse]
        side = jnp.zeros((LANES, wells), f32)
        for s in range(species):
            side = jnp.where(strip_hit & (strip_place == s), coarse[s], side)
        spread = jnp.concatenate(blocks + [side.astype(bf16)], axis=0)
        lam = lam + lax.dot_general(
            mask_ref[...], spread, (((1,), (1,)), ((), ())), preferred_element_type=f32
        )
    for s in range(species + 1):
        lam_ref[0, :, s] = lam[:, s * LANES : (s + 1) * LANES].reshape(rows, layers, LANES)

    strip_rate = strip_retard(retard_ref, shape)
    for m in reversed(range(STEPS)):
        now, later = (STEPS - 1 - m) % 2, (STEPS - m) % 2
        low, high = STEPS - m, rows - (STEPS - m)

        def retreat_row(r, carry, m=m, now=now, later=later):
            for s in range(species + 1):
                i = 1 if s == species else 0
                value = lam_ref[now, r, s]
                if i:
                    yp, ym = roll(value, 127, 1), roll(value, 1, 1)
                else:
                    yp, ym = y_neighbours(value, lam_ref[now, r, species], s)
                rate = strip_rate if i else retard_ref[s]
                lam_ref[later, r, s] = (
                    (rate - d_ref[r, i]) * value
                    + px_ref[r, i] * lam_ref[now, r + 1, s]
                    + qx_ref[r - 1, i] * lam_ref[now, r - 1, s]
                    + py_ref[r, i] * yp
                    + qym_ref[r, i] * ym
                    + RATE * z_pair(value)
                )
            return carry

        def sense_row(r, carry, m=m, now=now):
            along_x = jnp.zeros(shape, f32)
            along_y = jnp.zeros(shape, f32)
            for s in range(species):
                value = lam_ref[now, r, s]
                along_x += (c_ref[m, r + 1, s] - c_ref[m, r, s]) * (lam_ref[now, r + 1, s] - value)
                along_y += jy_ref[m, r, s] * (y_after(value, lam_ref[now, r, species], s) - value)
            strip = lam_ref[now, r, species]
            side = jy_ref[m, r, species] * (roll(strip, 127, 1) - strip)
            if m + 1 < STEPS:
                along_x += hx_ref[r]
                along_y += hy_ref[r, 0]
                side += hy_ref[r, 1]
            hx_ref[r] = along_x
            hy_ref[r, 0] = along_y
            hy_ref[r, 1] = side
            return carry

        lax.fori_loop(HALO - 1, HALO + width, sense_row, 0)
        if m > 0:
            lax.fori_loop(low, high, retreat_row, 0)

    main_mask = jnp.where((gy == lax.axis_size(Y) - 1) & (lane == LANES - 1), 0.0, 1.0).astype(f32)
    side_mask = jnp.where((gy == 0) & (lane == 0), 0.0, 1.0).astype(f32)

    def finish(x, carry):
        r = x + HALO
        at = gx * width + x
        lower = jnp.where(at > 0, 1.0, 0.0).astype(f32)
        upper = jnp.where(at + 1 < total_x, 1.0, 0.0).astype(f32)
        along_y, strip = hy_ref[r, 0] * main_mask, hy_ref[r, 1]
        side = roll(strip, -7, 1)
        for s in range(1, species):
            side = side + roll(strip, -(GROUP * s + 7), 1)
        before = jnp.where(lane == 0, side * side_mask, roll(along_y, 1, 1))
        total = hx_ref[r] * upper + hx_ref[r - 1] * lower + along_y + before
        out_ref[pl.ds(x, layers, stride=width), :] = -HALF_DT * f7_ref[x, species] * total
        return carry

    lax.fori_loop(0, width, finish, 0)


def adjoint(retard, decay, weight, meta, coefs, c, jy, f7, partials):
    width, count, layers, _ = f7.shape
    species = count - 4
    rows = width + 2 * HALO
    f32 = jnp.float32
    vmem = pl.BlockSpec(memory_space=pltpu.VMEM)
    smem = pl.BlockSpec(memory_space=pltpu.SMEM)
    parts = len(partials) - 1
    return pl.pallas_call(
        functools.partial(adjoint_kernel, layers=layers, width=width, species=species, parts=parts),
        out_shape=jax.ShapeDtypeStruct((layers * width, LANES), f32),
        in_specs=[smem] * 2 + [vmem] * (2 + len(coefs) + 3 + len(partials)),
        out_specs=vmem,
        scratch_shapes=[
            pltpu.VMEM((2, rows, species + 1, layers, LANES), f32),
            pltpu.VMEM((rows, layers, LANES), f32),
            pltpu.VMEM((rows, 2, layers, LANES), f32),
            pltpu.VMEM((rows * layers, meta.shape[1]), jnp.bfloat16),
        ],
        compiler_params=pltpu.CompilerParams(vmem_limit_bytes=VMEM_LIMIT),
        name="adjoint_steps",
    )(retard, decay, weight, meta, *coefs, c, jy, f7, *partials)


def swaps(first, second, axis):
    count = lax.axis_size(axis)
    even = [p for i in range(0, count - 1, 2) for p in ((i, i + 1), (i + 1, i))]
    odd = [p for i in range(1, count - 1, 2) for p in ((i, i + 1), (i + 1, i))]
    return lax.ppermute(first, axis, even), lax.ppermute(second, axis, odd)


def from_others(value, axis, reach):
    count = lax.axis_size(axis)
    if count in (2, 4):
        return [lax.ppermute(value, axis, [(i, i ^ d) for i in range(count)]) for d in range(1, count)]
    return [
        lax.ppermute(value, axis, [(i, i + d) for i in range(count) if 0 <= i + d < count])
        for distance in range(1, min(reach, count - 1) + 1)
        for d in (distance, -distance)
    ]


def well_table(screen_cells, screen_count, row_start, col_start, total_x, total_y):
    start, second = screen_cells[:, 0], screen_cells[:, 1]
    plane = total_x * total_y
    depth = start // plane
    x = start % plane // total_y
    y = start % total_y
    end = x + (screen_count - 1) * ((second - start) // total_y)
    first, last = jnp.minimum(x, end) - row_start, jnp.maximum(x, end) - row_start
    zero = jnp.zeros_like(depth)
    return jnp.stack([depth, first, last, y - col_start, screen_count, zero, zero, zero])


def shards(
    initial, logk, direction, face_speed, face_flags, retard, decay, screen_cells, screen_count, well_weight
):
    species, layers, width, columns = initial.shape
    total_x = width * lax.axis_size("gx")
    total_y = columns * lax.axis_size(Y)
    meta = well_table(
        screen_cells, screen_count, lax.axis_index("gx") * width, lax.axis_index(Y) * columns, total_x, total_y
    )
    f7, e, xa, xb = pack(initial, logk, direction, face_speed, face_flags)
    ea, eb = swaps(e, e, Y)
    xa, xb = add_strips(ea, eb, xa, xb)
    xa, xb = swaps(xa, xb, "gx")
    partial, px, qx, py, qym, d, c, jy = forward(retard, f7, e, ea, eb, xa, xb, meta)
    reach = -(-(screen_cells.shape[1] - 1 + HALO) // width)
    partials = [partial] + from_others(partial, "gx", reach)
    hessian = adjoint(retard, decay, well_weight, meta, (px, qx, py, qym, d), c, jy, f7, partials)
    return hessian.reshape(layers, width, columns)


def solution(mesh):
    in_specs = (
        P("grp", None, "gx", Y),
        P("grp", "gx", Y),
        P("grp", "gx", Y),
        P("grp", None, "gx", Y),
        P("grp", None, "gx", Y),
        P(),
        P(),
        P("grp", None),
        P("grp"),
        P("grp", None),
    )
    return jax.shard_map(shards, mesh=mesh, in_specs=in_specs, out_specs=P("grp", "gx", Y), check_vma=False)
```

profile of v0, /device:TPU:0, one launch (start us, length us, event | category | flops | bytes accessed | tf_op | source)
XLA Modules:
  0.0 70.0 jit_solution(16888021863437358090)
XLA Ops:
  0.0 4.1 %pack.1 = (f32[16,7,16,128]{3,2,1,0:T(8,128)}, f32[16,16,128]{2,1,0:T(8,128)}, f32[4,8,16,128]{3,2,1,0:T(8,128)}, f32[4,8,16,128]{3,2,1,0:T(8,128)}) custom-call(f32[768,128]{1,0:T(8,128)} %bitcast.19, f32[256,128]{1,0:T(8,128)} %bitcast.22, f32[256,128]{1,0:T(8,128)} %bitcast.23, f32[512,128]{1,0:T(8,128)} %bitcast.20, s32[512,128]{1,0:T(8,128)} %bitcast.21), custom_call_target="tpu_custom_call" | custom-call | tf_op jit(solution)/shard_map/pack/pallas_call | solution.py:99
  4.1 0.7 collective-permute-start.1
  4.8 4.4 %collective-permute-start = (f32[16,16,128]{2,1,0:T(8,128)}, f32[16,16,128]{2,1,0:T(8,128)S(1)}, u32[]{:S(2)}, u32[]{:S(2)}) collective-permute-start(f32[16,16,128]{2,1,0:T(8,128)} %get-tuple-element.20.e_ref), channel_id=1, source_target_pairs={{0,1},{1,0},{2,3},{3,2},{4,5},{5,4},{6,7},{7,6},{8,9},{9,8},{10,11... | collective-permute-start | bytes 393224 | tf_op jit(solution)/shard_map/ppermute | solution.py:500
  9.1 0.8 %slice_reduce_fusion.1 = (s32[384]{0:T(512)S(1)}, s32[384]{0:T(512)S(1)}) fusion(s32[384,32]{0,1:T(8,128)} %param.17), kind=kLoop, calls=%fused_computation.32 | loop fusion | bytes 6144 | tf_op jit(solution)/shard_map/slice | solution.py:515
  9.9 0.7 %fusion.1 = (s32[384]{0:T(512)S(1)}, s32[384]{0:T(512)S(1)}) fusion(s32[]{:T(128)S(6)} %mul.13, s32[384]{0:T(512)S(1)} %get-tuple-element.33, s32[384]{0:T(512)S(1)} %get-tuple-element.34, s32[384]{0:T(512)} %param.18), kind=kLoop, calls=%fused_computation.20 | loop fusion | flops 18048 | bytes 7684 | tf_op jit(solution)/shard_map/sub | solution.py:521
  10.7 0.6 copy-done.1
  11.3 1.6 %corner_strips.1 = (f32[4,8,16,128]{3,2,1,0:T(8,128)}, f32[4,8,16,128]{3,2,1,0:T(8,128)}) custom-call(f32[16,16,128]{2,1,0:T(8,128)} %copy-done.3, f32[16,16,128]{2,1,0:T(8,128)} %copy-done.1, f32[4,8,16,128]{3,2,1,0:T(8,128)} %get-tuple-element.21.xa_in, f32[4,8,16,128]{3,2,1,0:T(8,128)} %get-tuple-element.22.xb_in), custom_call_target="tpu_custom_call", output_to_operand_aliasing={{0}: (2, {}), {1}: (3, {})} | custom-call | tf_op jit(solution)/shard_map/corner_strips/pallas_call | solution.py:136
  13.0 1.6 %collective-permute-start.2 = (f32[4,8,16,128]{3,2,1,0:T(8,128)}, f32[4,8,16,128]{3,2,1,0:T(8,128)S(1)}, u32[]{:S(2)}, u32[]{:S(2)}) collective-permute-start(f32[4,8,16,128]{3,2,1,0:T(8,128)} %get-tuple-element.23), channel_id=1, source_target_pairs={{0,4},{4,0},{8,12},{12,8},{1,5},{5,1},{9,13},{13,9},{2,6},{6,2},{1... | collective-permute-start | bytes 786440 | tf_op jit(solution)/shard_map/ppermute | solution.py:500
  14.6 0.7 collective-permute-start.3
  15.3 0.7 stack.19
  16.0 0.7 %fusion.8 = (s32[1,384]{1,0:T(1,128)S(1)}, s32[1,384]{1,0:T(1,128)S(1)}) fusion(s32[]{:T(128)S(6)} %mul.15, s32[384,32]{0,1:T(8,128)} %param.17), kind=kLoop, calls=%fused_computation.29 | loop fusion | flops 9216 | bytes 4612 | tf_op jit(solution)/shard_map/sub | solution.py:523
  16.8 5.3 %collective-permute-done.2.xa_ref = f32[4,8,16,128]{3,2,1,0:T(8,128)S(1)} collective-permute-done((f32[4,8,16,128]{3,2,1,0:T(8,128)}, f32[4,8,16,128]{3,2,1,0:T(8,128)S(1)}, u32[]{:S(2)}, u32[]{:S(2)}) %collective-permute-start.2) | collective-permute-done | bytes 262176 | tf_op jit(solution)/shard_map/ppermute | solution.py:500
  22.1 1.2 %copy-done = f32[16,7,16,128]{3,2,1,0:T(8,128)S(1)} copy-done((f32[16,7,16,128]{3,2,1,0:T(8,128)S(1)}, f32[16,7,16,128]{3,2,1,0:T(8,128)}, u32[]{:S(2)}) %copy-start) | copy-done | bytes 917528
  23.3 0.9 %copy-done.2 = f32[16,16,128]{2,1,0:T(8,128)S(1)} copy-done((f32[16,16,128]{2,1,0:T(8,128)S(1)}, f32[16,16,128]{2,1,0:T(8,128)}, u32[]{:S(2)}) %copy-start.2) | copy-done | bytes 131096
  24.2 0.9 %copy-done.4 = f32[16,16,128]{2,1,0:T(8,128)S(1)} copy-done((f32[16,16,128]{2,1,0:T(8,128)S(1)}, f32[16,16,128]{2,1,0:T(8,128)}, u32[]{:S(2)}) %copy-start.4) | copy-done | bytes 131096
  25.1 0.9 %copy-done.5 = f32[16,16,128]{2,1,0:T(8,128)S(1)} copy-done((f32[16,16,128]{2,1,0:T(8,128)S(1)}, f32[16,16,128]{2,1,0:T(8,128)}, u32[]{:S(2)}) %copy-start.5) | copy-done | bytes 131096
  26.0 0.7 copy-done.7
  26.7 17.7 %forward_steps.1 = (f32[3,384]{1,0:T(4,128)S(1)}, f32[24,2,16,128]{3,2,1,0:T(8,128)S(1)}, f32[24,2,16,128]{3,2,1,0:T(8,128)S(1)}, f32[24,2,16,128]{3,2,1,0:T(8,1...) custom-call(f32[3]{0:T(128)S(1)} %copy-done.7, ...), custom_call_target="tpu_custom_call" | custom-call | tf_op jit(solution)/shard_map/forward_steps/pallas_call | solution.py:338
  44.4 3.7 %collective-permute-start.6 = (f32[3,384]{1,0:T(4,128)S(1)}, f32[3,384]{1,0:T(4,128)S(1)}, u32[]{:S(2)}, u32[]{:S(2)}) collective-permute-start(f32[3,384]{1,0:T(4,128)S(1)} %get-tuple-element.32.partial_ref), channel_id=1, source_target_pairs={{0,12},{4,8},{8,4},{12,0},{1,13},{5,9},{9,5},{13,1},{2,14},{6,10},... | collective-permute-start | bytes 13832 | tf_op jit(solution)/shard_map/ppermute | solution.py:506
  48.0 2.8 %collective-permute-start.5 = (f32[3,384]{1,0:T(4,128)S(1)}, f32[3,384]{1,0:T(4,128)S(1)}, u32[]{:S(2)}, u32[]{:S(2)}) collective-permute-start(f32[3,384]{1,0:T(4,128)S(1)} %get-tuple-element.32.partial_ref), channel_id=1, source_target_pairs={{0,8},{4,12},{8,0},{12,4},{1,9},{5,13},{9,1},{13,5},{2,10},{6,14},... | collective-permute-start | bytes 13832 | tf_op jit(solution)/shard_map/ppermute | solution.py:506
  50.8 0.5 collective-permute-start.4
  51.3 1.2 %collective-permute-done.5.rest_1_ = f32[3,384]{1,0:T(4,128)S(1)} collective-permute-done((f32[3,384]{1,0:T(4,128)S(1)}, f32[3,384]{1,0:T(4,128)S(1)}, u32[]{:S(2)}, u32[]{:S(2)}) %collective-permute-start.5) | collective-permute-done | bytes 4640 | tf_op jit(solution)/shard_map/ppermute | solution.py:506
  52.6 1.9 %collective-permute-done.4.rest_0_ = f32[3,384]{1,0:T(4,128)S(1)} collective-permute-done((f32[3,384]{1,0:T(4,128)S(1)}, f32[3,384]{1,0:T(4,128)S(1)}, u32[]{:S(2)}, u32[]{:S(2)}) %collective-permute-start.4) | collective-permute-done | bytes 4640 | tf_op jit(solution)/shard_map/ppermute | solution.py:506
  54.5 15.6 %adjoint_steps.1 = f32[256,128]{1,0:T(8,128)} custom-call(f32[3]{0:T(128)S(1)} %copy-done.7, f32[3]{0:T(128)S(1)} %copy-done.8, f32[3,384]{1,0:T(4,128)S(1)} %copy-done.6, s32[8,384]{1,0:T(8,128)S(1)} %stack.21.meta_ref, f32[24,2,16,128]{3,2,1,0:T(8,128)S(1)} %get-tuple-element.25.px_ref, f32[24,2,16,128]{3,2,1,0:T(8,128)S(1)} %get-tuple-element.26.qx_ref, ...), custom_call_target="tpu_custom_call" | custom-call | tf_op jit(solution)/shard_map/adjoint_steps/pallas_call | solution.py:480
  (22 shorter events, 0.1 us)
Async XLA Ops:
  0.0 54.5 %copy-start.6 = (f32[3,384]{1,0:T(4,128)S(1)}, f32[3,384]{1,0:T(4,128)}, u32[]{:S(2)}) copy-start(f32[3,384]{1,0:T(4,128)} %weight_ref.1) | copy-start | bytes 13828
  0.0 54.5 %copy-start.8 = (f32[3]{0:T(128)S(1)}, f32[3]{0:T(128)}, u32[]{:S(2)}) copy-start(f32[3]{0:T(128)} %decay_ref.1) | copy-start | bytes 40
  4.1 6.5 %collective-permute-start.1 = (f32[16,16,128]{2,1,0:T(8,128)}, f32[16,16,128]{2,1,0:T(8,128)S(1)}, u32[]{:S(2)}, u32[]{:S(2)}) collective-permute-start(f32[16,16,128]{2,1,0:T(8,128)} %get-tuple-element.20.e_ref), channel_id=1, source_target_pairs={{1,2},{2,1},{5,6},{6,5},{9,10},{10,9},{13,14},{14,13},{17,18},{18,... | collective-permute-start | bytes 393224 | tf_op jit(solution)/shard_map/ppermute | solution.py:500
  4.8 5.9 %collective-permute-start = (f32[16,16,128]{2,1,0:T(8,128)}, f32[16,16,128]{2,1,0:T(8,128)S(1)}, u32[]{:S(2)}, u32[]{:S(2)}) collective-permute-start(f32[16,16,128]{2,1,0:T(8,128)} %get-tuple-element.20.e_ref), channel_id=1, source_target_pairs={{0,1},{1,0},{2,3},{3,2},{4,5},{5,4},{6,7},{7,6},{8,9},{9,8},{10,11... | collective-permute-start | bytes 393224 | tf_op jit(solution)/shard_map/ppermute | solution.py:500
  10.6 0.6 copy-start.1
  10.7 0.7 copy-start.3
  13.0 9.2 %collective-permute-start.2 = (f32[4,8,16,128]{3,2,1,0:T(8,128)}, f32[4,8,16,128]{3,2,1,0:T(8,128)S(1)}, u32[]{:S(2)}, u32[]{:S(2)}) collective-permute-start(f32[4,8,16,128]{3,2,1,0:T(8,128)} %get-tuple-element.23), channel_id=1, source_target_pairs={{0,4},{4,0},{8,12},{12,8},{1,5},{5,1},{9,13},{13,9},{2,6},{6,2},{1... | collective-permute-start | bytes 786440 | tf_op jit(solution)/shard_map/ppermute | solution.py:500
  14.6 7.5 %collective-permute-start.3 = (f32[4,8,16,128]{3,2,1,0:T(8,128)}, f32[4,8,16,128]{3,2,1,0:T(8,128)S(1)}, u32[]{:S(2)}, u32[]{:S(2)}) collective-permute-start(f32[4,8,16,128]{3,2,1,0:T(8,128)} %get-tuple-element.24), channel_id=1, source_target_pairs={{4,8},{8,4},{5,9},{9,5},{6,10},{10,6},{7,11},{11,7},{20,24},{24,20... | collective-permute-start | bytes 786440 | tf_op jit(solution)/shard_map/ppermute | solution.py:500
  22.1 1.2 %copy-start = (f32[16,7,16,128]{3,2,1,0:T(8,128)S(1)}, f32[16,7,16,128]{3,2,1,0:T(8,128)}, u32[]{:S(2)}) copy-start(f32[16,7,16,128]{3,2,1,0:T(8,128)} %get-tuple-element.19.f7_ref) | copy-start | bytes 2752516
  23.3 0.9 %copy-start.2 = (f32[16,16,128]{2,1,0:T(8,128)S(1)}, f32[16,16,128]{2,1,0:T(8,128)}, u32[]{:S(2)}) copy-start(f32[16,16,128]{2,1,0:T(8,128)} %copy-done.1) | copy-start | bytes 393220
  24.2 0.9 %copy-start.4 = (f32[16,16,128]{2,1,0:T(8,128)S(1)}, f32[16,16,128]{2,1,0:T(8,128)}, u32[]{:S(2)}) copy-start(f32[16,16,128]{2,1,0:T(8,128)} %copy-done.3) | copy-start | bytes 393220
  25.1 0.9 %copy-start.5 = (f32[16,16,128]{2,1,0:T(8,128)S(1)}, f32[16,16,128]{2,1,0:T(8,128)}, u32[]{:S(2)}) copy-start(f32[16,16,128]{2,1,0:T(8,128)} %get-tuple-element.20.e_ref) | copy-start | bytes 393220
  26.0 0.7 copy-start.7
  44.4 7.0 %collective-permute-start.6 = (f32[3,384]{1,0:T(4,128)S(1)}, f32[3,384]{1,0:T(4,128)S(1)}, u32[]{:S(2)}, u32[]{:S(2)}) collective-permute-start(f32[3,384]{1,0:T(4,128)S(1)} %get-tuple-element.32.partial_ref), channel_id=1, source_target_pairs={{0,12},{4,8},{8,4},{12,0},{1,13},{5,9},{9,5},{13,1},{2,14},{6,10},... | collective-permute-start | bytes 13832 | tf_op jit(solution)/shard_map/ppermute | solution.py:506
  48.0 4.5 %collective-permute-start.5 = (f32[3,384]{1,0:T(4,128)S(1)}, f32[3,384]{1,0:T(4,128)S(1)}, u32[]{:S(2)}, u32[]{:S(2)}) collective-permute-start(f32[3,384]{1,0:T(4,128)S(1)} %get-tuple-element.32.partial_ref), channel_id=1, source_target_pairs={{0,8},{4,12},{8,0},{12,4},{1,9},{5,13},{9,1},{13,5},{2,10},{6,14},... | collective-permute-start | bytes 13832 | tf_op jit(solution)/shard_map/ppermute | solution.py:506
  50.8 3.6 %collective-permute-start.4 = (f32[3,384]{1,0:T(4,128)S(1)}, f32[3,384]{1,0:T(4,128)S(1)}, u32[]{:S(2)}, u32[]{:S(2)}) collective-permute-start(f32[3,384]{1,0:T(4,128)S(1)} %get-tuple-element.32.partial_ref), channel_id=1, source_target_pairs={{0,4},{4,0},{8,12},{12,8},{1,5},{5,1},{9,13},{13,9},{2,6},{6,2},{1... | collective-permute-start | bytes 13832 | tf_op jit(solution)/shard_map/ppermute | solution.py:506
where the time goes:
time: 70.5 us; the launch traced here: 70 us
  Pallas kernels  39 us (55%)
  starting transfers between devices  14.3 us (20%)
  waiting for transfers between devices  8.49 us (12%)
  local copies, waits for them, and re-layouts  6.76 us (10%)
  other arithmetic  1.45 us (2%)
    pallas_call x1, Pallas kernels, forward(): pl.pallas_call(functools.partial(forward_kernel, layers=layers, width=wid...  17.7 us
    pallas_call x1, Pallas kernels, adjoint(): pl.pallas_call(functools.partial(adjoint_kernel, layers=layers, width=wid...  15.6 us
    ppermute x4, starting transfers between devices, swaps(): return (lax.ppermute(first, axis, even), lax.ppermute(second, axis, odd))  7.32 us
    ppermute x3, starting transfers between devices, from_others(): lax.ppermute(value, axis, [(i, i ^ d) for i in range(count)])  6.95 us
    ppermute x4, waiting for transfers between devices, swaps(): return (lax.ppermute(first, axis, even), lax.ppermute(second, axis, odd))  5.35 us
    unnamed x18, local copies, waits for them, and re-layouts  5.23 us
    pallas_call x1, Pallas kernels, pack(): pl.pallas_call(functools.partial(pack_kernel, layers=layers, width=width,...  4.09 us
    ppermute x3, waiting for transfers between devices, from_others(): lax.ppermute(value, axis, [(i, i ^ d) for i in range(count)])  3.14 us
  transfers between devices with their start and end apart: 7, of which 3 were waited for; matrix products, arithmetic and copies ran while one was open for 4% of the time, Pallas kernels for 0%

commit v1 on v0

--- a/solution.py
+++ b/solution.py
@@ -15,7 +15,7 @@
 GROUP = 16
 RIGHT = 64
 Y = ("gy", "sa")
-VMEM_LIMIT = 40 * 1024 * 1024
+MIB = 1024 * 1024
 
 
 def lane_of(shape):
@@ -83,7 +83,7 @@
         e_ref[x] = pack_edges(fields)
         return carry
 
-    lax.fori_loop(0, width, row, 0)
+    lax.fori_loop(0, width, row, 0, unroll=True)
     count = species + 4
     start_a = jnp.where(even, top, bottom)
     start_b = jnp.where(even, bottom, top)
@@ -106,6 +106,7 @@
         ),
         in_specs=[pl.BlockSpec(memory_space=pltpu.VMEM)] * 5,
         out_specs=[pl.BlockSpec(memory_space=pltpu.VMEM)] * 4,
+        compiler_params=pltpu.CompilerParams(vmem_limit_bytes=4 * MIB),
         name="pack",
     )(flat(initial), flat(logk), flat(direction), flat(face_speed), flat(face_flags))
 
@@ -140,6 +141,7 @@
         out_specs=[pl.BlockSpec(memory_space=pl.ANY)] * 2,
         input_output_aliases={2: 0, 3: 1},
         scratch_shapes=[buffer, buffer, pltpu.SemaphoreType.DMA, pltpu.SemaphoreType.DMA],
+        compiler_params=pltpu.CompilerParams(vmem_limit_bytes=2 * MIB),
         name="corner_strips",
     )(ea, eb, xa, xb)
 
@@ -151,7 +153,7 @@
 def forward_kernel(
     retard_ref, f7_ref, e_ref, ea_ref, eb_ref, xa_ref, xb_ref, meta_ref,
     partial_ref, px_ref, qx_ref, py_ref, qym_ref, d_ref, c_ref, jy_ref,
-    k_ref, kd_ref, ux_ref, uy_ref, qy_ref, pym_ref, bx_ref, by_ref, bym_ref, t_ref, wide_ref,
+    k_ref, kd_ref, ux_ref, uy_ref, qy_ref, pym_ref, bx_ref, by_ref, bym_ref, t_ref,
     *, layers, width, species,
 ):
     f32 = jnp.float32
@@ -188,7 +190,7 @@
         place(x + HALO, [f7_ref[x, f] for f in range(count)], e_ref[x], outer)
         return carry
 
-    lax.fori_loop(0, width, own_row, 0)
+    lax.fori_loop(0, width, own_row, 0, unroll=True)
 
     def halo_row(r, carry):
         for low in (True, False):
@@ -197,7 +199,7 @@
             place(r if low else r + HALO + width, both[:count], pack_edges(both[:count]), both[count])
         return carry
 
-    lax.fori_loop(0, HALO, halo_row, 0)
+    lax.fori_loop(0, HALO, halo_row, 0, unroll=True)
 
     strip_mask = jnp.where(
         left, jnp.where(first_y & near, 0.0, 1.0), jnp.where(last_y & (column >= 7), 0.0, 1.0)
@@ -225,7 +227,7 @@
         d_ref[r, 0], d_ref[r, 1] = p + qm + 2 * RATE, p4 + qm4 + 2 * RATE
         return carry
 
-    lax.fori_loop(0, rows, y_faces, 0)
+    lax.fori_loop(0, rows, y_faces, 0, unroll=True)
 
     def x_faces(r, carry):
         x = gx * width + r - HALO
@@ -242,7 +244,7 @@
             d_ref[r + 1, i] = d_ref[r + 1, i] + q
         return carry
 
-    lax.fori_loop(0, rows - 1, x_faces, 0)
+    lax.fori_loop(0, rows - 1, x_faces, 0, unroll=True)
 
     strip_rate = strip_retard(retard_ref, shape)
     for m in range(STEPS):
@@ -289,7 +291,7 @@
                 t_ref[later, r, s] = source
             return carry
 
-        lax.fori_loop(m + 1, rows - 1 - m, step_row, 0)
+        lax.fori_loop(m + 1, rows - 1 - m, step_row, 0, unroll=True)
 
     final = STEPS % 2
     depth, first, last, where_y = well_rows(meta_ref)
@@ -300,8 +302,6 @@
     strip_col = own % GROUP + jnp.where(own < RIGHT, -8, 120)
     outside = (strip_col < 0) | (strip_col >= LANES)
     strip_hit = outside & (strip_col == where_y)
-    for x in range(width):
-        wide_ref[x, 0] = t_ref[final, x + HALO, species]
     layer = lax.broadcasted_iota(jnp.int32, (layers, wells), 0)
     in_layer = layer == depth
     for s in range(species):
@@ -343,8 +343,8 @@
         in_specs=[pl.BlockSpec(memory_space=pltpu.SMEM)] + [vmem] * 7,
         out_specs=[vmem] * 8,
         scratch_shapes=[pltpu.VMEM(coef, f32)] * 9
-        + [pltpu.VMEM((2,) + state, f32), pltpu.VMEM((width, 1, layers, LANES), f32)],
-        compiler_params=pltpu.CompilerParams(vmem_limit_bytes=VMEM_LIMIT),
+        + [pltpu.VMEM((2,) + state, f32)],
+        compiler_params=pltpu.CompilerParams(vmem_limit_bytes=24 * MIB),
         name="forward_steps",
     )(retard, f7, e, ea, eb, xa, xb, meta)
 
@@ -445,9 +445,9 @@
             hy_ref[r, 1] = side
             return carry
 
-        lax.fori_loop(HALO - 1, HALO + width, sense_row, 0)
+        lax.fori_loop(HALO - 1, HALO + width, sense_row, 0, unroll=True)
         if m > 0:
-            lax.fori_loop(low, high, retreat_row, 0)
+            lax.fori_loop(low, high, retreat_row, 0, unroll=True)
 
     main_mask = jnp.where((gy == lax.axis_size(Y) - 1) & (lane == LANES - 1), 0.0, 1.0).astype(f32)
     side_mask = jnp.where((gy == 0) & (lane == 0), 0.0, 1.0).astype(f32)
@@ -488,7 +488,7 @@
             pltpu.VMEM((rows, 2, layers, LANES), f32),
             pltpu.VMEM((rows * layers, meta.shape[1]), jnp.bfloat16),
         ],
-        compiler_params=pltpu.CompilerParams(vmem_limit_bytes=VMEM_LIMIT),
+        compiler_params=pltpu.CompilerParams(vmem_limit_bytes=16 * MIB),
         name="adjoint_steps",
     )(retard, decay, weight, meta, *coefs, c, jy, f7, *partials)
 

time: 70.5 us -> 47.8 us (0.68)
  Pallas kernels: 39 us -> 16.5 us
    pallas_call x1, Pallas kernels: 15.6 us -> 6.4 us  [adjoint(): pl.pallas_call(functools.partial(adjoint_kernel, layers=layers, width=wid...]
    pallas_call x1, Pallas kernels: 17.7 us -> 9.41 us  [forward(): pl.pallas_call(functools.partial(forward_kernel, layers=layers, width=wid...]
    pallas_call x1, Pallas kernels: 4.09 us -> 0.62 us  [pack(): pl.pallas_call(functools.partial(pack_kernel, layers=layers, width=width,...]
    pallas_call x1, Pallas kernels: 1.63 us -> 0.07 us  [add_strips(): pl.pallas_call(functools.partial(strips_kernel, width=width, count=xa.sha...]
    unnamed x18 -> x16, local copies, waits for them, and re-layouts: 5.23 us -> 5.39 us
  transfers between devices with their start and end apart: 7 -> 7, of which waited for: 3 -> 3; matrix products, arithmetic and copies ran while one was open for 4% -> 6% of each run, Pallas kernels for 0% -> 0%
where the time goes in v1:
time: 47.8 us; the launch traced here: 47.4 us
  Pallas kernels  16.5 us (35%)
  starting transfers between devices  13.8 us (29%)
  waiting for transfers between devices  8.61 us (18%)
  local copies, waits for them, and re-layouts  6.92 us (14%)
  other arithmetic  1.45 us (3%)
    pallas_call x1, Pallas kernels, forward(): pl.pallas_call(functools.partial(forward_kernel, layers=layers, width=wid...  9.41 us
    ppermute x4, starting transfers between devices, swaps(): return (lax.ppermute(first, axis, even), lax.ppermute(second, axis, odd))  7.32 us
    ppermute x3, starting transfers between devices, from_others(): lax.ppermute(value, axis, [(i, i ^ d) for i in range(count)])  6.52 us
    pallas_call x1, Pallas kernels, adjoint(): pl.pallas_call(functools.partial(adjoint_kernel, layers=layers, width=wid...  6.4 us
    unnamed x16, local copies, waits for them, and re-layouts  5.39 us
    ppermute x4, waiting for transfers between devices, swaps(): return (lax.ppermute(first, axis, even), lax.ppermute(second, axis, odd))  5.38 us
    ppermute x3, waiting for transfers between devices, from_others(): lax.ppermute(value, axis, [(i, i ^ d) for i in range(count)])  3.23 us
  transfers between devices with their start and end apart: 7, of which 3 were waited for; matrix products, arithmetic and copies ran while one was open for 6% of the time, Pallas kernels for 0%

profile of v1, /device:TPU:0, one launch (start us, length us, event | category | flops | bytes accessed | tf_op | source)
XLA Modules:
  0.0 47.4 jit_solution(11425171397788393319)
XLA Ops:
  0.0 1.0 %copy-done = f32[3,16,16,128]{3,2,1,0:T(8,128)S(1)} copy-done((f32[3,16,16,128]{3,2,1,0:T(8,128)S(1)}, f32[3,16,16,128]{3,2,1,0:T(8,128)}, u32[]{:S(2)}) %copy-start) | copy-done | bytes 393240
  1.0 0.9 %copy-done.1 = f32[2,16,16,128]{3,2,1,0:T(8,128)S(1)} copy-done((f32[2,16,16,128]{3,2,1,0:T(8,128)S(1)}, f32[2,16,16,128]{3,2,1,0:T(8,128)}, u32[]{:S(2)}) %copy-start.1) | copy-done | bytes 262168
  2.0 0.9 %copy-done.2 = s32[2,16,16,128]{3,2,1,0:T(8,128)S(1)} copy-done((s32[2,16,16,128]{3,2,1,0:T(8,128)S(1)}, s32[2,16,16,128]{3,2,1,0:T(8,128)}, u32[]{:S(2)}) %copy-start.2) | copy-done | bytes 262168
  2.9 0.9 %copy-done.3 = f32[16,16,128]{2,1,0:T(8,128)S(1)} copy-done((f32[16,16,128]{2,1,0:T(8,128)S(1)}, f32[16,16,128]{2,1,0:T(8,128)}, u32[]{:S(2)}) %copy-start.3) | copy-done | bytes 131096
  3.8 0.9 %copy-done.4 = f32[16,16,128]{2,1,0:T(8,128)S(1)} copy-done((f32[16,16,128]{2,1,0:T(8,128)S(1)}, f32[16,16,128]{2,1,0:T(8,128)}, u32[]{:S(2)}) %copy-start.4) | copy-done | bytes 131096
  4.7 0.6 %pack.1 = (f32[16,7,16,128]{3,2,1,0:T(8,128)S(1)}, f32[16,16,128]{2,1,0:T(8,128)S(1)}, f32[4,8,16,128]{3,2,1,0:T(8,128)S(1)}, f32[4,8,16,128]{3,2,1,0:T(8,128)S(1)}) custom-call(f32[768,128]{1,0:T(8,128)S(1)} %bitcast.19, f32[256,128]{1,0:T(8,128)S(1)} %bitcast.22, f32[256,128]{1,0:T(8,128)S(1)} %bitcast.23, f32[512,128]{1,0:T(8,128)S(1)} %bitcast.20, ...), custom_call_target="tpu_custom_call" | custom-call | tf_op jit(solution)/shard_map/pack/pallas_call | solution.py:99
  5.4 0.7 %collective-permute-start.1 = (f32[16,16,128]{2,1,0:T(8,128)S(1)}, f32[16,16,128]{2,1,0:T(8,128)S(1)}, u32[]{:S(2)}, u32[]{:S(2)}) collective-permute-start(f32[16,16,128]{2,1,0:T(8,128)S(1)} %get-tuple-element.20.e_ref), channel_id=1, source_target_pairs={{1,2},{2,1},{5,6},{6,5},{9,10},{10,9},{13,14},{14,13},{17,18},{18,... | collective-permute-start | bytes 393224 | tf_op jit(solution)/shard_map/ppermute | solution.py:500
  6.0 4.4 %collective-permute-start = (f32[16,16,128]{2,1,0:T(8,128)S(1)}, f32[16,16,128]{2,1,0:T(8,128)S(1)}, u32[]{:S(2)}, u32[]{:S(2)}) collective-permute-start(f32[16,16,128]{2,1,0:T(8,128)S(1)} %get-tuple-element.20.e_ref), channel_id=1, source_target_pairs={{0,1},{1,0},{2,3},{3,2},{4,5},{5,4},{6,7},{7,6},{8,9},{9,8},{10,11... | collective-permute-start | bytes 393224 | tf_op jit(solution)/shard_map/ppermute | solution.py:500
  10.4 0.8 %slice_reduce_fusion.1 = (s32[384]{0:T(512)S(1)}, s32[384]{0:T(512)S(1)}) fusion(s32[384,32]{0,1:T(8,128)} %param.17), kind=kLoop, calls=%fused_computation.32 | loop fusion | bytes 6144 | tf_op jit(solution)/shard_map/slice | solution.py:515
  11.2 0.7 %fusion.1 = (s32[384]{0:T(512)S(1)}, s32[384]{0:T(512)S(1)}) fusion(s32[]{:T(128)S(6)} %mul.13, s32[384]{0:T(512)S(1)} %get-tuple-element.33, s32[384]{0:T(512)S(1)} %get-tuple-element.34, s32[384]{0:T(512)} %param.18), kind=kLoop, calls=%fused_computation.20 | loop fusion | flops 18048 | bytes 7684 | tf_op jit(solution)/shard_map/sub | solution.py:521
  11.9 0.1 corner_strips.1
  12.0 1.6 %collective-permute-start.2 = (f32[4,8,16,128]{3,2,1,0:T(8,128)S(1)}, f32[4,8,16,128]{3,2,1,0:T(8,128)S(1)}, u32[]{:S(2)}, u32[]{:S(2)}) collective-permute-start(f32[4,8,16,128]{3,2,1,0:T(8,128)S(1)} %get-tuple-element.23), channel_id=1, source_target_pairs={{0,4},{4,0},{8,12},{12,8},{1,5},{5,1},{9,13},{13,9},{2,6},{6,2},{1... | collective-permute-start | bytes 786440 | tf_op jit(solution)/shard_map/ppermute | solution.py:500
  13.6 0.7 %collective-permute-start.3 = (f32[4,8,16,128]{3,2,1,0:T(8,128)S(1)}, f32[4,8,16,128]{3,2,1,0:T(8,128)S(1)}, u32[]{:S(2)}, u32[]{:S(2)}) collective-permute-start(f32[4,8,16,128]{3,2,1,0:T(8,128)S(1)} %get-tuple-element.24), channel_id=1, source_target_pairs={{4,8},{8,4},{5,9},{9,5},{6,10},{10,6},{7,11},{11,7},{20,24},{24,20... | collective-permute-start | bytes 786440 | tf_op jit(solution)/shard_map/ppermute | solution.py:500
  14.3 0.7 %stack.19 = s32[1,384]{1,0:T(1,128)S(1)} reshape(s32[384]{0:T(512)} %param.18) | data formatting | bytes 3072 | tf_op jit(solution)/shard_map/stack | solution.py:523
  15.0 0.7 %fusion.8 = (s32[1,384]{1,0:T(1,128)S(1)}, s32[1,384]{1,0:T(1,128)S(1)}) fusion(s32[]{:T(128)S(6)} %mul.15, s32[384,32]{0,1:T(8,128)} %param.17), kind=kLoop, calls=%fused_computation.29 | loop fusion | flops 9216 | bytes 4612 | tf_op jit(solution)/shard_map/sub | solution.py:523
  15.8 5.4 %collective-permute-done.2.xa_ref = f32[4,8,16,128]{3,2,1,0:T(8,128)S(1)} collective-permute-done((f32[4,8,16,128]{3,2,1,0:T(8,128)S(1)}, f32[4,8,16,128]{3,2,1,0:T(8,128)S(1)}, u32[]{:S(2)}, u32[]{:S(2)}) %collective-permute-start.2) | collective-permute-done | bytes 262176 | tf_op jit(solution)/shard_map/ppermute | solution.py:500
  21.2 0.7 %copy-done.6 = f32[3]{0:T(128)S(1)} copy-done((f32[3]{0:T(128)S(1)}, f32[3]{0:T(128)}, u32[]{:S(2)}) %copy-start.6) | copy-done | bytes 36
  21.8 9.4 %forward_steps.1 = (f32[3,384]{1,0:T(4,128)S(1)}, f32[24,2,16,128]{3,2,1,0:T(8,128)S(1)}, f32[24,2,16,128]{3,2,1,0:T(8,128)S(1)}, f32[24,2,16,128]{3,2,1,0:T(8,1...) custom-call(f32[3]{0:T(128)S(1)} %copy-done.6, ...), custom_call_target="tpu_custom_call" | custom-call | tf_op jit(solution)/shard_map/forward_steps/pallas_call | solution.py:338
  31.2 3.7 %collective-permute-start.6 = (f32[3,384]{1,0:T(4,128)S(1)}, f32[3,384]{1,0:T(4,128)S(1)}, u32[]{:S(2)}, u32[]{:S(2)}) collective-permute-start(f32[3,384]{1,0:T(4,128)S(1)} %get-tuple-element.32.partial_ref), channel_id=1, source_target_pairs={{0,12},{4,8},{8,4},{12,0},{1,13},{5,9},{9,5},{13,1},{2,14},{6,10},... | collective-permute-start | bytes 13832 | tf_op jit(solution)/shard_map/ppermute | solution.py:506
  34.9 2.5 %collective-permute-start.5 = (f32[3,384]{1,0:T(4,128)S(1)}, f32[3,384]{1,0:T(4,128)S(1)}, u32[]{:S(2)}, u32[]{:S(2)}) collective-permute-start(f32[3,384]{1,0:T(4,128)S(1)} %get-tuple-element.32.partial_ref), channel_id=1, source_target_pairs={{0,8},{4,12},{8,0},{12,4},{1,9},{5,13},{9,1},{13,5},{2,10},{6,14},... | collective-permute-start | bytes 13832 | tf_op jit(solution)/shard_map/ppermute | solution.py:506
  37.4 0.4 collective-permute-start.4
  37.8 1.7 %collective-permute-done.5.rest_1_ = f32[3,384]{1,0:T(4,128)S(1)} collective-permute-done((f32[3,384]{1,0:T(4,128)S(1)}, f32[3,384]{1,0:T(4,128)S(1)}, u32[]{:S(2)}, u32[]{:S(2)}) %collective-permute-start.5) | collective-permute-done | bytes 4640 | tf_op jit(solution)/shard_map/ppermute | solution.py:506
  39.4 1.6 %collective-permute-done.4.rest_0_ = f32[3,384]{1,0:T(4,128)S(1)} collective-permute-done((f32[3,384]{1,0:T(4,128)S(1)}, f32[3,384]{1,0:T(4,128)S(1)}, u32[]{:S(2)}, u32[]{:S(2)}) %collective-permute-start.4) | collective-permute-done | bytes 4640 | tf_op jit(solution)/shard_map/ppermute | solution.py:506
  41.0 6.4 %adjoint_steps.1 = f32[256,128]{1,0:T(8,128)} custom-call(f32[3]{0:T(128)S(1)} %copy-done.6, f32[3]{0:T(128)S(1)} %copy-done.7, f32[3,384]{1,0:T(4,128)S(1)} %copy-done.5, s32[8,384]{1,0:T(8,128)S(1)} %stack.21.meta_ref, f32[24,2,16,128]{3,2,1,0:T(8,128)S(1)} %get-tuple-element.25.px_ref, f32[24,2,16,128]{3,2,1,0:T(8,128)S(1)} %get-tuple-element.26.qx_ref, ...), custom_call_target="tpu_custom_call" | custom-call | tf_op jit(solution)/shard_map/adjoint_steps/pallas_call | solution.py:480
  (20 shorter events, 0.1 us)
Async XLA Ops:
  0.0 41.0 %copy-start.5 = (f32[3,384]{1,0:T(4,128)S(1)}, f32[3,384]{1,0:T(4,128)}, u32[]{:S(2)}) copy-start(f32[3,384]{1,0:T(4,128)} %weight_ref.1) | copy-start | bytes 13828
  0.0 41.0 %copy-start.7 = (f32[3]{0:T(128)S(1)}, f32[3]{0:T(128)}, u32[]{:S(2)}) copy-start(f32[3]{0:T(128)} %decay_ref.1) | copy-start | bytes 40
  0.0 1.0 %copy-start = (f32[3,16,16,128]{3,2,1,0:T(8,128)S(1)}, f32[3,16,16,128]{3,2,1,0:T(8,128)}, u32[]{:S(2)}) copy-start(f32[3,16,16,128]{3,2,1,0:T(8,128)} %param.10) | copy-start | bytes 1179652
  1.0 0.9 %copy-start.1 = (f32[2,16,16,128]{3,2,1,0:T(8,128)S(1)}, f32[2,16,16,128]{3,2,1,0:T(8,128)}, u32[]{:S(2)}) copy-start(f32[2,16,16,128]{3,2,1,0:T(8,128)} %param.13) | copy-start | bytes 786436
  2.0 0.9 %copy-start.2 = (s32[2,16,16,128]{3,2,1,0:T(8,128)S(1)}, s32[2,16,16,128]{3,2,1,0:T(8,128)}, u32[]{:S(2)}) copy-start(s32[2,16,16,128]{3,2,1,0:T(8,128)} %param.14) | copy-start | bytes 786436
  2.9 0.9 %copy-start.3 = (f32[16,16,128]{2,1,0:T(8,128)S(1)}, f32[16,16,128]{2,1,0:T(8,128)}, u32[]{:S(2)}) copy-start(f32[16,16,128]{2,1,0:T(8,128)} %param.11) | copy-start | bytes 393220
  3.8 0.9 %copy-start.4 = (f32[16,16,128]{2,1,0:T(8,128)S(1)}, f32[16,16,128]{2,1,0:T(8,128)}, u32[]{:S(2)}) copy-start(f32[16,16,128]{2,1,0:T(8,128)} %param.12) | copy-start | bytes 393220
  5.4 6.5 %collective-permute-start.1 = (f32[16,16,128]{2,1,0:T(8,128)S(1)}, f32[16,16,128]{2,1,0:T(8,128)S(1)}, u32[]{:S(2)}, u32[]{:S(2)}) collective-permute-start(f32[16,16,128]{2,1,0:T(8,128)S(1)} %get-tuple-element.20.e_ref), channel_id=1, source_target_pairs={{1,2},{2,1},{5,6},{6,5},{9,10},{10,9},{13,14},{14,13},{17,18},{18,... | collective-permute-start | bytes 393224 | tf_op jit(solution)/shard_map/ppermute | solution.py:500
  6.0 5.9 %collective-permute-start = (f32[16,16,128]{2,1,0:T(8,128)S(1)}, f32[16,16,128]{2,1,0:T(8,128)S(1)}, u32[]{:S(2)}, u32[]{:S(2)}) collective-permute-start(f32[16,16,128]{2,1,0:T(8,128)S(1)} %get-tuple-element.20.e_ref), channel_id=1, source_target_pairs={{0,1},{1,0},{2,3},{3,2},{4,5},{5,4},{6,7},{7,6},{8,9},{9,8},{10,11... | collective-permute-start | bytes 393224 | tf_op jit(solution)/shard_map/ppermute | solution.py:500
  12.0 9.2 %collective-permute-start.2 = (f32[4,8,16,128]{3,2,1,0:T(8,128)S(1)}, f32[4,8,16,128]{3,2,1,0:T(8,128)S(1)}, u32[]{:S(2)}, u32[]{:S(2)}) collective-permute-start(f32[4,8,16,128]{3,2,1,0:T(8,128)S(1)} %get-tuple-element.23), channel_id=1, source_target_pairs={{0,4},{4,0},{8,12},{12,8},{1,5},{5,1},{9,13},{13,9},{2,6},{6,2},{1... | collective-permute-start | bytes 786440 | tf_op jit(solution)/shard_map/ppermute | solution.py:500
  13.6 7.5 %collective-permute-start.3 = (f32[4,8,16,128]{3,2,1,0:T(8,128)S(1)}, f32[4,8,16,128]{3,2,1,0:T(8,128)S(1)}, u32[]{:S(2)}, u32[]{:S(2)}) collective-permute-start(f32[4,8,16,128]{3,2,1,0:T(8,128)S(1)} %get-tuple-element.24), channel_id=1, source_target_pairs={{4,8},{8,4},{5,9},{9,5},{6,10},{10,6},{7,11},{11,7},{20,24},{24,20... | collective-permute-start | bytes 786440 | tf_op jit(solution)/shard_map/ppermute | solution.py:500
  21.2 0.7 %copy-start.6 = (f32[3]{0:T(128)S(1)}, f32[3]{0:T(128)}, u32[]{:S(2)}) copy-start(f32[3]{0:T(128)} %retard_ref.3) | copy-start | bytes 40
  31.2 6.5 %collective-permute-start.6 = (f32[3,384]{1,0:T(4,128)S(1)}, f32[3,384]{1,0:T(4,128)S(1)}, u32[]{:S(2)}, u32[]{:S(2)}) collective-permute-start(f32[3,384]{1,0:T(4,128)S(1)} %get-tuple-element.32.partial_ref), channel_id=1, source_target_pairs={{0,12},{4,8},{8,4},{12,0},{1,13},{5,9},{9,5},{13,1},{2,14},{6,10},... | collective-permute-start | bytes 13832 | tf_op jit(solution)/shard_map/ppermute | solution.py:506
  34.9 4.5 %collective-permute-start.5 = (f32[3,384]{1,0:T(4,128)S(1)}, f32[3,384]{1,0:T(4,128)S(1)}, u32[]{:S(2)}, u32[]{:S(2)}) collective-permute-start(f32[3,384]{1,0:T(4,128)S(1)} %get-tuple-element.32.partial_ref), channel_id=1, source_target_pairs={{0,8},{4,12},{8,0},{12,4},{1,9},{5,13},{9,1},{13,5},{2,10},{6,14},... | collective-permute-start | bytes 13832 | tf_op jit(solution)/shard_map/ppermute | solution.py:506
  37.4 3.6 %collective-permute-start.4 = (f32[3,384]{1,0:T(4,128)S(1)}, f32[3,384]{1,0:T(4,128)S(1)}, u32[]{:S(2)}, u32[]{:S(2)}) collective-permute-start(f32[3,384]{1,0:T(4,128)S(1)} %get-tuple-element.32.partial_ref), channel_id=1, source_target_pairs={{0,4},{4,0},{8,12},{12,8},{1,5},{5,1},{9,13},{13,9},{2,6},{6,2},{1... | collective-permute-start | bytes 13832 | tf_op jit(solution)/shard_map/ppermute | solution.py:506

commit v2 on v1

v2 whole, which is shorter than its diff:
```python
import functools

import jax
import jax.numpy as jnp
from jax import lax
from jax.experimental import pallas as pl
from jax.experimental.pallas import tpu as pltpu
from jax.sharding import PartitionSpec as P

STEPS = 4
HALO = STEPS
RATE = 0.02
HALF_DT = 0.025
LANES = 128
TILE = 8
GROUP = 16
RIGHT = 64
Y = ("gy", "sa")
MIB = 1024 * 1024
PX, QX, BX, PY, QYM, QY, PYM, BY, BYM, D, KIND, KDIR = range(12)
KINDS = 12
VMEM = pl.BlockSpec(memory_space=pltpu.VMEM)
HBM = pl.BlockSpec(memory_space=pltpu.HBM)


def lane_of(shape):
    return lax.broadcasted_iota(jnp.int32, shape, len(shape) - 1)


def roll(value, shift, axis):
    return pltpu.roll(value, shift % value.shape[axis], axis)


def pack_edges(fields):
    lane = lane_of(fields[0].shape)
    packed = jnp.zeros_like(fields[0])
    for f, field in enumerate(fields):
        packed = jnp.where(lane // GROUP == f, roll(field, 8 + GROUP * f, 1), packed)
    return packed


def y_after(value, strip, s):
    edge = roll(strip, LANES - 1 - (RIGHT + GROUP * s + 8), 1)
    return jnp.where(lane_of(value.shape) == LANES - 1, edge, roll(value, LANES - 1, 1))


def y_before(value, strip, s):
    edge = roll(strip, -(GROUP * s + 7), 1)
    return jnp.where(lane_of(value.shape) == 0, edge, roll(value, 1, 1))


def z_pair(value):
    tiles = [value[i : i + TILE] for i in range(0, value.shape[0], TILE)]
    row = lax.broadcasted_iota(jnp.int32, tiles[0].shape, 0)
    ups = [roll(t, TILE - 1, 0) for t in tiles]
    downs = [roll(t, 1, 0) for t in tiles]
    pairs = []
    for i, tile in enumerate(tiles):
        above = jnp.where(row == TILE - 1, ups[i + 1] if i + 1 < len(tiles) else tile, ups[i])
        below = jnp.where(row == 0, downs[i - 1] if i else tile, downs[i])
        pairs.append(above + below)
    return jnp.concatenate(pairs, axis=0)


def state_row(m, width):
    low, high = HALO + m, HALO + width - 1 - m

    def find(r):
        if low <= r <= high:
            return 0, r - HALO
        return (1, r - m) if r < low else (1, HALO + r - high - 1)

    return find


def coef_row(kind, width):
    low, high = HALO, HALO + width - 1
    if kind in (PX, QX, BX, D):
        high -= 1
    if kind == D:
        low += 1

    def find(r):
        if low <= r <= high:
            return 0, r - HALO
        return (1, r) if r <= HALO else (1, HALO + 1 + r - (HALO + width - 1))

    return find


def read_state(refs, m, width, r, s):
    which, index = state_row(m, width)(r)
    return refs[which][m, index, s]


def read_coef(refs, kind, width, r, i):
    which, index = coef_row(kind, width)(r)
    return refs[which][index, kind, i]


def pack_kernel(*refs, layers, width, species):
    sources, (f7_ref, e_ref, xa_ref, xb_ref), buffers, sem = refs[:5], refs[5:9], refs[9:14], refs[14]
    copies = [pltpu.make_async_copy(a, b, sem.at[i]) for i, (a, b) in enumerate(zip(sources, buffers))]
    for copy in copies:
        copy.start()
    for copy in copies:
        copy.wait()
    initial_ref, logk_ref, direction_ref, speed_ref, flags_ref = buffers
    plane = layers * width
    even = lax.rem(lax.axis_index("gx"), 2) == 0
    top, bottom = width - HALO, 0
    for x in range(width):

        def take(ref, index):
            return ref[pl.ds(index * plane + x, layers, stride=width), :]

        fields = [take(initial_ref, s) for s in range(species)]
        conductance = jnp.exp(take(logk_ref, 0))
        fields += [conductance, conductance * take(direction_ref, 0)]
        for axis in range(2):
            speed = take(speed_ref, axis)
            fields.append(jnp.where(take(flags_ref, axis) == 1, speed, -speed))
        for f, field in enumerate(fields):
            f7_ref[x, f] = field
        e_ref[x] = pack_edges(fields)
    count = species + 4
    start_a = jnp.where(even, top, bottom)
    start_b = jnp.where(even, bottom, top)
    for r in range(HALO):
        xa_ref[r, 0:count] = f7_ref[start_a + r]
        xb_ref[r, 0:count] = f7_ref[start_b + r]


def pack(initial, logk, direction, face_speed, face_flags):
    species, layers, width, _ = initial.shape
    f32 = jnp.float32
    sources = [a.reshape(-1, LANES) for a in (initial, logk, direction, face_speed, face_flags)]
    return pl.pallas_call(
        functools.partial(pack_kernel, layers=layers, width=width, species=species),
        out_shape=(
            jax.ShapeDtypeStruct((width, species + 4, layers, LANES), f32),
            jax.ShapeDtypeStruct((width, layers, LANES), f32),
            jax.ShapeDtypeStruct((HALO, species + 5, layers, LANES), f32),
            jax.ShapeDtypeStruct((HALO, species + 5, layers, LANES), f32),
        ),
        in_specs=[HBM] * 5,
        out_specs=[VMEM] * 4,
        scratch_shapes=[pltpu.VMEM(a.shape, a.dtype) for a in sources] + [pltpu.SemaphoreType.DMA((5,))],
        compiler_params=pltpu.CompilerParams(vmem_limit_bytes=5 * MIB),
        name="pack",
    )(*sources)


def strips_kernel(ea_ref, eb_ref, xa_in, xb_in, xa_ref, xb_ref, buf_a, buf_b, sem_a, sem_b, *, width, count):
    even_x = lax.rem(lax.axis_index("gx"), 2) == 0
    even_y = lax.rem(lax.axis_index(Y), 2) == 0
    start_a = jnp.where(even_x, width - HALO, 0)
    start_b = jnp.where(even_x, 0, width - HALO)
    for r in range(HALO):
        for start, buf in ((start_a, buf_a), (start_b, buf_b)):
            one, two = ea_ref[start + r], eb_ref[start + r]
            from_left = lane_of(one.shape) % GROUP < 8
            buf[r] = jnp.where(from_left == even_y, two, one)
    copies = [
        pltpu.make_async_copy(buf_a, xa_ref.at[:, count], sem_a),
        pltpu.make_async_copy(buf_b, xb_ref.at[:, count], sem_b),
    ]
    for copy in copies:
        copy.start()
    for copy in copies:
        copy.wait()


def add_strips(ea, eb, xa, xb):
    width, layers, _ = ea.shape
    buffer = pltpu.VMEM((HALO, layers, LANES), jnp.float32)
    return pl.pallas_call(
        functools.partial(strips_kernel, width=width, count=xa.shape[1] - 1),
        out_shape=(jax.ShapeDtypeStruct(xa.shape, xa.dtype), jax.ShapeDtypeStruct(xb.shape, xb.dtype)),
        in_specs=[pl.BlockSpec(memory_space=pltpu.VMEM)] * 2 + [pl.BlockSpec(memory_space=pl.ANY)] * 2,
        out_specs=[pl.BlockSpec(memory_space=pl.ANY)] * 2,
        input_output_aliases={2: 0, 3: 1},
        scratch_shapes=[buffer, buffer, pltpu.SemaphoreType.DMA, pltpu.SemaphoreType.DMA],
        compiler_params=pltpu.CompilerParams(vmem_limit_bytes=2 * MIB),
        name="corner_strips",
    )(ea, eb, xa, xb)


def place(fields, own_edges, outer_edges, left, near, column, species):
    left_strip = jnp.where(near, outer_edges, own_edges)
    right_strip = jnp.where(near, own_edges, outer_edges)
    states = list(fields[:species]) + [jnp.where(left, left_strip, roll(right_strip, RIGHT, 1))]
    others = []
    for f in range(species, species + 4):
        index = GROUP * f + column
        strip = jnp.where(
            left,
            jnp.take_along_axis(left_strip, index, 1, mode="promise_in_bounds"),
            jnp.take_along_axis(right_strip, index, 1, mode="promise_in_bounds"),
        )
        others.append((fields[f], strip))
    return states, others


def y_coefs(k, kd, u, main_mask, strip_mask):
    half4 = HALF_DT * (k[1] + roll(k[1], 127, 1))
    p4 = (half4 + jnp.maximum(u[1], 0.0)) * strip_mask
    q4 = (half4 - jnp.minimum(u[1], 0.0)) * strip_mask
    b4 = HALF_DT * (kd[1] + roll(kd[1], 127, 1)) * strip_mask
    half = HALF_DT * (k[0] + y_after(k[0], k[1], 0))
    p = (half + jnp.maximum(u[0], 0.0)) * main_mask
    q = (half - jnp.minimum(u[0], 0.0)) * main_mask
    b = HALF_DT * (kd[0] + y_after(kd[0], kd[1], 0)) * main_mask
    return {
        PY: (p, p4),
        QY: (q, q4),
        BY: (b, b4),
        PYM: (y_before(p, p4, 0), roll(p4, 1, 1)),
        QYM: (y_before(q, q4, 0), roll(q4, 1, 1)),
        BYM: (y_before(b, b4, 0), roll(b4, 1, 1)),
    }


def x_coefs(k, k_next, kd, kd_next, u, mask):
    half = HALF_DT * (k + k_next)
    p = half + jnp.maximum(u, 0.0)
    q = half - jnp.minimum(u, 0.0)
    b = HALF_DT * (kd + kd_next)
    return (p, q, b) if mask is None else (p * mask, q * mask, b * mask)


def masks(layers):
    shape = (layers, LANES)
    lane = lane_of(shape)
    column = lane % GROUP
    near, left = column < 8, lane < RIGHT
    gy = lax.axis_index(Y)
    first_y, last_y = gy == 0, gy == lax.axis_size(Y) - 1
    strip_mask = jnp.where(
        left, jnp.where(first_y & near, 0.0, 1.0), jnp.where(last_y & (column >= 7), 0.0, 1.0)
    ).astype(jnp.float32)
    main_mask = jnp.where(last_y & (lane == LANES - 1), 0.0, 1.0).astype(jnp.float32)
    return column, near, left, main_mask, strip_mask


def step_row(r, m, rates, coef, state, tangent, put_c, put_t, put_jy):
    species = len(rates) - 1
    strips = state(r, species)
    strips_t = tangent(r, species) if m > 0 else None
    for s in (species,) + tuple(range(species)):
        i = 1 if s == species else 0
        kept = rates[s] - coef(D, r, i)
        upper, lower = coef(QX, r, i), coef(PX, r - 1, i)
        after, before = coef(QY, r, i), coef(PYM, r, i)

        def around(value, strip):
            if i:
                return roll(value, LANES - 1, 1), roll(value, 1, 1)
            return y_after(value, strip, s), y_before(value, strip, s)

        def moved(value, up, down, yp, ym):
            return kept * value + upper * up + lower * down + after * yp + before * ym + RATE * z_pair(value)

        c = strips if i else state(r, s)
        up, down = state(r + 1, s), state(r - 1, s)
        yp, ym = around(c, strips)
        jump = yp - c
        source = (
            coef(BX, r, i) * (up - c)
            - coef(BX, r - 1, i) * (c - down)
            + coef(BY, r, i) * jump
            - coef(BYM, r, i) * (c - ym)
        )
        put_jy(s, jump)
        if m + 1 < STEPS:
            put_c(s, moved(c, up, down, yp, ym))
        if m > 0:
            t = strips_t if i else tangent(r, s)
            tp, tm = around(t, strips_t)
            source = source + moved(t, tangent(r + 1, s), tangent(r - 1, s), tp, tm)
        put_t(s, source)


def well_rows(meta_ref):
    return [meta_ref[i : i + 1, :] for i in range(4)]


def strip_columns(wells):
    own = lax.broadcasted_iota(jnp.int32, (LANES, wells), 0)
    return own, own % RIGHT // GROUP, own % GROUP + jnp.where(own < RIGHT, -8, 120)


def cone_kernel(
    rate_ref, f7_ref, e_ref, ea_ref, eb_ref, meta_ref,
    coef_ref, c_ref, t_ref, jy_ref, mask_ref, hot_ref, *, layers, width, species,
):
    f32, bf16 = jnp.float32, jnp.bfloat16
    column, near, left, main_mask, strip_mask = masks(layers)
    even_y = lax.rem(lax.axis_index(Y), 2) == 0
    count = species + 4
    kept = []
    for x in range(width):
        outer = jnp.where(near == even_y, eb_ref[x], ea_ref[x])
        states, (k, kd, ux, uy) = place(
            [f7_ref[x, f] for f in range(count)], e_ref[x], outer, left, near, column, species
        )
        for s in range(species + 1):
            c_ref[0, x, s] = states[s]
        found = y_coefs(k, kd, uy, main_mask, strip_mask)
        for kind, pair in found.items():
            coef_ref[x, kind, 0], coef_ref[x, kind, 1] = pair
        for i in range(2):
            coef_ref[x, KIND, i], coef_ref[x, KDIR, i] = k[i], kd[i]
            diagonal = found[PY][i] + found[QYM][i] + 2 * RATE
            if x:
                p, q, b = x_coefs(kept[0][i], k[i], kept[1][i], kd[i], kept[2][i], None)
                coef_ref[x - 1, PX, i], coef_ref[x - 1, QX, i], coef_ref[x - 1, BX, i] = p, q, b
                coef_ref[x - 1, D, i] = coef_ref[x - 1, D, i] + p
                diagonal = diagonal + q
            coef_ref[x, D, i] = diagonal
            if x == width - 1:
                coef_ref[x, PX, i] = ux[i]
        kept = (k, kd, ux)

    rates = [rate_ref[s : s + 1, :] for s in range(species + 1)]
    for m in range(STEPS):
        for r in range(HALO + 1 + m, HALO + width - 1 - m):
            x = r - HALO

            def put(ref, slot):
                def store(s, value):
                    ref[slot, x, s] = value

                return store

            step_row(
                r, m, rates,
                lambda kind, r, i: coef_ref[r - HALO, kind, i],
                lambda r, s: c_ref[m, r - HALO, s],
                lambda r, s: t_ref[m - 1, r - HALO, s],
                put(c_ref, m + 1), put(t_ref, m), put(jy_ref, m),
            )

    depth, first, last, where_y = well_rows(meta_ref)
    wells = meta_ref.shape[1]
    in_layer = lax.broadcasted_iota(jnp.int32, (layers, wells), 0) == depth
    for r in range(width + 2 * HALO):
        inside = (first <= r - HALO) & (last >= r - HALO) & in_layer
        mask_ref[r * layers : (r + 1) * layers, :] = jnp.where(inside, 1.0, 0.0).astype(bf16)
    own, strip_species, strip_column = strip_columns(wells)
    hit = ((strip_column < 0) | (strip_column >= LANES)) & (strip_column == where_y)
    for s in range(species):
        hot_ref[s, 0:LANES] = jnp.where(own == where_y, 1.0, 0.0).astype(bf16)
        hot_ref[s, LANES : 2 * LANES] = jnp.where(hit & (strip_species == s), 1.0, 0.0).astype(bf16)


def cone(rates, f7, e, ea, eb, meta):
    width, count, layers, _ = f7.shape
    species, wells = count - 4, meta.shape[1]
    f32 = jnp.float32
    state = jax.ShapeDtypeStruct((STEPS, width, species + 1, layers, LANES), f32)
    return pl.pallas_call(
        functools.partial(cone_kernel, layers=layers, width=width, species=species),
        out_shape=(
            jax.ShapeDtypeStruct((width, KINDS, 2, layers, LANES), f32),
            state,
            state,
            state,
            jax.ShapeDtypeStruct(((width + 2 * HALO) * layers, wells), jnp.bfloat16),
            jax.ShapeDtypeStruct((species, 2 * LANES, wells), jnp.bfloat16),
        ),
        in_specs=[VMEM] * 6,
        out_specs=[VMEM] * 6,
        compiler_params=pltpu.CompilerParams(vmem_limit_bytes=4 * MIB),
        cost_estimate=pl.CostEstimate(flops=10**7, bytes_accessed=10**7, transcendentals=0),
        name="cone_steps",
    )(rates, f7, e, ea, eb, meta)


def rim_kernel(
    rate_ref, xa_ref, xb_ref, coef_in, c_in, t_in, mask_ref, hot_ref,
    partial_ref, coef_out, c_out, jy_out, t_out, *, layers, width, species,
):
    f32, bf16 = jnp.float32, jnp.bfloat16
    column, near, left, main_mask, strip_mask = masks(layers)
    gx = lax.axis_index("gx")
    even_x = lax.rem(gx, 2) == 0
    count = species + 4
    rows = width + 2 * HALO
    coefs = (coef_in, coef_out)

    def put_coef(kind, r, i, value):
        which, index = coef_row(kind, width)(r)
        coefs[which][index, kind, i] = value

    speeds = {}
    for r in list(range(HALO)) + list(range(HALO + width, rows)):
        from_a = even_x if r > HALO else jnp.logical_not(even_x)
        both = [jnp.where(from_a, xa_ref[r % (HALO + width), f], xb_ref[r % (HALO + width), f]) for f in range(count + 1)]
        states, (k, kd, ux, uy) = place(
            both[:count], pack_edges(both[:count]), both[count], left, near, column, species
        )
        index = state_row(0, width)(r)[1]
        for s in range(species + 1):
            c_out[0, index, s] = states[s]
        for kind, pair in y_coefs(k, kd, uy, main_mask, strip_mask).items():
            for i in range(2):
                put_coef(kind, r, i, pair[i])
        for i in range(2):
            put_coef(KIND, r, i, k[i])
            put_coef(KDIR, r, i, kd[i])
        speeds[r] = ux
    last = HALO + width - 1
    speeds[last] = [coef_in[width - 1, PX, i] for i in range(2)]
    inside_low = jnp.where(gx > 0, 1.0, 0.0).astype(f32)
    inside_high = jnp.where(gx < lax.axis_size("gx") - 1, 1.0, 0.0).astype(f32)
    get = lambda kind, r, i: read_coef(coefs, kind, width, r, i)
    for r in list(range(HALO)) + list(range(last, rows - 1)):
        for i in range(2):
            p, q, b = x_coefs(
                get(KIND, r, i), get(KIND, r + 1, i), get(KDIR, r, i), get(KDIR, r + 1, i), speeds[r][i],
                inside_low if r < HALO else inside_high,
            )
            put_coef(PX, r, i, p)
            put_coef(QX, r, i, q)
            put_coef(BX, r, i, b)
    for r in list(range(1, HALO + 1)) + list(range(last, rows - 1)):
        for i in range(2):
            if r == HALO:
                value = coef_in[0, D, i] + get(QX, r - 1, i)
            elif r == last:
                value = coef_in[width - 1, D, i] + get(PX, r, i)
            else:
                value = get(PY, r, i) + get(QYM, r, i) + 2 * RATE + get(PX, r, i) + get(QX, r - 1, i)
            put_coef(D, r, i, value)

    rates = [rate_ref[s : s + 1, :] for s in range(species + 1)]
    for m in range(STEPS):
        for r in list(range(1 + m, HALO + 1 + m)) + list(range(last - m, rows - 1 - m)):
            index = state_row(m + 1, width)(r)[1]

            def put(ref, slot):
                def store(s, value):
                    ref[slot, index, s] = value

                return store

            step_row(
                r, m, rates, get,
                lambda r, s: read_state((c_in, c_out), m, width, r, s),
                lambda r, s: tangent_row(t_in, t_out, m, width, r)[s],
                put(c_out, m + 1), put(t_out, m), put(jy_out, m),
            )

    wells = mask_ref.shape[1]
    for s in range(species):
        total = jnp.zeros((layers, wells), f32)
        for half in range(2):
            span = range(HALO + half * width // 2, HALO + (half + 1) * width // 2)
            both = jnp.concatenate(
                [
                    jnp.concatenate([tangent_row(t_in, t_out, STEPS, width, r)[p] for r in span], axis=0)
                    for p in (s, species)
                ],
                axis=1,
            )
            picked = jnp.zeros((len(span) * layers, wells), f32)
            for piece in range(3):
                coarse = both.astype(bf16)
                picked = picked + jnp.dot(coarse, hot_ref[s], preferred_element_type=f32)
                both = both - coarse.astype(f32)
            picked = picked * mask_ref[span[0] * layers : (span[-1] + 1) * layers, :].astype(f32)
            for x in range(len(span)):
                total = total + picked[x * layers : (x + 1) * layers]
        partial_ref[s : s + 1, :] = jnp.sum(total, axis=0, keepdims=True)


def tangent_row(t_in, t_out, m, width, r):
    which, index = state_row(m, width)(r)
    return (t_in, t_out)[which].at[m - 1, index]


def rim(rates, xa, xb, coef, c, t, mask, hot):
    _, width, planes, layers, _ = c.shape
    species, wells = planes - 1, mask.shape[1]
    f32 = jnp.float32
    state = (STEPS, 2 * HALO, planes, layers, LANES)
    return pl.pallas_call(
        functools.partial(rim_kernel, layers=layers, width=width, species=species),
        out_shape=(
            jax.ShapeDtypeStruct((species, wells), f32),
            jax.ShapeDtypeStruct((2 * HALO + 2, KINDS, 2, layers, LANES), f32),
            jax.ShapeDtypeStruct(state, f32),
            jax.ShapeDtypeStruct(state, f32),
        ),
        in_specs=[VMEM] * 8,
        out_specs=[VMEM] * 4,
        scratch_shapes=[pltpu.VMEM(state, f32)],
        compiler_params=pltpu.CompilerParams(vmem_limit_bytes=8 * MIB),
        name="rim_steps",
    )(rates, xa, xb, coef, c, t, mask, hot)


def adjoint_kernel(
    rate_ref, weight_ref, meta_ref, coef_in, coef_out, c_in, c_out, jy_in, jy_out, mask_ref, partial_ref, *rest,
    layers, width, species, parts,
):
    others, out_ref, lam_ref = rest[:parts], *rest[parts:]
    f32, bf16 = jnp.float32, jnp.bfloat16
    rows = width + 2 * HALO
    shape = (layers, LANES)
    lane = lane_of(shape)
    gx, gy = lax.axis_index("gx"), lax.axis_index(Y)
    where_y = meta_ref[3:4, :]
    counts = meta_ref[4:5, :].astype(f32)
    wells = meta_ref.shape[1]
    coefs, states = (coef_in, coef_out), (c_in, c_out)
    coef = lambda kind, r, i: read_coef(coefs, kind, width, r, i)

    own, strip_species, strip_column = strip_columns(wells)
    strip_hit, own_hit = strip_column == where_y, own == where_y
    residuals = []
    for s in range(species):
        total = partial_ref[s : s + 1, :]
        for other in others:
            total = total + other[s : s + 1, :]
        factor = rate_ref[species + 1 + s, 0:1][:, None]
        residual = weight_ref[s : s + 1, :] * (total * factor) / counts
        residuals.append(residual / counts * factor)
    lam = jnp.zeros((rows * layers, (species + 1) * LANES), f32)
    for piece in range(3):
        coarse = [r.astype(bf16).astype(f32) for r in residuals]
        residuals = [r - q for r, q in zip(residuals, coarse)]
        blocks = [jnp.where(own_hit, q, 0.0).astype(bf16) for q in coarse]
        side = jnp.zeros((LANES, wells), f32)
        for s in range(species):
            side = jnp.where(strip_hit & (strip_species == s), coarse[s], side)
        spread = jnp.concatenate(blocks + [side.astype(bf16)], axis=0)
        lam = lam + lax.dot_general(mask_ref[...], spread, (((1,), (1,)), ((), ())), preferred_element_type=f32)
    for s in range(species + 1):
        lam_ref[0, :, s] = lam[:, s * LANES : (s + 1) * LANES].reshape(rows, layers, LANES)

    rates = [rate_ref[s : s + 1, :] for s in range(species + 1)]
    first_row, last_row = HALO - 1, HALO + width - 1
    sums_x, sums_y, sums_side = {}, {}, {}
    for m in reversed(range(STEPS)):
        now = STEPS - 1 - m
        low, high = STEPS - m, rows - 1 - (STEPS - m)
        for r in range(min(low, first_row), max(high, last_row) + 1):
            sense, retreat = first_row <= r <= last_row, m > 0 and low <= r <= high
            strip = lam_ref[now, r, species]
            along_x = along_y = side = None
            for s in range(species + 1):
                i = 1 if s == species else 0
                value = strip if i else lam_ref[now, r, s]
                up = lam_ref[now, r + 1, s]
                yp = roll(value, LANES - 1, 1) if i else y_after(value, strip, s)
                if sense:
                    if not i:
                        jump = read_state(states, m, width, r + 1, s) - read_state(states, m, width, r, s)
                        term = jump * (up - value)
                        along_x = term if along_x is None else along_x + term
                    if r >= HALO:
                        which, index = state_row(m + 1, width)(r)
                        term = (jy_in, jy_out)[which][m, index, s] * (yp - value)
                        if i:
                            side = term
                        else:
                            along_y = term if along_y is None else along_y + term
                if retreat:
                    ym = roll(value, 1, 1) if i else y_before(value, strip, s)
                    lam_ref[now + 1, r, s] = (
                        (rates[s] - coef(D, r, i)) * value
                        + coef(PX, r, i) * up
                        + coef(QX, r - 1, i) * lam_ref[now, r - 1, s]
                        + coef(PY, r, i) * yp
                        + coef(QYM, r, i) * ym
                        + RATE * z_pair(value)
                    )
            if sense:
                for store, term in ((sums_x, along_x), (sums_y, along_y), (sums_side, side)):
                    if term is not None:
                        store[r] = store[r] + term if r in store else term

    main_mask = jnp.where((gy == lax.axis_size(Y) - 1) & (lane == LANES - 1), 0.0, 1.0).astype(f32)
    side_mask = jnp.where((gy == 0) & (lane == 0), 0.0, 1.0).astype(f32)
    for x in range(width):
        r = x + HALO
        upper, lower = sums_x[r], sums_x[r - 1]
        if x == 0:
            lower = lower * jnp.where(gx > 0, 1.0, 0.0).astype(f32)
        if x == width - 1:
            upper = upper * jnp.where(gx < lax.axis_size("gx") - 1, 1.0, 0.0).astype(f32)
        along_y, strip = sums_y[r] * main_mask, sums_side[r]
        side = roll(strip, -7, 1)
        for s in range(1, species):
            side = side + roll(strip, -(GROUP * s + 7), 1)
        before = jnp.where(lane == 0, side * side_mask, roll(along_y, 1, 1))
        out_ref[pl.ds(x, layers, stride=width), :] = -HALF_DT * coef(KIND, r, 0) * (upper + lower + along_y + before)


def adjoint(rates, weight, meta, coef_in, coef_out, c_in, c_out, jy_in, jy_out, mask, partials):
    _, width, planes, layers, _ = c_in.shape
    species = planes - 1
    parts = len(partials) - 1
    return pl.pallas_call(
        functools.partial(adjoint_kernel, layers=layers, width=width, species=species, parts=parts),
        out_shape=jax.ShapeDtypeStruct((layers * width, LANES), jnp.float32),
        in_specs=[VMEM] * (10 + len(partials)),
        out_specs=VMEM,
        scratch_shapes=[pltpu.VMEM((STEPS, width + 2 * HALO, planes, layers, LANES), jnp.float32)],
        compiler_params=pltpu.CompilerParams(vmem_limit_bytes=12 * MIB),
        name="adjoint_steps",
    )(rates, weight, meta, coef_in, coef_out, c_in, c_out, jy_in, jy_out, mask, *partials)


def swaps(first, second, axis):
    count = lax.axis_size(axis)
    even = [p for i in range(0, count - 1, 2) for p in ((i, i + 1), (i + 1, i))]
    odd = [p for i in range(1, count - 1, 2) for p in ((i, i + 1), (i + 1, i))]
    return lax.ppermute(first, axis, even), lax.ppermute(second, axis, odd)


def from_others(value, axis, reach):
    count = lax.axis_size(axis)
    if count in (2, 4):
        return [lax.ppermute(value, axis, [(i, i ^ d) for i in range(count)]) for d in range(1, count)]
    return [
        lax.ppermute(value, axis, [(i, i + d) for i in range(count) if 0 <= i + d < count])
        for distance in range(1, min(reach, count - 1) + 1)
        for d in (distance, -distance)
    ]


def well_table(screen_cells, screen_count, row_start, col_start, total_x, total_y):
    start, second = screen_cells[:, 0], screen_cells[:, 1]
    plane = total_x * total_y
    depth = start // plane
    x = start % plane // total_y
    y = start % total_y
    end = x + (screen_count - 1) * ((second - start) // total_y)
    first, last = jnp.minimum(x, end) - row_start, jnp.maximum(x, end) - row_start
    zero = jnp.zeros_like(depth)
    return jnp.stack([depth, first, last, y - col_start, screen_count, zero, zero, zero])


def rate_table(retard, decay):
    species = retard.shape[0]
    factor = (jnp.exp(-decay) / retard) ** STEPS
    place = jnp.minimum(jnp.arange(LANES) % RIGHT // GROUP, species - 1)
    strips = jnp.where(place == 0, retard[0], jnp.where(place == 1, retard[1], retard[2]))
    rows = [jnp.broadcast_to(retard[:, None], (species, LANES)), strips[None]]
    rows.append(jnp.broadcast_to(factor[:, None], (species, LANES)))
    rows.append(jnp.zeros((1, LANES), jnp.float32))
    return jnp.concatenate(rows, axis=0)


def shards(
    initial, logk, direction, face_speed, face_flags, retard, decay, screen_cells, screen_count, well_weight
):
    species, layers, width, columns = initial.shape
    total_x = width * lax.axis_size("gx")
    total_y = columns * lax.axis_size(Y)
    meta = well_table(
        screen_cells, screen_count, lax.axis_index("gx") * width, lax.axis_index(Y) * columns, total_x, total_y
    )
    rates = rate_table(retard, decay)
    f7, e, xa, xb = pack(initial, logk, direction, face_speed, face_flags)
    ea, eb = swaps(e, e, Y)
    xa, xb = add_strips(ea, eb, xa, xb)
    xa, xb = swaps(xa, xb, "gx")
    coef_in, c_in, t_in, jy_in, mask, hot = cone(rates, f7, e, ea, eb, meta)
    partial, coef_out, c_out, jy_out = rim(rates, xa, xb, coef_in, c_in, t_in, mask, hot)
    reach = -(-(screen_cells.shape[1] - 1 + HALO) // width)
    partials = [partial] + from_others(partial, "gx", reach)
    hessian = adjoint(
        rates, well_weight, meta, coef_in, coef_out, c_in, c_out, jy_in, jy_out, mask, partials
    )
    return hessian.reshape(layers, width, columns)


def solution(mesh):
    in_specs = (
        P("grp", None, "gx", Y),
        P("grp", "gx", Y),
        P("grp", "gx", Y),
        P("grp", None, "gx", Y),
        P("grp", None, "gx", Y),
        P(),
        P(),
        P("grp", None),
        P("grp"),
        P("grp", None),
    )
    return jax.shard_map(shards, mesh=mesh, in_specs=in_specs, out_specs=P("grp", "gx", Y), check_vma=False)
```

time: 47.8 us -> 45 us (0.941)
  waiting for transfers between devices: 8.61 us -> 3.64 us
  other arithmetic: 1.45 us -> 4.11 us
  Pallas kernels: 16.5 us -> 14.9 us
  local copies, waits for them, and re-layouts: 6.92 us -> 8.45 us
  starting transfers between devices: 13.8 us -> 13.2 us
    ppermute x4, waiting for transfers between devices: 5.38 us -> 0.01 us  [swaps(): return (lax.ppermute(first, axis, even), lax.ppermute(second, axis, odd))]
    pallas_call x1, Pallas kernels: 6.4 us -> 4.18 us  [adjoint(): pl.pallas_call(functools.partial(adjoint_kernel, layers=layers, width=wid...]
    select_n x0 -> x1, other arithmetic: none -> 1.91 us  [rate_table(): jnp.where(place == 0, retard[0], jnp.where(place == 1, retard[1], retard[...]
    slice x0 -> x1, local copies, waits for them, and re-layouts: none -> 1.41 us  [rate_table(): retard[0]]
    concatenate x0 -> x3, local copies, waits for them, and re-layouts: none -> 0.81 us  [rate_table(): return jnp.concatenate(rows, axis=0)]
    unnamed x16 -> x12, local copies, waits for them, and re-layouts: 5.39 us -> 4.71 us
    mul x0 -> x1, other arithmetic: none -> 0.68 us  [rate_table(): factor = (jnp.exp(-decay) / retard) ** STEPS]
    pallas_call x1, Pallas kernels: 0.62 us -> 1.22 us  [pack(): pl.pallas_call(functools.partial(pack_kernel, layers=layers, width=width,...]
  transfers between devices with their start and end apart: 7 -> 7, of which waited for: 3 -> 2; matrix products, arithmetic and copies ran while one was open for 6% -> 18% of each run, Pallas kernels for 0% -> 11%
where the time goes in v2:
time: 45 us; the launch traced here: 44.5 us
  Pallas kernels  14.9 us (33%)
  starting transfers between devices  13.2 us (29%)
  local copies, waits for them, and re-layouts  8.45 us (19%)
  other arithmetic  4.11 us (9%)
  waiting for transfers between devices  3.64 us (8%)
    ppermute x4, starting transfers between devices, swaps(): return (lax.ppermute(first, axis, even), lax.ppermute(second, axis, odd))  7.33 us
    ppermute x3, starting transfers between devices, from_others(): lax.ppermute(value, axis, [(i, i ^ d) for i in range(count)])  5.92 us
    pallas_call x1, Pallas kernels, cone(): pl.pallas_call(functools.partial(cone_kernel, layers=layers, width=width,...  5.11 us
    unnamed x12, local copies, waits for them, and re-layouts  4.71 us
    pallas_call x1, Pallas kernels, rim(): pl.pallas_call(functools.partial(rim_kernel, layers=layers, width=width,...  4.37 us
    pallas_call x1, Pallas kernels, adjoint(): pl.pallas_call(functools.partial(adjoint_kernel, layers=layers, width=wid...  4.18 us
    ppermute x3, waiting for transfers between devices, from_others(): lax.ppermute(value, axis, [(i, i ^ d) for i in range(count)])  3.63 us
    select_n x1, other arithmetic, rate_table(): jnp.where(place == 0, retard[0], jnp.where(place == 1, retard[1], retard[...  1.91 us
  transfers between devices with their start and end apart: 7, of which 2 were waited for; matrix products, arithmetic and copies ran while one was open for 18% of the time, Pallas kernels for 11%

profile of v2, /device:TPU:0, one launch (start us, length us, event | category | flops | bytes accessed | tf_op | source)
XLA Modules:
  0.0 44.5 jit_solution(3587033238004781137)
XLA Ops:
  0.0 1.0 %copy-done = f32[3,16,16,128]{3,2,1,0:T(8,128)S(1)} copy-done((f32[3,16,16,128]{3,2,1,0:T(8,128)S(1)}, f32[3,16,16,128]{3,2,1,0:T(8,128)}, u32[]{:S(2)}) %copy-start) | copy-done | bytes 393240
  1.0 0.9 %copy-done.1 = f32[2,16,16,128]{3,2,1,0:T(8,128)S(1)} copy-done((f32[2,16,16,128]{3,2,1,0:T(8,128)S(1)}, f32[2,16,16,128]{3,2,1,0:T(8,128)}, u32[]{:S(2)}) %copy-start.1) | copy-done | bytes 262168
  1.9 0.9 %copy-done.2 = s32[2,16,16,128]{3,2,1,0:T(8,128)S(1)} copy-done((s32[2,16,16,128]{3,2,1,0:T(8,128)S(1)}, s32[2,16,16,128]{3,2,1,0:T(8,128)}, u32[]{:S(2)}) %copy-start.2) | copy-done | bytes 262168
  2.9 0.9 %copy-done.3 = f32[16,16,128]{2,1,0:T(8,128)S(1)} copy-done((f32[16,16,128]{2,1,0:T(8,128)S(1)}, f32[16,16,128]{2,1,0:T(8,128)}, u32[]{:S(2)}) %copy-start.3) | copy-done | bytes 131096
  3.8 0.9 %copy-done.4 = f32[16,16,128]{2,1,0:T(8,128)S(1)} copy-done((f32[16,16,128]{2,1,0:T(8,128)S(1)}, f32[16,16,128]{2,1,0:T(8,128)}, u32[]{:S(2)}) %copy-start.4) | copy-done | bytes 131096
  4.7 1.2 %pack.1 = (f32[16,7,16,128]{3,2,1,0:T(8,128)S(1)}, f32[16,16,128]{2,1,0:T(8,128)S(1)}, f32[4,8,16,128]{3,2,1,0:T(8,128)S(1)}, f32[4,8,16,128]{3,2,1,0:T(8,128)S(1)}) custom-call(f32[768,128]{1,0:T(8,128)S(1)} %bitcast.23, f32[256,128]{1,0:T(8,128)S(1)} %bitcast.26, f32[256,128]{1,0:T(8,128)S(1)} %bitcast.27, f32[512,128]{1,0:T(8,128)S(1)} %bitcast.24, ...), custom_call_target="tpu_custom_call" | custom-call | tf_op jit(solution)/shard_map/pack/pallas_call | solution.py:138
  5.9 0.7 %collective-permute-start.1 = (f32[16,16,128]{2,1,0:T(8,128)S(1)}, f32[16,16,128]{2,1,0:T(8,128)S(1)}, u32[]{:S(2)}, u32[]{:S(2)}) collective-permute-start(f32[16,16,128]{2,1,0:T(8,128)S(1)} %get-tuple-element.22.e_ref), channel_id=1, source_target_pairs={{1,2},{2,1},{5,6},{6,5},{9,10},{10,9},{13,14},{14,13},{17,18},{18,... | collective-permute-start | bytes 393224 | tf_op jit(solution)/shard_map/ppermute | solution.py:621
  6.6 4.4 %collective-permute-start = (f32[16,16,128]{2,1,0:T(8,128)S(1)}, f32[16,16,128]{2,1,0:T(8,128)S(1)}, u32[]{:S(2)}, u32[]{:S(2)}) collective-permute-start(f32[16,16,128]{2,1,0:T(8,128)S(1)} %get-tuple-element.22.e_ref), channel_id=1, source_target_pairs={{0,1},{1,0},{2,3},{3,2},{4,5},{5,4},{6,7},{7,6},{8,9},{9,8},{10,11... | collective-permute-start | bytes 393224 | tf_op jit(solution)/shard_map/ppermute | solution.py:621
  11.0 0.8 %slice_reduce_fusion.1 = (s32[384]{0:T(512)S(1)}, s32[384]{0:T(512)S(1)}) fusion(s32[384,32]{0,1:T(8,128)} %param.17), kind=kLoop, calls=%fused_computation.41 | loop fusion | bytes 6144 | tf_op jit(solution)/shard_map/slice | solution.py:636
  11.8 0.7 %fusion.8 = (s32[1,384]{1,0:T(1,128)S(1)}, s32[1,384]{1,0:T(1,128)S(1)}) fusion(s32[]{:T(128)S(6)} %mul.23, s32[384,32]{0,1:T(8,128)} %param.17), kind=kLoop, calls=%fused_computation.34 | loop fusion | flops 9216 | bytes 4612 | tf_op jit(solution)/shard_map/sub | solution.py:644
  12.5 0.7 %fusion.1 = (s32[384]{0:T(512)S(1)}, s32[384]{0:T(512)S(1)}) fusion(s32[]{:T(128)S(6)} %mul.21, s32[384]{0:T(512)S(1)} %get-tuple-element.37, s32[384]{0:T(512)S(1)} %get-tuple-element.38, s32[384]{0:T(512)} %param.18), kind=kLoop, calls=%fused_computation.21 | loop fusion | flops 18048 | bytes 7684 | tf_op jit(solution)/shard_map/sub | solution.py:642
  13.2 0.7 %multiply_multiply_fusion = f32[3]{0:T(128)S(1)} fusion(f32[3]{0:T(128)} %param.15, f32[3]{0:T(128)} %param.16), kind=kLoop, calls=%fused_computation.40 | loop fusion | flops 12 | bytes 36 | tf_op jit(solution)/shard_map/mul | solution.py:649
  13.9 1.4 %fusion.10 = (f32[1]{0:T(128)}, f32[1]{0:T(128)}, f32[1]{0:T(128)}) fusion(f32[3]{0:T(128)} %param.15), kind=kLoop, calls=%fused_computation.42 | loop fusion | bytes 24 | tf_op jit(solution)/shard_map/slice | solution.py:651
  15.4 1.6 %collective-permute-start.2 = (f32[4,8,16,128]{3,2,1,0:T(8,128)S(1)}, f32[4,8,16,128]{3,2,1,0:T(8,128)S(1)}, u32[]{:S(2)}, u32[]{:S(2)}) collective-permute-start(f32[4,8,16,128]{3,2,1,0:T(8,128)S(1)} %get-tuple-element.26), channel_id=1, source_target_pairs={{0,4},{4,0},{8,12},{12,8},{1,5},{5,1},{9,13},{13,9},{2,6},{6,2},{1... | collective-permute-start | bytes 786440 | tf_op jit(solution)/shard_map/ppermute | solution.py:621
  17.1 0.7 %collective-permute-start.3 = (f32[4,8,16,128]{3,2,1,0:T(8,128)S(1)}, f32[4,8,16,128]{3,2,1,0:T(8,128)S(1)}, u32[]{:S(2)}, u32[]{:S(2)}) collective-permute-start(f32[4,8,16,128]{3,2,1,0:T(8,128)S(1)} %get-tuple-element.27), channel_id=1, source_target_pairs={{4,8},{8,4},{5,9},{9,5},{6,10},{10,6},{7,11},{11,7},{20,24},{24,20... | collective-permute-start | bytes 786440 | tf_op jit(solution)/shard_map/ppermute | solution.py:621
  17.7 1.9 %compare_select_fusion.1 = f32[1,128]{1,0:T(1,128)S(1)} fusion(f32[]{:T(128)} %bitcast.2, f32[]{:T(128)} %bitcast.1, f32[]{:T(128)} %bitcast), kind=kLoop, calls=%fused_computation.31 | loop fusion | flops 3328 | bytes 524 | tf_op jit(solution)/shard_map/jit(_where)/select_n | solution.py:651
  19.6 0.7 %stack.19 = s32[1,384]{1,0:T(1,128)S(1)} reshape(s32[384]{0:T(512)} %param.18) | data formatting | bytes 3072 | tf_op jit(solution)/shard_map/stack | solution.py:644
  21.3 5.1 %cone_steps.1 = (f32[16,12,2,16,128]{4,3,2,1,0:T(8,128)S(1)}, f32[4,16,4,16,128]{4,3,2,1,0:T(8,128)S(1)}, f32[4,16,4,16,128]{4,3,2,1,0:T(8,128)S(1)}, f32[4,16,4...) custom-call(f32[8,128]{1,0:T(8,128)S(1)} %maximum_maximum_fusion.rate_ref, ...), custom_call_target="tpu_custom_call" | custom-call | flops 10000000 | bytes 10000000 | tf_op jit(solution)/shard_map/cone_steps/pallas_call | solution.py:362
  26.4 4.4 %rim_steps.1 = (f32[3,384]{1,0:T(4,128)S(1)}, f32[10,12,2,16,128]{4,3,2,1,0:T(8,128)S(1)}, f32[4,8,4,16,128]{4,3,2,1,0:T(8,128)S(1)}, f32[4,8,4,16,128]{4,3,2,1,0:T(8,128)S(1)}) custom-call(f32[8,128]{1,0:T(8,128)S(1)} %maximum_maximum_fusion.rate_ref, f32[4,8,16,128]{3,2,1,0:T(8,128)S(1)} %collective-permute-done.2.xa_ref, ...), custom_call_target="tpu_custom_call" | custom-call | tf_op jit(solution)/shard_map/rim_steps/pallas_call | solution.py:488
  30.8 2.5 %collective-permute-start.6 = (f32[3,384]{1,0:T(4,128)S(1)}, f32[3,384]{1,0:T(4,128)S(1)}, u32[]{:S(2)}, u32[]{:S(2)}) collective-permute-start(f32[3,384]{1,0:T(4,128)S(1)} %get-tuple-element.36.partial_ref), channel_id=1, source_target_pairs={{0,12},{4,8},{8,4},{12,0},{1,13},{5,9},{9,5},{13,1},{2,14},{6,10},... | collective-permute-start | bytes 13832 | tf_op jit(solution)/shard_map/ppermute | solution.py:627
  33.3 3.4 %collective-permute-start.5 = (f32[3,384]{1,0:T(4,128)S(1)}, f32[3,384]{1,0:T(4,128)S(1)}, u32[]{:S(2)}, u32[]{:S(2)}) collective-permute-start(f32[3,384]{1,0:T(4,128)S(1)} %get-tuple-element.36.partial_ref), channel_id=1, source_target_pairs={{0,8},{4,12},{8,0},{12,4},{1,9},{5,13},{9,1},{13,5},{2,10},{6,14},... | collective-permute-start | bytes 13832 | tf_op jit(solution)/shard_map/ppermute | solution.py:627
  36.7 1.7 %collective-permute-done.5.rest_1_ = f32[3,384]{1,0:T(4,128)S(1)} collective-permute-done((f32[3,384]{1,0:T(4,128)S(1)}, f32[3,384]{1,0:T(4,128)S(1)}, u32[]{:S(2)}, u32[]{:S(2)}) %collective-permute-start.5) | collective-permute-done | bytes 4640 | tf_op jit(solution)/shard_map/ppermute | solution.py:627
  38.4 2.0 %collective-permute-done.4.rest_0_ = f32[3,384]{1,0:T(4,128)S(1)} collective-permute-done((f32[3,384]{1,0:T(4,128)S(1)}, f32[3,384]{1,0:T(4,128)S(1)}, u32[]{:S(2)}, u32[]{:S(2)}) %collective-permute-start.4) | collective-permute-done | bytes 4640 | tf_op jit(solution)/shard_map/ppermute | solution.py:627
  40.3 4.2 %adjoint_steps.1 = f32[256,128]{1,0:T(8,128)} custom-call(f32[8,128]{1,0:T(8,128)S(1)} %maximum_maximum_fusion.rate_ref, f32[3,384]{1,0:T(4,128)S(1)} %copy-done.5, s32[8,384]{1,0:T(8,128)S(1)} %stack.21.meta_ref, f32[16,12,2,16,128]{4,3,2,1,0:T(8,128)S(1)} %get-tuple-element.23.coef_in, f32[10,12,2,16,128]{4,3,2,1,0:T(8,128)S(1)} %get-tuple-element.32.coef_out, ...), custom_call_target="tpu_custom_call" | custom-call | tf_op jit(solution)/shard_map/adjoint_steps/pallas_call | solution.py:606
  (24 shorter events, 1.0 us)
Async XLA Ops:
  0.0 1.0 %copy-start = (f32[3,16,16,128]{3,2,1,0:T(8,128)S(1)}, f32[3,16,16,128]{3,2,1,0:T(8,128)}, u32[]{:S(2)}) copy-start(f32[3,16,16,128]{3,2,1,0:T(8,128)} %param.10) | copy-start | bytes 1179652
  1.0 0.9 %copy-start.1 = (f32[2,16,16,128]{3,2,1,0:T(8,128)S(1)}, f32[2,16,16,128]{3,2,1,0:T(8,128)}, u32[]{:S(2)}) copy-start(f32[2,16,16,128]{3,2,1,0:T(8,128)} %param.13) | copy-start | bytes 786436
  1.9 0.9 %copy-start.2 = (s32[2,16,16,128]{3,2,1,0:T(8,128)S(1)}, s32[2,16,16,128]{3,2,1,0:T(8,128)}, u32[]{:S(2)}) copy-start(s32[2,16,16,128]{3,2,1,0:T(8,128)} %param.14) | copy-start | bytes 786436
  2.9 0.9 %copy-start.3 = (f32[16,16,128]{2,1,0:T(8,128)S(1)}, f32[16,16,128]{2,1,0:T(8,128)}, u32[]{:S(2)}) copy-start(f32[16,16,128]{2,1,0:T(8,128)} %param.11) | copy-start | bytes 393220
  3.8 0.9 %copy-start.4 = (f32[16,16,128]{2,1,0:T(8,128)S(1)}, f32[16,16,128]{2,1,0:T(8,128)}, u32[]{:S(2)}) copy-start(f32[16,16,128]{2,1,0:T(8,128)} %param.12) | copy-start | bytes 393220
  5.9 9.4 %collective-permute-start.1 = (f32[16,16,128]{2,1,0:T(8,128)S(1)}, f32[16,16,128]{2,1,0:T(8,128)S(1)}, u32[]{:S(2)}, u32[]{:S(2)}) collective-permute-start(f32[16,16,128]{2,1,0:T(8,128)S(1)} %get-tuple-element.22.e_ref), channel_id=1, source_target_pairs={{1,2},{2,1},{5,6},{6,5},{9,10},{10,9},{13,14},{14,13},{17,18},{18,... | collective-permute-start | bytes 393224 | tf_op jit(solution)/shard_map/ppermute | solution.py:621
  6.6 8.7 %collective-permute-start = (f32[16,16,128]{2,1,0:T(8,128)S(1)}, f32[16,16,128]{2,1,0:T(8,128)S(1)}, u32[]{:S(2)}, u32[]{:S(2)}) collective-permute-start(f32[16,16,128]{2,1,0:T(8,128)S(1)} %get-tuple-element.22.e_ref), channel_id=1, source_target_pairs={{0,1},{1,0},{2,3},{3,2},{4,5},{5,4},{6,7},{7,6},{8,9},{9,8},{10,11... | collective-permute-start | bytes 393224 | tf_op jit(solution)/shard_map/ppermute | solution.py:621
  15.4 11.0 %collective-permute-start.2 = (f32[4,8,16,128]{3,2,1,0:T(8,128)S(1)}, f32[4,8,16,128]{3,2,1,0:T(8,128)S(1)}, u32[]{:S(2)}, u32[]{:S(2)}) collective-permute-start(f32[4,8,16,128]{3,2,1,0:T(8,128)S(1)} %get-tuple-element.26), channel_id=1, source_target_pairs={{0,4},{4,0},{8,12},{12,8},{1,5},{5,1},{9,13},{13,9},{2,6},{6,2},{1... | collective-permute-start | bytes 786440 | tf_op jit(solution)/shard_map/ppermute | solution.py:621
  17.1 9.3 %collective-permute-start.3 = (f32[4,8,16,128]{3,2,1,0:T(8,128)S(1)}, f32[4,8,16,128]{3,2,1,0:T(8,128)S(1)}, u32[]{:S(2)}, u32[]{:S(2)}) collective-permute-start(f32[4,8,16,128]{3,2,1,0:T(8,128)S(1)} %get-tuple-element.27), channel_id=1, source_target_pairs={{4,8},{8,4},{5,9},{9,5},{6,10},{10,6},{7,11},{11,7},{20,24},{24,20... | collective-permute-start | bytes 786440 | tf_op jit(solution)/shard_map/ppermute | solution.py:621
  26.4 13.9 %copy-start.5 = (f32[3,384]{1,0:T(4,128)S(1)}, f32[3,384]{1,0:T(4,128)}, u32[]{:S(2)}) copy-start(f32[3,384]{1,0:T(4,128)} %weight_ref.1) | copy-start | bytes 13828
  30.8 5.9 %collective-permute-start.6 = (f32[3,384]{1,0:T(4,128)S(1)}, f32[3,384]{1,0:T(4,128)S(1)}, u32[]{:S(2)}, u32[]{:S(2)}) collective-permute-start(f32[3,384]{1,0:T(4,128)S(1)} %get-tuple-element.36.partial_ref), channel_id=1, source_target_pairs={{0,12},{4,8},{8,4},{12,0},{1,13},{5,9},{9,5},{13,1},{2,14},{6,10},... | collective-permute-start | bytes 13832 | tf_op jit(solution)/shard_map/ppermute | solution.py:627
  33.3 5.0 %collective-permute-start.5 = (f32[3,384]{1,0:T(4,128)S(1)}, f32[3,384]{1,0:T(4,128)S(1)}, u32[]{:S(2)}, u32[]{:S(2)}) collective-permute-start(f32[3,384]{1,0:T(4,128)S(1)} %get-tuple-element.36.partial_ref), channel_id=1, source_target_pairs={{0,8},{4,12},{8,0},{12,4},{1,9},{5,13},{9,1},{13,5},{2,10},{6,14},... | collective-permute-start | bytes 13832 | tf_op jit(solution)/shard_map/ppermute | solution.py:627
  36.7 3.6 %collective-permute-start.4 = (f32[3,384]{1,0:T(4,128)S(1)}, f32[3,384]{1,0:T(4,128)S(1)}, u32[]{:S(2)}, u32[]{:S(2)}) collective-permute-start(f32[3,384]{1,0:T(4,128)S(1)} %get-tuple-element.36.partial_ref), channel_id=1, source_target_pairs={{0,4},{4,0},{8,12},{12,8},{1,5},{5,1},{9,13},{13,9},{2,6},{6,2},{1... | collective-permute-start | bytes 13832 | tf_op jit(solution)/shard_map/ppermute | solution.py:627

commit v3 on v2

--- a/solution.py
+++ b/solution.py
@@ -21,6 +21,10 @@
 KINDS = 12
 VMEM = pl.BlockSpec(memory_space=pltpu.VMEM)
 HBM = pl.BlockSpec(memory_space=pltpu.HBM)
+
+
+def in_hbm(*arrays):
+    return [pltpu.with_memory_space_constraint(a, pltpu.HBM) for a in arrays]
 
 
 def lane_of(shape):
@@ -148,7 +152,7 @@
         scratch_shapes=[pltpu.VMEM(a.shape, a.dtype) for a in sources] + [pltpu.SemaphoreType.DMA((5,))],
         compiler_params=pltpu.CompilerParams(vmem_limit_bytes=5 * MIB),
         name="pack",
-    )(*sources)
+    )(*in_hbm(*sources))
 
 
 def strips_kernel(ea_ref, eb_ref, xa_in, xb_in, xa_ref, xb_ref, buf_a, buf_b, sem_a, sem_b, *, width, count):
@@ -281,20 +285,41 @@
         put_t(s, source)
 
 
-def well_rows(meta_ref):
-    return [meta_ref[i : i + 1, :] for i in range(4)]
-
-
 def strip_columns(wells):
     own = lax.broadcasted_iota(jnp.int32, (LANES, wells), 0)
     return own, own % RIGHT // GROUP, own % GROUP + jnp.where(own < RIGHT, -8, 120)
 
 
+def divide(value, by):
+    return lax.shift_right_logical(value, by.bit_length() - 1) if by & (by - 1) == 0 else lax.div(value, by)
+
+
+def well_table(cells, counts, width):
+    total_x, total_y = width * lax.axis_size("gx"), LANES * lax.axis_size(Y)
+    start, second = cells[0:1], cells[1:2]
+    depth = divide(start, total_x * total_y)
+    rest = start - depth * (total_x * total_y)
+    x = divide(rest, total_y)
+    y = rest - x * total_y
+    end = x + jnp.where(second > start, counts - 1, 1 - counts)
+    row_start, col_start = lax.axis_index("gx") * width, lax.axis_index(Y) * LANES
+    return [depth, jnp.minimum(x, end) - row_start, jnp.maximum(x, end) - row_start, y - col_start, counts]
+
+
 def cone_kernel(
-    rate_ref, f7_ref, e_ref, ea_ref, eb_ref, meta_ref,
-    coef_ref, c_ref, t_ref, jy_ref, mask_ref, hot_ref, *, layers, width, species,
+    retard_hbm, decay_hbm, cells_hbm, count_hbm, f7_ref, e_ref, ea_ref, eb_ref,
+    coef_ref, c_ref, t_ref, jy_ref, mask_ref, hot_ref, rate_ref, meta_ref,
+    retard_ref, decay_ref, cells_ref, count_ref, sem, *, layers, width, species,
 ):
     f32, bf16 = jnp.float32, jnp.bfloat16
+    copies = [
+        pltpu.make_async_copy(a, b, sem.at[i])
+        for i, (a, b) in enumerate(
+            ((retard_hbm, retard_ref), (decay_hbm, decay_ref), (cells_hbm, cells_ref), (count_hbm, count_ref))
+        )
+    ]
+    for copy in copies:
+        copy.start()
     column, near, left, main_mask, strip_mask = masks(layers)
     even_y = lax.rem(lax.axis_index(Y), 2) == 0
     count = species + 4
@@ -322,6 +347,18 @@
                 coef_ref[x, PX, i] = ux[i]
         kept = (k, kd, ux)
 
+    for copy in copies:
+        copy.wait()
+    lane = lane_of((1, LANES))
+    strips = jnp.full((1, LANES), retard_ref[species - 1], f32)
+    for s in range(species):
+        rate = jnp.full((1, LANES), retard_ref[s], f32)
+        strips = jnp.where(lane % RIGHT // GROUP == s, rate, strips)
+        factor = jnp.exp(jnp.full((1, LANES), -decay_ref[s], f32)) / rate
+        rate_ref[s : s + 1, :] = rate
+        rate_ref[species + 1 + s : species + 2 + s, :] = factor**STEPS
+    rate_ref[species : species + 1, :] = strips
+
     rates = [rate_ref[s : s + 1, :] for s in range(species + 1)]
     for m in range(STEPS):
         for r in range(HALO + 1 + m, HALO + width - 1 - m):
@@ -341,8 +378,13 @@
                 put(c_ref, m + 1), put(t_ref, m), put(jy_ref, m),
             )
 
-    depth, first, last, where_y = well_rows(meta_ref)
     wells = meta_ref.shape[1]
+    cells = cells_ref[...]
+    cells = jnp.concatenate([cells, jnp.zeros((wells, LANES - cells.shape[1]), jnp.int32)], axis=1)
+    table = well_table(cells.T, count_ref[...].reshape(1, wells), width)
+    for i, row in enumerate(table):
+        meta_ref[i : i + 1, :] = row
+    depth, first, last, where_y = table[:4]
     in_layer = lax.broadcasted_iota(jnp.int32, (layers, wells), 0) == depth
     for r in range(width + 2 * HALO):
         inside = (first <= r - HALO) & (last >= r - HALO) & in_layer
@@ -354,10 +396,10 @@
         hot_ref[s, LANES : 2 * LANES] = jnp.where(hit & (strip_species == s), 1.0, 0.0).astype(bf16)
 
 
-def cone(rates, f7, e, ea, eb, meta):
+def cone(retard, decay, cells, counts, f7, e, ea, eb):
     width, count, layers, _ = f7.shape
-    species, wells = count - 4, meta.shape[1]
-    f32 = jnp.float32
+    species, wells = count - 4, counts.shape[0]
+    f32, i32 = jnp.float32, jnp.int32
     state = jax.ShapeDtypeStruct((STEPS, width, species + 1, layers, LANES), f32)
     return pl.pallas_call(
         functools.partial(cone_kernel, layers=layers, width=width, species=species),
@@ -368,13 +410,22 @@
             state,
             jax.ShapeDtypeStruct(((width + 2 * HALO) * layers, wells), jnp.bfloat16),
             jax.ShapeDtypeStruct((species, 2 * LANES, wells), jnp.bfloat16),
+            jax.ShapeDtypeStruct((2 * species + 2, LANES), f32),
+            jax.ShapeDtypeStruct((TILE, wells), i32),
         ),
-        in_specs=[VMEM] * 6,
-        out_specs=[VMEM] * 6,
+        in_specs=[HBM] * 4 + [VMEM] * 4,
+        out_specs=[VMEM] * 8,
+        scratch_shapes=[
+            pltpu.SMEM(retard.shape, f32),
+            pltpu.SMEM(decay.shape, f32),
+            pltpu.VMEM(cells.shape, i32),
+            pltpu.VMEM(counts.shape, i32),
+            pltpu.SemaphoreType.DMA((4,)),
+        ],
         compiler_params=pltpu.CompilerParams(vmem_limit_bytes=4 * MIB),
         cost_estimate=pl.CostEstimate(flops=10**7, bytes_accessed=10**7, transcendentals=0),
         name="cone_steps",
-    )(rates, f7, e, ea, eb, meta)
+    )(*in_hbm(retard, decay, cells, counts), f7, e, ea, eb)
 
 
 def rim_kernel(
@@ -632,44 +683,17 @@
     ]
 
 
-def well_table(screen_cells, screen_count, row_start, col_start, total_x, total_y):
-    start, second = screen_cells[:, 0], screen_cells[:, 1]
-    plane = total_x * total_y
-    depth = start // plane
-    x = start % plane // total_y
-    y = start % total_y
-    end = x + (screen_count - 1) * ((second - start) // total_y)
-    first, last = jnp.minimum(x, end) - row_start, jnp.maximum(x, end) - row_start
-    zero = jnp.zeros_like(depth)
-    return jnp.stack([depth, first, last, y - col_start, screen_count, zero, zero, zero])
-
-
-def rate_table(retard, decay):
-    species = retard.shape[0]
-    factor = (jnp.exp(-decay) / retard) ** STEPS
-    place = jnp.minimum(jnp.arange(LANES) % RIGHT // GROUP, species - 1)
-    strips = jnp.where(place == 0, retard[0], jnp.where(place == 1, retard[1], retard[2]))
-    rows = [jnp.broadcast_to(retard[:, None], (species, LANES)), strips[None]]
-    rows.append(jnp.broadcast_to(factor[:, None], (species, LANES)))
-    rows.append(jnp.zeros((1, LANES), jnp.float32))
-    return jnp.concatenate(rows, axis=0)
-
-
 def shards(
     initial, logk, direction, face_speed, face_flags, retard, decay, screen_cells, screen_count, well_weight
 ):
     species, layers, width, columns = initial.shape
-    total_x = width * lax.axis_size("gx")
-    total_y = columns * lax.axis_size(Y)
-    meta = well_table(
-        screen_cells, screen_count, lax.axis_index("gx") * width, lax.axis_index(Y) * columns, total_x, total_y
-    )
-    rates = rate_table(retard, decay)
     f7, e, xa, xb = pack(initial, logk, direction, face_speed, face_flags)
     ea, eb = swaps(e, e, Y)
     xa, xb = add_strips(ea, eb, xa, xb)
     xa, xb = swaps(xa, xb, "gx")
-    coef_in, c_in, t_in, jy_in, mask, hot = cone(rates, f7, e, ea, eb, meta)
+    coef_in, c_in, t_in, jy_in, mask, hot, rates, meta = cone(
+        retard, decay, screen_cells, screen_count, f7, e, ea, eb
+    )
     partial, coef_out, c_out, jy_out = rim(rates, xa, xb, coef_in, c_in, t_in, mask, hot)
     reach = -(-(screen_cells.shape[1] - 1 + HALO) // width)
     partials = [partial] + from_others(partial, "gx", reach)

time: 45 us -> 36.4 us (0.81)
  local copies, waits for them, and re-layouts: 8.45 us -> 1.62 us
  other arithmetic: 4.11 us -> 0 us
  Pallas kernels: 14.9 us -> 16.4 us
  waiting for transfers between devices: 3.64 us -> 4.62 us
    unnamed x12 -> x3, local copies, waits for them, and re-layouts: 4.71 us -> 1.62 us
    slice x2 -> x0, local copies, waits for them, and re-layouts: 2.21 us -> none  [the longest x1 1.41 us: rate_table(): retard[0]]
    select_n x1 -> x0, other arithmetic: 1.91 us -> none  [rate_table(): jnp.where(place == 0, retard[0], jnp.where(place == 1, retard[1], retard[...]
    sub x3 -> x0, other arithmetic: 1.45 us -> none  [the longest x1 0.72 us: well_table(): y - col_start]
    ppermute x4, waiting for transfers between devices: 0.01 us -> 0.99 us  [swaps(): return (lax.ppermute(first, axis, even), lax.ppermute(second, axis, odd))]
    concatenate x3 -> x0, local copies, waits for them, and re-layouts: 0.81 us -> none  [rate_table(): return jnp.concatenate(rows, axis=0)]
    pallas_call x1, Pallas kernels: 5.11 us -> 5.89 us  [cone(): pl.pallas_call(functools.partial(cone_kernel, layers=layers, width=width,...]
    another operation x6 -> x0, local copies, waits for them, and re-layouts: 0.73 us -> none  [the longest x5 0.72 us: well_table(): jnp.stack([depth, first, last, y - col_start, screen_count, zero, zero, z...]
  transfers between devices with their start and end apart: 7 -> 7, of which waited for: 2 -> 3; matrix products, arithmetic and copies ran while one was open for 18% -> 4% of each run, Pallas kernels for 11% -> 16%
where the time goes in v3:
time: 36.4 us; the launch traced here: 35.9 us
  Pallas kernels  16.4 us (45%)
  starting transfers between devices  13.2 us (36%)
  waiting for transfers between devices  4.62 us (13%)
  local copies, waits for them, and re-layouts  1.62 us (4%)
    ppermute x4, starting transfers between devices, swaps(): return (lax.ppermute(first, axis, even), lax.ppermute(second, axis, odd))  7.33 us
    ppermute x3, starting transfers between devices, from_others(): lax.ppermute(value, axis, [(i, i ^ d) for i in range(count)])  5.91 us
    pallas_call x1, Pallas kernels, cone(): pl.pallas_call(functools.partial(cone_kernel, layers=layers, width=width,...  5.89 us
    pallas_call x1, Pallas kernels, rim(): pl.pallas_call(functools.partial(rim_kernel, layers=layers, width=width,...  4.37 us
    pallas_call x1, Pallas kernels, adjoint(): pl.pallas_call(functools.partial(adjoint_kernel, layers=layers, width=wid...  4.18 us
    ppermute x3, waiting for transfers between devices, from_others(): lax.ppermute(value, axis, [(i, i ^ d) for i in range(count)])  3.63 us
    pallas_call x1, Pallas kernels, pack(): pl.pallas_call(functools.partial(pack_kernel, layers=layers, width=width,...  1.9 us
    unnamed x3, local copies, waits for them, and re-layouts  1.62 us
  transfers between devices with their start and end apart: 7, of which 3 were waited for; matrix products, arithmetic and copies ran while one was open for 4% of the time, Pallas kernels for 16%

profile of v3, /device:TPU:0, one launch (start us, length us, event | category | flops | bytes accessed | tf_op | source)
XLA Modules:
  0.0 35.9 jit_solution(11245590316746688553)
XLA Ops:
  0.0 1.9 %pack.1 = (f32[16,7,16,128]{3,2,1,0:T(8,128)S(1)}, f32[16,16,128]{2,1,0:T(8,128)S(1)}, f32[4,8,16,128]{3,2,1,0:T(8,128)S(1)}, f32[4,8,16,128]{3,2,1,0:T(8,128)S(1)}) custom-call(f32[768,128]{1,0:T(8,128)} %bitcast.6, f32[256,128]{1,0:T(8,128)} %bitcast.9, f32[256,128]{1,0:T(8,128)} %bitcast.10, f32[512,128]{1,0:T(8,128)} %bitcast.7, s32[512,128]{1,0:T(8,128)} %bitcast.8), custom_call_target="tpu_custom_call" | custom-call | tf_op jit(solution)/shard_map/pack/pallas_call | solution.py:142
  1.9 0.7 %collective-permute-start.1 = (f32[16,16,128]{2,1,0:T(8,128)S(1)}, f32[16,16,128]{2,1,0:T(8,128)S(1)}, u32[]{:S(2)}, u32[]{:S(2)}) collective-permute-start(f32[16,16,128]{2,1,0:T(8,128)S(1)} %get-tuple-element.24.e_ref), channel_id=1, source_target_pairs={{1,2},{2,1},{5,6},{6,5},{9,10},{10,9},{13,14},{14,13},{17,18},{18,... | collective-permute-start | bytes 393224 | tf_op jit(solution)/shard_map/ppermute | solution.py:672
  2.6 4.4 %collective-permute-start = (f32[16,16,128]{2,1,0:T(8,128)S(1)}, f32[16,16,128]{2,1,0:T(8,128)S(1)}, u32[]{:S(2)}, u32[]{:S(2)}) collective-permute-start(f32[16,16,128]{2,1,0:T(8,128)S(1)} %get-tuple-element.24.e_ref), channel_id=1, source_target_pairs={{0,1},{1,0},{2,3},{3,2},{4,5},{5,4},{6,7},{7,6},{8,9},{9,8},{10,11... | collective-permute-start | bytes 393224 | tf_op jit(solution)/shard_map/ppermute | solution.py:672
  6.9 0.0 collective-permute-done.1.eb_ref
  7.0 1.0 %collective-permute-done.ea_ref = f32[16,16,128]{2,1,0:T(8,128)S(1)} collective-permute-done((f32[16,16,128]{2,1,0:T(8,128)S(1)}, f32[16,16,128]{2,1,0:T(8,128)S(1)}, u32[]{:S(2)}, u32[]{:S(2)}) %collective-permute-start) | collective-permute-done | bytes 131104 | tf_op jit(solution)/shard_map/ppermute | solution.py:672
  7.9 0.1 corner_strips.1
  8.0 1.6 %collective-permute-start.2 = (f32[4,8,16,128]{3,2,1,0:T(8,128)S(1)}, f32[4,8,16,128]{3,2,1,0:T(8,128)S(1)}, u32[]{:S(2)}, u32[]{:S(2)}) collective-permute-start(f32[4,8,16,128]{3,2,1,0:T(8,128)S(1)} %get-tuple-element.30), channel_id=1, source_target_pairs={{0,4},{4,0},{8,12},{12,8},{1,5},{5,1},{9,13},{13,9},{2,6},{6,2},{1... | collective-permute-start | bytes 786440 | tf_op jit(solution)/shard_map/ppermute | solution.py:672
  9.6 0.7 %collective-permute-start.3 = (f32[4,8,16,128]{3,2,1,0:T(8,128)S(1)}, f32[4,8,16,128]{3,2,1,0:T(8,128)S(1)}, u32[]{:S(2)}, u32[]{:S(2)}) collective-permute-start(f32[4,8,16,128]{3,2,1,0:T(8,128)S(1)} %get-tuple-element.31), channel_id=1, source_target_pairs={{4,8},{8,4},{5,9},{9,5},{6,10},{10,6},{7,11},{11,7},{20,24},{24,20... | collective-permute-start | bytes 786440 | tf_op jit(solution)/shard_map/ppermute | solution.py:672
  10.3 1.6 %copy.13.cells_hbm = s32[384,32]{1,0:T(8,128)} copy(s32[384,32]{0,1:T(8,128)} %param.17) | data formatting | bytes 98304 | tf_op args[7]
  11.9 5.9 %cone_steps.1 = (f32[16,12,2,16,128]{4,3,2,1,0:T(8,128)S(1)}, f32[4,16,4,16,128]{4,3,2,1,0:T(8,128)S(1)}, f32[4,16,4,16,128]{4,3,2,1,0:T(8,128)S(1)}, f32[4,16,4...) custom-call(f32[3]{0:T(128)} %retard_hbm.1, ...), custom_call_target="tpu_custom_call" | custom-call | flops 10000000 | bytes 10000000 | tf_op jit(solution)/shard_map/cone_steps/pallas_call | solution.py:404
  17.8 0.0 collective-permute-done.2.xa_ref
  17.8 0.0 collective-permute-done.3.xb_ref
  17.8 0.0 copy-start
  17.9 4.4 %rim_steps.1 = (f32[3,384]{1,0:T(4,128)S(1)}, f32[10,12,2,16,128]{4,3,2,1,0:T(8,128)S(1)}, f32[4,8,4,16,128]{4,3,2,1,0:T(8,128)S(1)}, f32[4,8,4,16,128]{4,3,2,1,0:T(8,128)S(1)}) custom-call(f32[8,128]{1,0:T(8,128)S(1)} %get-tuple-element.25.rate_ref, f32[4,8,16,128]{3,2,1,0:T(8,128)S(1)} %collective-permute-done.2.xa_ref, ...), custom_call_target="tpu_custom_call" | custom-call | tf_op jit(solution)/shard_map/rim_steps/pallas_call | solution.py:539
  22.2 2.5 %collective-permute-start.6 = (f32[3,384]{1,0:T(4,128)S(1)}, f32[3,384]{1,0:T(4,128)S(1)}, u32[]{:S(2)}, u32[]{:S(2)}) collective-permute-start(f32[3,384]{1,0:T(4,128)S(1)} %get-tuple-element.40.partial_ref), channel_id=1, source_target_pairs={{0,12},{4,8},{8,4},{12,0},{1,13},{5,9},{9,5},{13,1},{2,14},{6,10},... | collective-permute-start | bytes 13832 | tf_op jit(solution)/shard_map/ppermute | solution.py:678
  24.8 3.4 %collective-permute-start.5 = (f32[3,384]{1,0:T(4,128)S(1)}, f32[3,384]{1,0:T(4,128)S(1)}, u32[]{:S(2)}, u32[]{:S(2)}) collective-permute-start(f32[3,384]{1,0:T(4,128)S(1)} %get-tuple-element.40.partial_ref), channel_id=1, source_target_pairs={{0,8},{4,12},{8,0},{12,4},{1,9},{5,13},{9,1},{13,5},{2,10},{6,14},... | collective-permute-start | bytes 13832 | tf_op jit(solution)/shard_map/ppermute | solution.py:678
  28.1 0.0 collective-permute-start.4
  28.1 0.0 collective-permute-done.6.rest_2_
  28.1 1.7 %collective-permute-done.5.rest_1_ = f32[3,384]{1,0:T(4,128)S(1)} collective-permute-done((f32[3,384]{1,0:T(4,128)S(1)}, f32[3,384]{1,0:T(4,128)S(1)}, u32[]{:S(2)}, u32[]{:S(2)}) %collective-permute-start.5) | collective-permute-done | bytes 4640 | tf_op jit(solution)/shard_map/ppermute | solution.py:678
  29.9 1.9 %collective-permute-done.4.rest_0_ = f32[3,384]{1,0:T(4,128)S(1)} collective-permute-done((f32[3,384]{1,0:T(4,128)S(1)}, f32[3,384]{1,0:T(4,128)S(1)}, u32[]{:S(2)}, u32[]{:S(2)}) %collective-permute-start.4) | collective-permute-done | bytes 4640 | tf_op jit(solution)/shard_map/ppermute | solution.py:678
  31.8 0.0 copy-done
  31.8 4.2 %adjoint_steps.1 = f32[256,128]{1,0:T(8,128)} custom-call(f32[8,128]{1,0:T(8,128)S(1)} %get-tuple-element.25.rate_ref, f32[3,384]{1,0:T(4,128)S(1)} %copy-done, s32[8,384]{1,0:T(8,128)S(1)} %get-tuple-element.26.meta_ref, f32[16,12,2,16,128]{4,3,2,1,0:T(8,128)S(1)} %get-tuple-element.27.coef_in, f32[10,12,2,16,128]{4,3,2,1,0:T(8,128)S(1)} %get-tuple-element.36.coef_out, ...), custom_call_target="tpu_custom_call" | custom-call | tf_op jit(solution)/shard_map/adjoint_steps/pallas_call | solution.py:657
Async XLA Ops:
  1.9 5.0 %collective-permute-start.1 = (f32[16,16,128]{2,1,0:T(8,128)S(1)}, f32[16,16,128]{2,1,0:T(8,128)S(1)}, u32[]{:S(2)}, u32[]{:S(2)}) collective-permute-start(f32[16,16,128]{2,1,0:T(8,128)S(1)} %get-tuple-element.24.e_ref), channel_id=1, source_target_pairs={{1,2},{2,1},{5,6},{6,5},{9,10},{10,9},{13,14},{14,13},{17,18},{18,... | collective-permute-start | bytes 393224 | tf_op jit(solution)/shard_map/ppermute | solution.py:672
  2.6 5.3 %collective-permute-start = (f32[16,16,128]{2,1,0:T(8,128)S(1)}, f32[16,16,128]{2,1,0:T(8,128)S(1)}, u32[]{:S(2)}, u32[]{:S(2)}) collective-permute-start(f32[16,16,128]{2,1,0:T(8,128)S(1)} %get-tuple-element.24.e_ref), channel_id=1, source_target_pairs={{0,1},{1,0},{2,3},{3,2},{4,5},{5,4},{6,7},{7,6},{8,9},{9,8},{10,11... | collective-permute-start | bytes 393224 | tf_op jit(solution)/shard_map/ppermute | solution.py:672
  8.0 9.8 %collective-permute-start.2 = (f32[4,8,16,128]{3,2,1,0:T(8,128)S(1)}, f32[4,8,16,128]{3,2,1,0:T(8,128)S(1)}, u32[]{:S(2)}, u32[]{:S(2)}) collective-permute-start(f32[4,8,16,128]{3,2,1,0:T(8,128)S(1)} %get-tuple-element.30), channel_id=1, source_target_pairs={{0,4},{4,0},{8,12},{12,8},{1,5},{5,1},{9,13},{13,9},{2,6},{6,2},{1... | collective-permute-start | bytes 786440 | tf_op jit(solution)/shard_map/ppermute | solution.py:672
  9.6 8.2 %collective-permute-start.3 = (f32[4,8,16,128]{3,2,1,0:T(8,128)S(1)}, f32[4,8,16,128]{3,2,1,0:T(8,128)S(1)}, u32[]{:S(2)}, u32[]{:S(2)}) collective-permute-start(f32[4,8,16,128]{3,2,1,0:T(8,128)S(1)} %get-tuple-element.31), channel_id=1, source_target_pairs={{4,8},{8,4},{5,9},{9,5},{6,10},{10,6},{7,11},{11,7},{20,24},{24,20... | collective-permute-start | bytes 786440 | tf_op jit(solution)/shard_map/ppermute | solution.py:672
  17.8 13.9 %copy-start = (f32[3,384]{1,0:T(4,128)S(1)}, f32[3,384]{1,0:T(4,128)}, u32[]{:S(2)}) copy-start(f32[3,384]{1,0:T(4,128)} %weight_ref.1) | copy-start | bytes 13828
  22.2 5.9 %collective-permute-start.6 = (f32[3,384]{1,0:T(4,128)S(1)}, f32[3,384]{1,0:T(4,128)S(1)}, u32[]{:S(2)}, u32[]{:S(2)}) collective-permute-start(f32[3,384]{1,0:T(4,128)S(1)} %get-tuple-element.40.partial_ref), channel_id=1, source_target_pairs={{0,12},{4,8},{8,4},{12,0},{1,13},{5,9},{9,5},{13,1},{2,14},{6,10},... | collective-permute-start | bytes 13832 | tf_op jit(solution)/shard_map/ppermute | solution.py:678
  24.8 5.1 %collective-permute-start.5 = (f32[3,384]{1,0:T(4,128)S(1)}, f32[3,384]{1,0:T(4,128)S(1)}, u32[]{:S(2)}, u32[]{:S(2)}) collective-permute-start(f32[3,384]{1,0:T(4,128)S(1)} %get-tuple-element.40.partial_ref), channel_id=1, source_target_pairs={{0,8},{4,12},{8,0},{12,4},{1,9},{5,13},{9,1},{13,5},{2,10},{6,14},... | collective-permute-start | bytes 13832 | tf_op jit(solution)/shard_map/ppermute | solution.py:678
  28.1 3.6 %collective-permute-start.4 = (f32[3,384]{1,0:T(4,128)S(1)}, f32[3,384]{1,0:T(4,128)S(1)}, u32[]{:S(2)}, u32[]{:S(2)}) collective-permute-start(f32[3,384]{1,0:T(4,128)S(1)} %get-tuple-element.40.partial_ref), channel_id=1, source_target_pairs={{0,4},{4,0},{8,12},{12,8},{1,5},{5,1},{9,13},{13,9},{2,6},{6,2},{1... | collective-permute-start | bytes 13832 | tf_op jit(solution)/shard_map/ppermute | solution.py:678

commit v4 on v3

v4 whole, which is shorter than its diff:
```python
import functools

import jax
import jax.numpy as jnp
from jax import lax
from jax.experimental import pallas as pl
from jax.experimental.pallas import tpu as pltpu
from jax.sharding import PartitionSpec as P

STEPS = 4
HALO = STEPS
RATE = 0.02
HALF_DT = 0.025
LANES = 128
TILE = 8
GROUP = 16
RIGHT = 64
Y = ("gy", "sa")
MIB = 1024 * 1024
PX, QX, BX, PY, QYM, QY, PYM, BY, BYM, D, K, KDIR = range(12)
KINDS = 12
VMEM = pl.BlockSpec(memory_space=pltpu.VMEM)
HBM = pl.BlockSpec(memory_space=pltpu.HBM)
F32, BF16, I32 = jnp.float32, jnp.bfloat16, jnp.int32


def in_hbm(*arrays):
    return [pltpu.with_memory_space_constraint(a, pltpu.HBM) for a in arrays]


def lane_of(shape):
    return lax.broadcasted_iota(I32, shape, len(shape) - 1)


def roll(value, shift, axis):
    return pltpu.roll(value, shift % value.shape[axis], axis)


def y_next(value):
    return roll(value, LANES - 1, 1)


def y_previous(value):
    return roll(value, 1, 1)


def pack_edges(fields):
    lane = lane_of(fields[0].shape)
    packed = jnp.zeros_like(fields[0])
    for f, field in enumerate(fields):
        packed = jnp.where(lane // GROUP == f, roll(field, 8 + GROUP * f, 1), packed)
    return packed


def z_pair(value):
    tiles = [value[i : i + TILE] for i in range(0, value.shape[0], TILE)]
    row = lax.broadcasted_iota(I32, tiles[0].shape, 0)
    ups = [roll(t, TILE - 1, 0) for t in tiles]
    downs = [roll(t, 1, 0) for t in tiles]
    pairs = []
    for i, tile in enumerate(tiles):
        above = jnp.where(row == TILE - 1, ups[i + 1] if i + 1 < len(tiles) else tile, ups[i])
        below = jnp.where(row == 0, downs[i - 1] if i else tile, downs[i])
        pairs.append(above + below)
    return jnp.concatenate(pairs, axis=0)


def state_row(m, width):
    low, high = HALO + m, HALO + width - 1 - m

    def find(r):
        if low <= r <= high:
            return 0, r - HALO
        return (1, r - m) if r < low else (1, HALO + r - high - 1)

    return find


def coef_row(kind, width):
    low, high = HALO, HALO + width - 1
    if kind in (PX, QX, BX, D):
        high -= 1
    if kind == D:
        low += 1

    def find(r):
        if low <= r <= high:
            return 0, r - HALO
        return (1, r) if r <= HALO else (1, HALO + 1 + r - (HALO + width - 1))

    return find


def read_state(refs, m, width, r, s):
    which, index = state_row(m, width)(r)
    return refs[which][m, index, s]


def read_coef(refs, kind, width, r):
    which, index = coef_row(kind, width)(r)
    return refs[which][index, kind]


def row_fields(raw, x, layers, width, species):
    initial_ref, logk_ref, direction_ref, speed_ref, flags_ref = raw
    plane = layers * width

    def take(ref, index):
        return ref[pl.ds(index * plane + x, layers, stride=width), :]

    fields = [take(initial_ref, s) for s in range(species)]
    conductance = jnp.exp(take(logk_ref, 0))
    fields += [conductance, conductance * take(direction_ref, 0)]
    for axis in range(2):
        speed = take(speed_ref, axis)
        fields.append(jnp.where(take(flags_ref, axis) == 1, speed, -speed))
    return fields


def y_coefs(k, kd, u, mask=None):
    half = HALF_DT * (k + y_next(k))
    p = half + jnp.maximum(u, 0.0)
    q = half - jnp.minimum(u, 0.0)
    b = HALF_DT * (kd + y_next(kd))
    if mask is not None:
        p, q, b = p * mask, q * mask, b * mask
    return {PY: p, QY: q, BY: b, PYM: y_previous(p), QYM: y_previous(q), BYM: y_previous(b), K: k, KDIR: kd}


def x_coefs(k, k_next, kd, kd_next, u, mask=None):
    half = HALF_DT * (k + k_next)
    p = half + jnp.maximum(u, 0.0)
    q = half - jnp.minimum(u, 0.0)
    b = HALF_DT * (kd + kd_next)
    return (p, q, b) if mask is None else (p * mask, q * mask, b * mask)


def step_cell(r, m, s, rate, coef, state, tangent, put_c, put_t, put_jy):
    kept = rate - coef(D, r)
    upper, lower = coef(QX, r), coef(PX, r - 1)
    after, before = coef(QY, r), coef(PYM, r)

    def moved(value, up, down, yp, ym):
        return kept * value + upper * up + lower * down + after * yp + before * ym + RATE * z_pair(value)

    c, up, down = state(r, s), state(r + 1, s), state(r - 1, s)
    yp, ym = y_next(c), y_previous(c)
    jump = yp - c
    source = (
        coef(BX, r) * (up - c) - coef(BX, r - 1) * (c - down) + coef(BY, r) * jump - coef(BYM, r) * (c - ym)
    )
    put_jy(s, jump)
    if m + 1 < STEPS:
        put_c(s, moved(c, up, down, yp, ym))
    if m > 0:
        t = tangent(r, s)
        source = source + moved(t, tangent(r + 1, s), tangent(r - 1, s), y_next(t), y_previous(t))
    put_t(s, source)


def put_at(ref, m, index):
    def store(s, value):
        ref[m, index, s] = value

    return store


def picked_sums(wide, hot, masks, layers):
    picked = jnp.zeros((wide.shape[0], hot.shape[1]), F32)
    for piece in range(3):
        coarse = wide.astype(BF16)
        picked = picked + jnp.dot(coarse, hot, preferred_element_type=F32)
        wide = wide - coarse.astype(F32)
    wells = masks.shape[1]
    totals = []
    for s in range(hot.shape[1] // wells):
        total = jnp.zeros((layers, wells), F32)
        for i in range(0, wide.shape[0], layers):
            total = total + picked[i : i + layers, s * wells : (s + 1) * wells] * masks[i : i + layers].astype(F32)
        totals.append(jnp.sum(total, axis=0, keepdims=True))
    return totals


def send_kernel(*refs, layers, width, species):
    sources, raw, (xa_ref, xb_ref, sem) = refs[:5], refs[5:10], refs[10:]
    copies = [pltpu.make_async_copy(a, b, sem.at[i]) for i, (a, b) in enumerate(zip(sources, raw))]
    for copy in copies:
        copy.start()
    for copy in copies:
        copy.wait()
    even = lax.rem(lax.axis_index("gx"), 2) == 0
    for r in range(HALO):
        bottom = row_fields(raw, r, layers, width, species)
        top = row_fields(raw, width - HALO + r, layers, width, species)
        for f in range(species + 4):
            xa_ref[r, f] = jnp.where(even, top[f], bottom[f])
            xb_ref[r, f] = jnp.where(even, bottom[f], top[f])


def send_rows(initial, logk, direction, face_speed, face_flags):
    species, layers, width, _ = initial.shape
    sources = [a.reshape(-1, LANES) for a in (initial, logk, direction, face_speed, face_flags)]
    rows = jax.ShapeDtypeStruct((HALO, species + 4, layers, LANES), F32)
    *raw, xa, xb = pl.pallas_call(
        functools.partial(send_kernel, layers=layers, width=width, species=species),
        out_shape=tuple(jax.ShapeDtypeStruct(a.shape, a.dtype) for a in sources) + (rows, rows),
        in_specs=[HBM] * 5,
        out_specs=[VMEM] * 7,
        scratch_shapes=[pltpu.SemaphoreType.DMA((5,))],
        compiler_params=pltpu.CompilerParams(vmem_limit_bytes=3 * MIB),
        name="send_rows",
    )(*in_hbm(*sources))
    return raw, xa, xb


def divide(value, by):
    return lax.shift_right_logical(value, by.bit_length() - 1) if by & (by - 1) == 0 else lax.div(value, by)


def well_table(cells, counts, width):
    total_x, total_y = width * lax.axis_size("gx"), LANES * lax.axis_size(Y)
    start, second = cells[0:1], cells[1:2]
    depth = divide(start, total_x * total_y)
    rest = start - depth * (total_x * total_y)
    x = divide(rest, total_y)
    y = rest - x * total_y
    end = x + jnp.where(second > start, counts - 1, 1 - counts)
    row_start, col_start = lax.axis_index("gx") * width, lax.axis_index(Y) * LANES
    return [depth, jnp.minimum(x, end) - row_start, jnp.maximum(x, end) - row_start, y - col_start, counts]


def strip_columns(wells):
    own = lax.broadcasted_iota(I32, (LANES, wells), 0)
    return own, own % RIGHT // GROUP, own % GROUP + jnp.where(own < RIGHT, -8, 120)


def cone_kernel(
    retard_hbm, decay_hbm, cells_hbm, count_hbm, initial_ref, logk_ref, direction_ref, speed_ref, flags_ref,
    coef_ref, c_ref, t_ref, jy_ref, e_ref, mask_ref, hot_ref, side_hot_ref, rate_ref, meta_ref,
    retard_ref, decay_ref, cells_ref, count_ref, sem, *, layers, width, species,
):
    copies = [
        pltpu.make_async_copy(a, b, sem.at[i])
        for i, (a, b) in enumerate(
            ((retard_hbm, retard_ref), (decay_hbm, decay_ref), (cells_hbm, cells_ref), (count_hbm, count_ref))
        )
    ]
    for copy in copies:
        copy.start()
    raw = initial_ref, logk_ref, direction_ref, speed_ref, flags_ref
    kept = None
    for x in range(width):
        fields = row_fields(raw, x, layers, width, species)
        k, kd, ux, uy = fields[species:]
        e_ref[x] = pack_edges(fields)
        for s in range(species):
            c_ref[0, x, s] = fields[s]
        found = y_coefs(k, kd, uy)
        for kind, value in found.items():
            coef_ref[x, kind] = value
        diagonal = found[PY] + found[QYM] + 2 * RATE
        if x:
            p, q, b = x_coefs(kept[0], k, kept[1], kd, kept[2])
            coef_ref[x - 1, PX], coef_ref[x - 1, QX], coef_ref[x - 1, BX] = p, q, b
            coef_ref[x - 1, D] = kept[3] + p
            diagonal = diagonal + q
        kept = (k, kd, ux, diagonal)
    coef_ref[width - 1, D] = kept[3]
    coef_ref[width - 1, PX] = kept[2]

    for copy in copies:
        copy.wait()
    lane = lane_of((1, LANES))
    strips = jnp.full((1, LANES), retard_ref[species - 1], F32)
    rates = []
    for s in range(species):
        rate = jnp.full((1, LANES), retard_ref[s], F32)
        strips = jnp.where(lane % RIGHT // GROUP == s, rate, strips)
        factor = jnp.exp(jnp.full((1, LANES), -decay_ref[s], F32)) / rate
        rate_ref[s : s + 1, :] = rate
        rate_ref[species + 1 + s : species + 2 + s, :] = factor**STEPS
        rates.append(rate)
    rate_ref[species : species + 1, :] = strips

    for m in range(STEPS):
        for r in range(HALO + 1 + m, HALO + width - 1 - m):
            x = r - HALO
            for s in range(species):
                step_cell(
                    r, m, s, rates[s],
                    lambda kind, r: coef_ref[r - HALO, kind],
                    lambda r, s: c_ref[m, r - HALO, s],
                    lambda r, s: t_ref[m - 1, r - HALO, s],
                    put_at(c_ref, m + 1, x), put_at(t_ref, m, x), put_at(jy_ref, m, x),
                )

    wells = meta_ref.shape[1]
    table = well_table(cells_ref, count_ref[...].reshape(1, wells), width)
    for i, row in enumerate(table):
        meta_ref[i : i + 1, :] = row
    depth, first, last, where_y = table[:4]
    in_layer = lax.broadcasted_iota(I32, (layers, wells), 0) == depth
    for r in range(width + 2 * HALO):
        inside = (first <= r - HALO) & (last >= r - HALO) & in_layer
        mask_ref[r * layers : (r + 1) * layers, :] = jnp.where(inside, 1.0, 0.0).astype(BF16)
    own, strip_species, strip_column = strip_columns(wells)
    hit = (own == where_y) & (own >= STEPS) & (own < LANES - STEPS)
    hot_ref[...] = jnp.where(hit, 1.0, 0.0).astype(BF16)
    reach = (strip_column < STEPS) & (strip_column >= -HALO)
    reach = reach | ((strip_column >= LANES - STEPS) & (strip_column < LANES + HALO))
    hit = reach & (strip_column == where_y)
    for s in range(species):
        side_hot_ref[:, s * wells : (s + 1) * wells] = jnp.where(hit & (strip_species == s), 1.0, 0.0).astype(BF16)


def cone(retard, decay, cells, counts, raw, layers, width, species):
    wells = counts.shape[0]
    state = jax.ShapeDtypeStruct((STEPS, width, species, layers, LANES), F32)
    return pl.pallas_call(
        functools.partial(cone_kernel, layers=layers, width=width, species=species),
        out_shape=(
            jax.ShapeDtypeStruct((width, KINDS, layers, LANES), F32),
            state,
            state,
            state,
            jax.ShapeDtypeStruct((width, layers, LANES), F32),
            jax.ShapeDtypeStruct(((width + 2 * HALO) * layers, wells), BF16),
            jax.ShapeDtypeStruct((LANES, wells), BF16),
            jax.ShapeDtypeStruct((LANES, species * wells), BF16),
            jax.ShapeDtypeStruct((2 * species + 2, LANES), F32),
            jax.ShapeDtypeStruct((TILE, wells), I32),
        ),
        in_specs=[HBM] * 4 + [VMEM] * 5,
        out_specs=[VMEM] * 10,
        scratch_shapes=[
            pltpu.SMEM(retard.shape, F32),
            pltpu.SMEM(decay.shape, F32),
            pltpu.VMEM(cells.shape, I32),
            pltpu.VMEM(counts.shape, I32),
            pltpu.SemaphoreType.DMA((4,)),
        ],
        compiler_params=pltpu.CompilerParams(vmem_limit_bytes=4 * MIB),
        cost_estimate=pl.CostEstimate(flops=10**7, bytes_accessed=10**7, transcendentals=0),
        name="cone_steps",
    )(*in_hbm(retard, decay, cells, counts), *raw)


def neighbour_row(r, a_ref, b_ref, width):
    even = lax.rem(lax.axis_index("gx"), 2) == 0
    from_a = even if r >= HALO else jnp.logical_not(even)
    index = r % (HALO + width)
    return [jnp.where(from_a, a_ref[index, f], b_ref[index, f]) for f in range(a_ref.shape[1])]


def edges_kernel(e_ref, xa_ref, xb_ref, out_ref, *, width):
    out_ref[HALO : HALO + width] = e_ref[...]
    for r in list(range(HALO)) + list(range(HALO + width, 2 * HALO + width)):
        out_ref[r] = pack_edges(neighbour_row(r, xa_ref, xb_ref, width))


def all_edges(e, xa, xb):
    width, layers, _ = e.shape
    return pl.pallas_call(
        functools.partial(edges_kernel, width=width),
        out_shape=jax.ShapeDtypeStruct((width + 2 * HALO, layers, LANES), F32),
        in_specs=[VMEM] * 3,
        out_specs=VMEM,
        compiler_params=pltpu.CompilerParams(vmem_limit_bytes=1 * MIB),
        name="edge_columns",
    )(e, xa, xb)


def rim_kernel(
    rate_ref, xa_ref, xb_ref, coef_in, c_in, t_in, mask_ref, hot_ref,
    partial_ref, coef_out, c_out, jy_out, t_out, *, layers, width, species,
):
    gx = lax.axis_index("gx")
    rows = width + 2 * HALO
    coefs = (coef_in, coef_out)
    last = HALO + width - 1
    get = lambda kind, r: read_coef(coefs, kind, width, r)

    def put_coef(kind, r, value):
        which, index = coef_row(kind, width)(r)
        coefs[which][index, kind] = value

    speeds = {last: coef_in[width - 1, PX]}
    for r in list(range(HALO)) + list(range(HALO + width, rows)):
        fields = neighbour_row(r, xa_ref, xb_ref, width)
        k, kd, speeds[r], uy = fields[species:]
        index = state_row(0, width)(r)[1]
        for s in range(species):
            c_out[0, index, s] = fields[s]
        for kind, value in y_coefs(k, kd, uy).items():
            put_coef(kind, r, value)
    inside_low = jnp.where(gx > 0, 1.0, 0.0).astype(F32)
    inside_high = jnp.where(gx < lax.axis_size("gx") - 1, 1.0, 0.0).astype(F32)
    for r in list(range(HALO)) + list(range(last, rows - 1)):
        mask = inside_low if r < HALO else inside_high
        values = x_coefs(get(K, r), get(K, r + 1), get(KDIR, r), get(KDIR, r + 1), speeds[r], mask)
        for kind, value in zip((PX, QX, BX), values):
            put_coef(kind, r, value)
    for r in list(range(1, HALO + 1)) + list(range(last, rows - 1)):
        if r == HALO:
            value = coef_in[0, D] + get(QX, r - 1)
        elif r == last:
            value = coef_in[width - 1, D] + get(PX, r)
        else:
            value = get(PY, r) + get(QYM, r) + 2 * RATE + get(PX, r) + get(QX, r - 1)
        put_coef(D, r, value)

    for m in range(STEPS):
        for r in list(range(1 + m, HALO + 1 + m)) + list(range(last - m, rows - 1 - m)):
            index = state_row(m + 1, width)(r)[1]
            for s in range(species):
                step_cell(
                    r, m, s, rate_ref[s : s + 1, :], get,
                    lambda r, s: read_state((c_in, c_out), m, width, r, s),
                    lambda r, s: tangent_row(t_in, t_out, m, width, r)[s],
                    put_at(c_out, m + 1, index), put_at(t_out, m, index), put_at(jy_out, m, index),
                )

    masks = mask_ref[HALO * layers : (HALO + width) * layers, :]
    for s in range(species):
        block = [tangent_row(t_in, t_out, STEPS, width, r)[s] for r in range(HALO, HALO + width)]
        partial_ref[s : s + 1, :] = picked_sums(jnp.concatenate(block, axis=0), hot_ref[...], masks, layers)[0]


def tangent_row(t_in, t_out, m, width, r):
    which, index = state_row(m, width)(r)
    return (t_in, t_out)[which].at[m - 1, index]


def rim(rates, xa, xb, coef, c, t, mask, hot):
    _, width, species, layers, _ = c.shape
    wells = mask.shape[1]
    state = (STEPS, 2 * HALO, species, layers, LANES)
    return pl.pallas_call(
        functools.partial(rim_kernel, layers=layers, width=width, species=species),
        out_shape=(
            jax.ShapeDtypeStruct((species, wells), F32),
            jax.ShapeDtypeStruct((2 * HALO + 2, KINDS, layers, LANES), F32),
            jax.ShapeDtypeStruct(state, F32),
            jax.ShapeDtypeStruct(state, F32),
        ),
        in_specs=[VMEM] * 8,
        out_specs=[VMEM] * 4,
        scratch_shapes=[pltpu.VMEM(state, F32)],
        compiler_params=pltpu.CompilerParams(vmem_limit_bytes=6 * MIB),
        cost_estimate=pl.CostEstimate(flops=10**7, bytes_accessed=10**7, transcendentals=0),
        name="rim_steps",
    )(rates, xa, xb, coef, c, t, mask, hot)


def strips_kernel(
    rate_ref, e_ref, ea_ref, eb_ref, partial_in, mask_ref, hot_ref,
    partial_ref, coef_ref, c_ref, jy_ref, t_ref, *, layers, width, species,
):
    shape = (layers, LANES)
    rows = width + 2 * HALO
    lane = lane_of(shape)
    column = lane % GROUP
    near, left = column < 8, lane < RIGHT
    gx, gy = lax.axis_index("gx"), lax.axis_index(Y)
    even_y = lax.rem(gy, 2) == 0
    first_y, last_y = gy == 0, gy == lax.axis_size(Y) - 1
    mask = jnp.where(
        left, jnp.where(first_y & near, 0.0, 1.0), jnp.where(last_y & (column >= 7), 0.0, 1.0)
    ).astype(F32)
    inside_low = jnp.where(gx > 0, 1.0, 0.0).astype(F32)
    inside_high = jnp.where(gx < lax.axis_size("gx") - 1, 1.0, 0.0).astype(F32)
    kept = None
    for r in range(rows):
        own = e_ref[r]
        outer = jnp.where(near == even_y, eb_ref[r], ea_ref[r])
        left_strip = jnp.where(near, outer, own)
        right_strip = jnp.where(near, own, outer)
        c_ref[0, r] = jnp.where(left, left_strip, roll(right_strip, RIGHT, 1))
        k, kd, ux, uy = [
            jnp.where(
                left,
                jnp.take_along_axis(left_strip, GROUP * f + column, 1, mode="promise_in_bounds"),
                jnp.take_along_axis(right_strip, GROUP * f + column, 1, mode="promise_in_bounds"),
            )
            for f in range(species, species + 4)
        ]
        found = y_coefs(k, kd, uy, mask)
        for kind, value in found.items():
            coef_ref[r, kind] = value
        diagonal = found[PY] + found[QYM] + 2 * RATE
        if r:
            inside = inside_low if r <= HALO else inside_high if r >= HALO + width else None
            p, q, b = x_coefs(kept[0], k, kept[1], kd, kept[2], inside)
            coef_ref[r - 1, PX], coef_ref[r - 1, QX], coef_ref[r - 1, BX] = p, q, b
            coef_ref[r - 1, D] = kept[3] + p
            diagonal = diagonal + q
        kept = (k, kd, ux, diagonal)

    rate = rate_ref[species : species + 1, :]
    for m in range(STEPS):
        for r in range(1 + m, rows - 1 - m):

            def put(ref, slot):
                def store(s, value):
                    ref[slot, r] = value

                return store

            step_cell(
                r, m, 0, rate,
                lambda kind, r: coef_ref[r, kind],
                lambda r, s: c_ref[m, r],
                lambda r, s: t_ref[m - 1, r],
                put(c_ref, m + 1), put(t_ref, m), put(jy_ref, m),
            )

    masks = mask_ref[HALO * layers : (HALO + width) * layers, :]
    block = jnp.concatenate([t_ref[STEPS - 1, r] for r in range(HALO, HALO + width)], axis=0)
    for s, total in enumerate(picked_sums(block, hot_ref[...], masks, layers)):
        partial_ref[s : s + 1, :] = partial_in[s : s + 1, :] + total


def side_steps(rates, e, ea, eb, partial, mask, hot):
    rows, layers, _ = e.shape
    species, wells = partial.shape
    state = (STEPS, rows, layers, LANES)
    return pl.pallas_call(
        functools.partial(strips_kernel, layers=layers, width=rows - 2 * HALO, species=species),
        out_shape=(
            jax.ShapeDtypeStruct((species, wells), F32),
            jax.ShapeDtypeStruct((rows, KINDS, layers, LANES), F32),
            jax.ShapeDtypeStruct(state, F32),
            jax.ShapeDtypeStruct(state, F32),
        ),
        in_specs=[VMEM] * 7,
        out_specs=[VMEM] * 4,
        scratch_shapes=[pltpu.VMEM(state, F32)],
        compiler_params=pltpu.CompilerParams(vmem_limit_bytes=6 * MIB),
        name="strip_steps",
    )(rates, e, ea, eb, partial, mask, hot)


def adjoint_kernel(
    rate_ref, weight_ref, meta_ref, mask_ref, coef_in, coef_out, c_in, c_out, jy_in, jy_out,
    coef_side, c_side, jy_side, partial_ref, *rest, layers, width, species, parts,
):
    others, out_ref, lam_ref = rest[:parts], *rest[parts:]
    rows = width + 2 * HALO
    shape = (layers, LANES)
    lane = lane_of(shape)
    gx, gy = lax.axis_index("gx"), lax.axis_index(Y)
    where_y = meta_ref[3:4, :]
    counts = meta_ref[4:5, :].astype(F32)
    wells = meta_ref.shape[1]

    own, strip_species, strip_column = strip_columns(wells)
    strip_hit, own_hit = strip_column == where_y, own == where_y
    residuals = []
    for s in range(species):
        total = partial_ref[s : s + 1, :]
        for other in others:
            total = total + other[s : s + 1, :]
        factor = rate_ref[species + 1 + s, 0:1][:, None]
        residual = weight_ref[s : s + 1, :] * (total * factor) / counts
        residuals.append(residual / counts * factor)
    lam = jnp.zeros((rows * layers, (species + 1) * LANES), F32)
    for piece in range(3):
        coarse = [r.astype(BF16).astype(F32) for r in residuals]
        residuals = [r - q for r, q in zip(residuals, coarse)]
        blocks = [jnp.where(own_hit, q, 0.0).astype(BF16) for q in coarse]
        side = jnp.zeros((LANES, wells), F32)
        for s in range(species):
            side = jnp.where(strip_hit & (strip_species == s), coarse[s], side)
        spread = jnp.concatenate(blocks + [side.astype(BF16)], axis=0)
        lam = lam + lax.dot_general(mask_ref[...], spread, (((1,), (1,)), ((), ())), preferred_element_type=F32)
    for s in range(species + 1):
        lam_ref[0, :, s] = lam[:, s * LANES : (s + 1) * LANES].reshape(rows, layers, LANES)

    def main_coef(kind, r):
        return read_coef((coef_in, coef_out), kind, width, r)

    def side_coef(kind, r):
        return coef_side[r, kind]

    first_row, last_row = HALO - 1, HALO + width - 1
    sums = {}

    def add(key, term):
        sums[key] = sums[key] + term if key in sums else term

    for m in reversed(range(STEPS)):
        now = STEPS - 1 - m
        low, high = STEPS - m, rows - 1 - (STEPS - m)
        for r in range(min(low, first_row), max(high, last_row) + 1):
            sense, retreat = first_row <= r <= last_row, m > 0 and low <= r <= high
            for s in range(species + 1):
                is_side = s == species
                coef = side_coef if is_side else main_coef
                value, up = lam_ref[now, r, s], lam_ref[now, r + 1, s]
                after = y_next(value)
                if sense:
                    if is_side:
                        jump = c_side[m, r + 1] - c_side[m, r]
                    else:
                        states = (c_in, c_out)
                        jump = read_state(states, m, width, r + 1, s) - read_state(states, m, width, r, s)
                    add(("x", is_side, r), jump * (up - value))
                    if r >= HALO:
                        if is_side:
                            jump = jy_side[m, r]
                        else:
                            which, index = state_row(m + 1, width)(r)
                            jump = (jy_in, jy_out)[which][m, index, s]
                        add(("y", is_side, r), jump * (after - value))
                if retreat:
                    lam_ref[now + 1, r, s] = (
                        (rate_ref[s : s + 1, :] - coef(D, r)) * value
                        + coef(PX, r) * up
                        + coef(QX, r - 1) * lam_ref[now, r - 1, s]
                        + coef(PY, r) * after
                        + coef(QYM, r) * y_previous(value)
                        + RATE * z_pair(value)
                    )

    column, left = lane % GROUP, lane < RIGHT
    first_y, last_y = gy == 0, gy == lax.axis_size(Y) - 1
    side_mask = jnp.where(
        left, jnp.where(first_y & (column < 8), 0.0, 1.0), jnp.where(last_y & (column >= 7), 0.0, 1.0)
    ).astype(F32)
    inside_low = jnp.where(gx > 0, 1.0, 0.0).astype(F32)
    inside_high = jnp.where(gx < lax.axis_size("gx") - 1, 1.0, 0.0).astype(F32)
    for x in range(width):
        r = x + HALO
        totals = []
        for is_side in (False, True):
            upper, lower = sums["x", is_side, r], sums["x", is_side, r - 1]
            if x == 0:
                lower = lower * inside_low
            if x == width - 1:
                upper = upper * inside_high
            along_y = sums["y", is_side, r]
            if is_side:
                along_y = along_y * side_mask
            totals.append(upper + lower + along_y + y_previous(along_y))
        total, side = totals
        all_species = side
        for s in range(1, species):
            all_species = all_species + roll(side, -GROUP * s, 1)
        total = jnp.where(lane < STEPS, roll(all_species, -8, 1), total)
        total = jnp.where(lane >= LANES - STEPS, roll(all_species, 120 - RIGHT, 1), total)
        out_ref[pl.ds(x, layers, stride=width), :] = -HALF_DT * main_coef(K, r) * total


def adjoint(rates, weight, meta, mask, inner, outer, side, partials):
    (coef_in, c_in, jy_in), (coef_out, c_out, jy_out) = inner, outer
    _, width, species, layers, _ = c_in.shape
    parts = len(partials) - 1
    operands = (rates, weight, meta, mask, coef_in, coef_out, c_in, c_out, jy_in, jy_out, *side, *partials)
    return pl.pallas_call(
        functools.partial(adjoint_kernel, layers=layers, width=width, species=species, parts=parts),
        out_shape=jax.ShapeDtypeStruct((layers * width, LANES), F32),
        in_specs=[VMEM] * len(operands),
        out_specs=VMEM,
        scratch_shapes=[pltpu.VMEM((STEPS, width + 2 * HALO, species + 1, layers, LANES), F32)],
        compiler_params=pltpu.CompilerParams(vmem_limit_bytes=12 * MIB),
        name="adjoint_steps",
    )(*operands)


def swaps(first, second, axis):
    count = lax.axis_size(axis)
    even = [p for i in range(0, count - 1, 2) for p in ((i, i + 1), (i + 1, i))]
    odd = [p for i in range(1, count - 1, 2) for p in ((i, i + 1), (i + 1, i))]
    return lax.ppermute(first, axis, even), lax.ppermute(second, axis, odd)


def from_others(value, axis, reach):
    count = lax.axis_size(axis)
    if count in (2, 4):
        return [lax.ppermute(value, axis, [(i, i ^ d) for i in range(count)]) for d in range(1, count)]
    return [
        lax.ppermute(value, axis, [(i, i + d) for i in range(count) if 0 <= i + d < count])
        for distance in range(1, min(reach, count - 1) + 1)
        for d in (distance, -distance)
    ]


def shards(
    initial, logk, direction, face_speed, face_flags, retard, decay, screen_cells, screen_count, well_weight
):
    species, layers, width, columns = initial.shape
    raw, xa, xb = send_rows(initial, logk, direction, face_speed, face_flags)
    xa, xb = swaps(xa, xb, "gx")
    coef_in, c_in, t_in, jy_in, e, mask, hot, side_hot, rates, meta = cone(
        retard, decay, screen_cells.T, screen_count, raw, layers, width, species
    )
    e = all_edges(e, xa, xb)
    ea, eb = swaps(e, e, Y)
    partial, coef_out, c_out, jy_out = rim(rates, xa, xb, coef_in, c_in, t_in, mask, hot)
    partial, *side = side_steps(rates, e, ea, eb, partial, mask, side_hot)
    reach = -(-(screen_cells.shape[1] - 1 + HALO) // width)
    partials = [partial] + from_others(partial, "gx", reach)
    inner, outer = (coef_in, c_in, jy_in), (coef_out, c_out, jy_out)
    hessian = adjoint(rates, well_weight, meta, mask, inner, outer, side, partials)
    return hessian.reshape(layers, width, columns)


def solution(mesh):
    in_specs = (
        P("grp", None, "gx", Y),
        P("grp", "gx", Y),
        P("grp", "gx", Y),
        P("grp", None, "gx", Y),
        P("grp", None, "gx", Y),
        P(),
        P(),
        P("grp", None),
        P("grp"),
        P("grp", None),
    )
    return jax.shard_map(shards, mesh=mesh, in_specs=in_specs, out_specs=P("grp", "gx", Y), check_vma=False)
```

time: 36.4 us -> 34.5 us (0.948)
  local copies, waits for them, and re-layouts: 1.62 us -> 0.01 us
  starting transfers between devices: 13.2 us -> 13.9 us
  Pallas kernels: 16.4 us -> 15.7 us
    pallas_call x2 -> x3, Pallas kernels: 1.96 us -> 6.09 us  [the longest x1 4.41 us: side_steps(): pl.pallas_call(functools.partial(strips_kernel, layers=layers, width=rows...]
    pallas_call x1, Pallas kernels: 4.37 us -> 1.85 us  [rim(): pl.pallas_call(functools.partial(rim_kernel, layers=layers, width=width,...]
    pallas_call x1, Pallas kernels: 5.89 us -> 3.65 us  [cone(): pl.pallas_call(functools.partial(cone_kernel, layers=layers, width=width,...]
    unnamed x3 -> x2, local copies, waits for them, and re-layouts: 1.62 us -> 0.01 us
    ppermute x3, starting transfers between devices: 5.91 us -> 6.4 us  [from_others(): lax.ppermute(value, axis, [(i, i ^ d) for i in range(count)])]
  transfers between devices with their start and end apart: 7 -> 7, of which waited for: 3 -> 3; matrix products, arithmetic and copies ran while one was open for 4% -> 0% of each run, Pallas kernels for 16% -> 16%
where the time goes in v4:
time: 34.5 us; the launch traced here: 34.3 us
  Pallas kernels  15.7 us (46%)
  starting transfers between devices  13.9 us (40%)
  waiting for transfers between devices  4.64 us (13%)
    ppermute x4, starting transfers between devices, swaps(): return (lax.ppermute(first, axis, even), lax.ppermute(second, axis, odd))  7.5 us
    ppermute x3, starting transfers between devices, from_others(): lax.ppermute(value, axis, [(i, i ^ d) for i in range(count)])  6.4 us
    pallas_call x1, Pallas kernels, side_steps(): pl.pallas_call(functools.partial(strips_kernel, layers=layers, width=rows...  4.41 us
    pallas_call x1, Pallas kernels, adjoint(): pl.pallas_call(functools.partial(adjoint_kernel, layers=layers, width=wid...  4.08 us
    pallas_call x1, Pallas kernels, cone(): pl.pallas_call(functools.partial(cone_kernel, layers=layers, width=width,...  3.65 us
    ppermute x3, waiting for transfers between devices, from_others(): lax.ppermute(value, axis, [(i, i ^ d) for i in range(count)])  3.36 us
    pallas_call x1, Pallas kernels, rim(): pl.pallas_call(functools.partial(rim_kernel, layers=layers, width=width,...  1.85 us
    pallas_call x1, Pallas kernels, send_rows(): pl.pallas_call(functools.partial(send_kernel, layers=layers, width=width,...  1.48 us
  transfers between devices with their start and end apart: 7, of which 3 were waited for; matrix products, arithmetic and copies ran while one was open for 0% of the time, Pallas kernels for 16%

profile of v4, /device:TPU:0, one launch (start us, length us, event | category | flops | bytes accessed | tf_op | source)
XLA Modules:
  0.0 34.3 jit_solution(18294323253228804914)
XLA Ops:
  0.0 1.5 %send_rows.1 = (f32[768,128]{1,0:T(8,128)S(1)}, f32[256,128]{1,0:T(8,128)S(1)}, f32[256,128]{1,0:T(8,128)S(1)}, f32[512,128]{1,0:T(8,128)S(1)}, s32[512,128]{1,0...) custom-call(f32[768,128]{1,0:T(8,128)} %bitcast.7, f32[256,128]{1,0:T(8,128)} %bitcast.10, ...), custom_call_target="tpu_custom_call" | custom-call | tf_op jit(solution)/shard_map/send_rows/pallas_call | solution.py:204
  1.5 3.1 %collective-permute-start = (f32[4,7,16,128]{3,2,1,0:T(8,128)S(1)}, f32[4,7,16,128]{3,2,1,0:T(8,128)S(1)}, u32[]{:S(2)}, u32[]{:S(2)}) collective-permute-start(f32[4,7,16,128]{3,2,1,0:T(8,128)S(1)} %get-tuple-element.39), channel_id=1, source_target_pairs={{0,4},{4,0},{8,12},{12,8},{1,5},{5,1},{9,13},{13,9},{2,6},{6,2},{1... | collective-permute-start | bytes 688136 | tf_op jit(solution)/shard_map/ppermute | solution.py:674
  4.6 0.7 %collective-permute-start.1 = (f32[4,7,16,128]{3,2,1,0:T(8,128)S(1)}, f32[4,7,16,128]{3,2,1,0:T(8,128)S(1)}, u32[]{:S(2)}, u32[]{:S(2)}) collective-permute-start(f32[4,7,16,128]{3,2,1,0:T(8,128)S(1)} %get-tuple-element.40), channel_id=1, source_target_pairs={{4,8},{8,4},{5,9},{9,5},{6,10},{10,6},{7,11},{11,7},{20,24},{24,20... | collective-permute-start | bytes 688136 | tf_op jit(solution)/shard_map/ppermute | solution.py:674
  5.2 3.7 %cone_steps.1 = (f32[16,12,16,128]{3,2,1,0:T(8,128)S(1)}, f32[4,16,3,16,128]{4,3,2,1,0:T(8,128)S(1)}, f32[4,16,3,16,128]{4,3,2,1,0:T(8,128)S(1)}, f32[4,16,3,16,...) custom-call(f32[3]{0:T(128)} %retard_hbm.1, ...), custom_call_target="tpu_custom_call" | custom-call | flops 10000000 | bytes 10000000 | tf_op jit(solution)/shard_map/cone_steps/pallas_call | solution.py:319
  8.9 1.3 %collective-permute-done.xa_ref = f32[4,7,16,128]{3,2,1,0:T(8,128)S(1)} collective-permute-done((f32[4,7,16,128]{3,2,1,0:T(8,128)S(1)}, f32[4,7,16,128]{3,2,1,0:T(8,128)S(1)}, u32[]{:S(2)}, u32[]{:S(2)}) %collective-permute-start) | collective-permute-done | bytes 229408 | tf_op jit(solution)/shard_map/ppermute | solution.py:674
  10.2 0.0 collective-permute-done.1.xb_ref
  10.2 0.2 edge_columns.1.e_ref
  10.4 0.7 %collective-permute-start.3 = (f32[24,16,128]{2,1,0:T(8,128)S(1)}, f32[24,16,128]{2,1,0:T(8,128)S(1)}, u32[]{:S(2)}, u32[]{:S(2)}) collective-permute-start(f32[24,16,128]{2,1,0:T(8,128)S(1)} %edge_columns.1.e_ref), channel_id=1, source_target_pairs={{1,2},{2,1},{5,6},{6,5},{9,10},{10,9},{13,14},{14,13},{17,18},{18,... | collective-permute-start | bytes 589832 | tf_op jit(solution)/shard_map/ppermute | solution.py:674
  11.1 3.1 %collective-permute-start.2 = (f32[24,16,128]{2,1,0:T(8,128)S(1)}, f32[24,16,128]{2,1,0:T(8,128)S(1)}, u32[]{:S(2)}, u32[]{:S(2)}) collective-permute-start(f32[24,16,128]{2,1,0:T(8,128)S(1)} %edge_columns.1.e_ref), channel_id=1, source_target_pairs={{0,1},{1,0},{2,3},{3,2},{4,5},{5,4},{6,7},{7,6},{8,9},{9,8},{10,11... | collective-permute-start | bytes 589832 | tf_op jit(solution)/shard_map/ppermute | solution.py:674
  14.1 0.0 copy-start
  14.1 1.8 %rim_steps.1 = (f32[3,384]{1,0:T(4,128)S(1)}, f32[10,12,16,128]{3,2,1,0:T(8,128)S(1)}, f32[4,8,3,16,128]{4,3,2,1,0:T(8,128)S(1)}, f32[4,8,3,16,128]{4,3,2,1,0:T(8,128)S(1)}) custom-call(f32[8,128]{1,0:T(8,128)S(1)} %get-tuple-element.35.rate_ref, f32[4,7,16,128]{3,2,1,0:T(8,128)S(1)} %collective-permute-done.xa_ref, ...), custom_call_target="tpu_custom_call" | custom-call | flops 10000000 | bytes 10000000 | tf_op jit(solution)/shard_map/rim_steps/pallas_call | solution.py:438
  16.0 0.0 collective-permute-done.3.eb_ref
  16.0 0.0 collective-permute-done.2.ea_ref
  16.0 4.4 %strip_steps.1 = (f32[3,384]{1,0:T(4,128)S(1)}, f32[24,12,16,128]{3,2,1,0:T(8,128)S(1)}, f32[4,24,16,128]{3,2,1,0:T(8,128)S(1)}, f32[4,24,16,128]{3,2,1,0:T(8,128)S(1)}) custom-call(f32[8,128]{1,0:T(8,128)S(1)} %get-tuple-element.35.rate_ref, f32[24,16,128]{2,1,0:T(8,128)S(1)} %edge_columns.1.e_ref, f32[24,16,128]{2,1,0:T(8,128)S(1)} %collective-permute-done.2.ea_ref, ...), custom_call_target="tpu_custom_call" | custom-call | tf_op jit(solution)/shard_map/strip_steps/pallas_call | solution.py:527
  20.4 3.7 %collective-permute-start.6 = (f32[3,384]{1,0:T(4,128)S(1)}, f32[3,384]{1,0:T(4,128)S(1)}, u32[]{:S(2)}, u32[]{:S(2)}) collective-permute-start(f32[3,384]{1,0:T(4,128)S(1)} %get-tuple-element.54.partial_ref), channel_id=1, source_target_pairs={{0,12},{4,8},{8,4},{12,0},{1,13},{5,9},{9,5},{13,1},{2,14},{6,10},... | collective-permute-start | bytes 13832 | tf_op jit(solution)/shard_map/ppermute | solution.py:680
  24.1 2.5 %collective-permute-start.5 = (f32[3,384]{1,0:T(4,128)S(1)}, f32[3,384]{1,0:T(4,128)S(1)}, u32[]{:S(2)}, u32[]{:S(2)}) collective-permute-start(f32[3,384]{1,0:T(4,128)S(1)} %get-tuple-element.54.partial_ref), channel_id=1, source_target_pairs={{0,8},{4,12},{8,0},{12,4},{1,9},{5,13},{9,1},{13,5},{2,10},{6,14},... | collective-permute-start | bytes 13832 | tf_op jit(solution)/shard_map/ppermute | solution.py:680
  26.6 0.3 collective-permute-start.4
  26.8 0.0 collective-permute-done.6.rest_2_
  26.8 1.8 %collective-permute-done.5.rest_1_ = f32[3,384]{1,0:T(4,128)S(1)} collective-permute-done((f32[3,384]{1,0:T(4,128)S(1)}, f32[3,384]{1,0:T(4,128)S(1)}, u32[]{:S(2)}, u32[]{:S(2)}) %collective-permute-start.5) | collective-permute-done | bytes 4640 | tf_op jit(solution)/shard_map/ppermute | solution.py:680
  28.6 1.5 %collective-permute-done.4.rest_0_ = f32[3,384]{1,0:T(4,128)S(1)} collective-permute-done((f32[3,384]{1,0:T(4,128)S(1)}, f32[3,384]{1,0:T(4,128)S(1)}, u32[]{:S(2)}, u32[]{:S(2)}) %collective-permute-start.4) | collective-permute-done | bytes 4640 | tf_op jit(solution)/shard_map/ppermute | solution.py:680
  30.2 0.0 copy-done
  30.2 4.1 %adjoint_steps.1 = f32[256,128]{1,0:T(8,128)} custom-call(f32[8,128]{1,0:T(8,128)S(1)} %get-tuple-element.35.rate_ref, f32[3,384]{1,0:T(4,128)S(1)} %copy-done, s32[8,384]{1,0:T(8,128)S(1)} %get-tuple-element.36.meta_ref, bf16[384,384]{1,0:T(8,128)(2,1)S(1)} %get-tuple-element.37.mask_ref, f32[16,12,16,128]{3,2,1,0:T(8,128)S(1)} %get-tuple-element.38.coef_in, ...), custom_call_target="tpu_custom_call" | custom-call | tf_op jit(solution)/shard_map/adjoint_steps/pallas_call | solution.py:659
Async XLA Ops:
  1.5 8.7 %collective-permute-start = (f32[4,7,16,128]{3,2,1,0:T(8,128)S(1)}, f32[4,7,16,128]{3,2,1,0:T(8,128)S(1)}, u32[]{:S(2)}, u32[]{:S(2)}) collective-permute-start(f32[4,7,16,128]{3,2,1,0:T(8,128)S(1)} %get-tuple-element.39), channel_id=1, source_target_pairs={{0,4},{4,0},{8,12},{12,8},{1,5},{5,1},{9,13},{13,9},{2,6},{6,2},{1... | collective-permute-start | bytes 688136 | tf_op jit(solution)/shard_map/ppermute | solution.py:674
  4.6 5.6 %collective-permute-start.1 = (f32[4,7,16,128]{3,2,1,0:T(8,128)S(1)}, f32[4,7,16,128]{3,2,1,0:T(8,128)S(1)}, u32[]{:S(2)}, u32[]{:S(2)}) collective-permute-start(f32[4,7,16,128]{3,2,1,0:T(8,128)S(1)} %get-tuple-element.40), channel_id=1, source_target_pairs={{4,8},{8,4},{5,9},{9,5},{6,10},{10,6},{7,11},{11,7},{20,24},{24,20... | collective-permute-start | bytes 688136 | tf_op jit(solution)/shard_map/ppermute | solution.py:674
  10.4 5.6 %collective-permute-start.3 = (f32[24,16,128]{2,1,0:T(8,128)S(1)}, f32[24,16,128]{2,1,0:T(8,128)S(1)}, u32[]{:S(2)}, u32[]{:S(2)}) collective-permute-start(f32[24,16,128]{2,1,0:T(8,128)S(1)} %edge_columns.1.e_ref), channel_id=1, source_target_pairs={{1,2},{2,1},{5,6},{6,5},{9,10},{10,9},{13,14},{14,13},{17,18},{18,... | collective-permute-start | bytes 589832 | tf_op jit(solution)/shard_map/ppermute | solution.py:674
  11.1 4.9 %collective-permute-start.2 = (f32[24,16,128]{2,1,0:T(8,128)S(1)}, f32[24,16,128]{2,1,0:T(8,128)S(1)}, u32[]{:S(2)}, u32[]{:S(2)}) collective-permute-start(f32[24,16,128]{2,1,0:T(8,128)S(1)} %edge_columns.1.e_ref), channel_id=1, source_target_pairs={{0,1},{1,0},{2,3},{3,2},{4,5},{5,4},{6,7},{7,6},{8,9},{9,8},{10,11... | collective-permute-start | bytes 589832 | tf_op jit(solution)/shard_map/ppermute | solution.py:674
  14.1 16.1 %copy-start = (f32[3,384]{1,0:T(4,128)S(1)}, f32[3,384]{1,0:T(4,128)}, u32[]{:S(2)}) copy-start(f32[3,384]{1,0:T(4,128)} %weight_ref.1) | copy-start | bytes 13828
  20.4 6.4 %collective-permute-start.6 = (f32[3,384]{1,0:T(4,128)S(1)}, f32[3,384]{1,0:T(4,128)S(1)}, u32[]{:S(2)}, u32[]{:S(2)}) collective-permute-start(f32[3,384]{1,0:T(4,128)S(1)} %get-tuple-element.54.partial_ref), channel_id=1, source_target_pairs={{0,12},{4,8},{8,4},{12,0},{1,13},{5,9},{9,5},{13,1},{2,14},{6,10},... | collective-permute-start | bytes 13832 | tf_op jit(solution)/shard_map/ppermute | solution.py:680
  24.1 4.5 %collective-permute-start.5 = (f32[3,384]{1,0:T(4,128)S(1)}, f32[3,384]{1,0:T(4,128)S(1)}, u32[]{:S(2)}, u32[]{:S(2)}) collective-permute-start(f32[3,384]{1,0:T(4,128)S(1)} %get-tuple-element.54.partial_ref), channel_id=1, source_target_pairs={{0,8},{4,12},{8,0},{12,4},{1,9},{5,13},{9,1},{13,5},{2,10},{6,14},... | collective-permute-start | bytes 13832 | tf_op jit(solution)/shard_map/ppermute | solution.py:680
  26.6 3.6 %collective-permute-start.4 = (f32[3,384]{1,0:T(4,128)S(1)}, f32[3,384]{1,0:T(4,128)S(1)}, u32[]{:S(2)}, u32[]{:S(2)}) collective-permute-start(f32[3,384]{1,0:T(4,128)S(1)} %get-tuple-element.54.partial_ref), channel_id=1, source_target_pairs={{0,4},{4,0},{8,12},{12,8},{1,5},{5,1},{9,13},{13,9},{2,6},{6,2},{1... | collective-permute-start | bytes 13832 | tf_op jit(solution)/shard_map/ppermute | solution.py:680

commit v5 on v4

--- a/solution.py
+++ b/solution.py
@@ -352,19 +352,44 @@
     return [jnp.where(from_a, a_ref[index, f], b_ref[index, f]) for f in range(a_ref.shape[1])]
 
 
-def edges_kernel(e_ref, xa_ref, xb_ref, out_ref, *, width):
-    out_ref[HALO : HALO + width] = e_ref[...]
-    for r in list(range(HALO)) + list(range(HALO + width, 2 * HALO + width)):
-        out_ref[r] = pack_edges(neighbour_row(r, xa_ref, xb_ref, width))
+def edges_kernel(e_ref, xa_ref, xb_ref, all_ref, a_ref, b_ref, *, width):
+    rows = width + 2 * HALO
+    half = rows // 2
+    even = lax.rem(lax.axis_index(Y), 2) == 0
+    edges = {}
+    for r in range(rows):
+        inner = HALO <= r < HALO + width
+        edges[r] = e_ref[r - HALO] if inner else pack_edges(neighbour_row(r, xa_ref, xb_ref, width))
+        all_ref[r] = edges[r]
+    near = lane_of(edges[0].shape) % GROUP < 8
+    for r in range(half):
+        one, two = edges[r], edges[r + half]
+        to_right = jnp.where(near, one, roll(two, 8, 1))
+        to_left = jnp.where(near, roll(two, -8, 1), one)
+        a_ref[r] = jnp.where(even, to_right, to_left)
+        b_ref[r] = jnp.where(even, to_left, to_right)
+
+
+def outer_edges(r, a_ref, b_ref, near):
+    half = a_ref.shape[0]
+    even = lax.rem(lax.axis_index(Y), 2) == 0
+    if r < half:
+        return jnp.where(near == even, b_ref[r], a_ref[r])
+    both = jnp.where(near == even, a_ref[r - half], b_ref[r - half])
+    return jnp.where(near, roll(both, -8, 1), roll(both, 8, 1))
 
 
 def all_edges(e, xa, xb):
     width, layers, _ = e.shape
     return pl.pallas_call(
         functools.partial(edges_kernel, width=width),
-        out_shape=jax.ShapeDtypeStruct((width + 2 * HALO, layers, LANES), F32),
+        out_shape=(
+            jax.ShapeDtypeStruct((width + 2 * HALO, layers, LANES), F32),
+            jax.ShapeDtypeStruct((width // 2 + HALO, layers, LANES), F32),
+            jax.ShapeDtypeStruct((width // 2 + HALO, layers, LANES), F32),
+        ),
         in_specs=[VMEM] * 3,
-        out_specs=VMEM,
+        out_specs=[VMEM] * 3,
         compiler_params=pltpu.CompilerParams(vmem_limit_bytes=1 * MIB),
         name="edge_columns",
     )(e, xa, xb)
@@ -462,28 +487,30 @@
     column = lane % GROUP
     near, left = column < 8, lane < RIGHT
     gx, gy = lax.axis_index("gx"), lax.axis_index(Y)
-    even_y = lax.rem(gy, 2) == 0
     first_y, last_y = gy == 0, gy == lax.axis_size(Y) - 1
     mask = jnp.where(
         left, jnp.where(first_y & near, 0.0, 1.0), jnp.where(last_y & (column >= 7), 0.0, 1.0)
     ).astype(F32)
     inside_low = jnp.where(gx > 0, 1.0, 0.0).astype(F32)
     inside_high = jnp.where(gx < lax.axis_size("gx") - 1, 1.0, 0.0).astype(F32)
+    group = lane % RIGHT // GROUP
+
+    def spread(first, second, third):
+        return jnp.where(group == 0, first, jnp.where(group == 1, second, third))
+
     kept = None
     for r in range(rows):
         own = e_ref[r]
-        outer = jnp.where(near == even_y, eb_ref[r], ea_ref[r])
+        outer = outer_edges(r, ea_ref, eb_ref, near)
         left_strip = jnp.where(near, outer, own)
         right_strip = jnp.where(near, own, outer)
-        c_ref[0, r] = jnp.where(left, left_strip, roll(right_strip, RIGHT, 1))
-        k, kd, ux, uy = [
-            jnp.where(
-                left,
-                jnp.take_along_axis(left_strip, GROUP * f + column, 1, mode="promise_in_bounds"),
-                jnp.take_along_axis(right_strip, GROUP * f + column, 1, mode="promise_in_bounds"),
-            )
-            for f in range(species, species + 4)
-        ]
+        low = jnp.where(left, left_strip, roll(right_strip, RIGHT, 1))
+        high = jnp.where(left, roll(left_strip, RIGHT, 1), right_strip)
+        c_ref[0, r] = low
+        by_one, by_two = roll(high, GROUP, 1), roll(high, 2 * GROUP, 1)
+        back_one, back_two = roll(high, -GROUP, 1), roll(high, -2 * GROUP, 1)
+        k = spread(roll(low, -3 * GROUP, 1), roll(low, -2 * GROUP, 1), roll(low, -GROUP, 1))
+        kd, ux, uy = spread(high, by_one, by_two), spread(back_one, high, by_one), spread(back_two, back_one, high)
         found = y_coefs(k, kd, uy, mask)
         for kind, value in found.items():
             coef_ref[r, kind] = value
@@ -667,11 +694,25 @@
     )(*operands)
 
 
-def swaps(first, second, axis):
-    count = lax.axis_size(axis)
-    even = [p for i in range(0, count - 1, 2) for p in ((i, i + 1), (i + 1, i))]
-    odd = [p for i in range(1, count - 1, 2) for p in ((i, i + 1), (i + 1, i))]
-    return lax.ppermute(first, axis, even), lax.ppermute(second, axis, odd)
+def pairs(count, start):
+    return [p for i in range(start, count - 1, 2) for p in ((i, i + 1), (i + 1, i))]
+
+
+def swap_x(first, second):
+    count, side = lax.axis_size("gx"), lax.axis_size(Y)
+    partner = dict(pairs(count, 1))
+    odd = [
+        (i * side + j, partner[i] * side + j if i in partner else i * side + (j ^ 1))
+        for i in range(count)
+        for j in range(side)
+    ]
+    return lax.ppermute(first, "gx", pairs(count, 0)), lax.ppermute(second, ("gx",) + Y, odd)
+
+
+def swap_y(first, second):
+    count = lax.axis_size(Y)
+    odd = pairs(count, 1) + [(0, count - 1), (count - 1, 0)]
+    return lax.ppermute(first, Y, pairs(count, 0)), lax.ppermute(second, Y, odd)
 
 
 def from_others(value, axis, reach):
@@ -690,12 +731,12 @@
 ):
     species, layers, width, columns = initial.shape
     raw, xa, xb = send_rows(initial, logk, direction, face_speed, face_flags)
-    xa, xb = swaps(xa, xb, "gx")
+    xa, xb = swap_x(xa, xb)
     coef_in, c_in, t_in, jy_in, e, mask, hot, side_hot, rates, meta = cone(
         retard, decay, screen_cells.T, screen_count, raw, layers, width, species
     )
-    e = all_edges(e, xa, xb)
-    ea, eb = swaps(e, e, Y)
+    e, ea, eb = all_edges(e, xa, xb)
+    ea, eb = swap_y(ea, eb)
     partial, coef_out, c_out, jy_out = rim(rates, xa, xb, coef_in, c_in, t_in, mask, hot)
     partial, *side = side_steps(rates, e, ea, eb, partial, mask, side_hot)
     reach = -(-(screen_cells.shape[1] - 1 + HALO) // width)

time: 34.5 us -> 32.1 us (0.930)
  starting transfers between devices: 13.9 us -> 9.62 us
  waiting for transfers between devices: 4.64 us -> 6.58 us
    ppermute x4, starting transfers between devices: 7.5 us -> 4.92 us  [the longest x1 3.09 us: swap_x(): lax.ppermute(first, 'gx', pairs(count, 0))]
    ppermute x3, starting transfers between devices: 6.4 us -> 4.71 us  [from_others(): lax.ppermute(value, axis, [(i, i ^ d) for i in range(count)])]
    ppermute x4, waiting for transfers between devices: 1.28 us -> 2.9 us  [the longest x1 1.95 us: swap_x(): lax.ppermute(first, 'gx', pairs(count, 0))]
  transfers between devices with their start and end apart: 7 -> 7, of which waited for: 3 -> 4; matrix products, arithmetic and copies ran while one was open for 0% -> 0% of each run, Pallas kernels for 16% -> 17%
where the time goes in v5:
time: 32.1 us; the launch traced here: 31.9 us
  Pallas kernels  15.6 us (49%)
  starting transfers between devices  9.62 us (30%)
  waiting for transfers between devices  6.58 us (20%)
    ppermute x3, starting transfers between devices, from_others(): lax.ppermute(value, axis, [(i, i ^ d) for i in range(count)])  4.71 us
    pallas_call x1, Pallas kernels, side_steps(): pl.pallas_call(functools.partial(strips_kernel, layers=layers, width=rows...  4.3 us
    pallas_call x1, Pallas kernels, adjoint(): pl.pallas_call(functools.partial(adjoint_kernel, layers=layers, width=wid...  4.08 us
    ppermute x3, waiting for transfers between devices, from_others(): lax.ppermute(value, axis, [(i, i ^ d) for i in range(count)])  3.68 us
    pallas_call x1, Pallas kernels, cone(): pl.pallas_call(functools.partial(cone_kernel, layers=layers, width=width,...  3.64 us
    ppermute x1, starting transfers between devices, swap_x(): lax.ppermute(first, 'gx', pairs(count, 0))  3.09 us
    ppermute x1, waiting for transfers between devices, swap_x(): lax.ppermute(first, 'gx', pairs(count, 0))  1.95 us
    pallas_call x1, Pallas kernels, rim(): pl.pallas_call(functools.partial(rim_kernel, layers=layers, width=width,...  1.85 us
  transfers between devices with their start and end apart: 7, of which 4 were waited for; matrix products, arithmetic and copies ran while one was open for 0% of the time, Pallas kernels for 17%

profile of v5, /device:TPU:0, one launch (start us, length us, event | category | flops | bytes accessed | tf_op | source)
XLA Modules:
  0.0 31.9 jit_solution(15821409381328206535)
XLA Ops:
  0.0 1.5 %send_rows.1 = (f32[768,128]{1,0:T(8,128)S(1)}, f32[256,128]{1,0:T(8,128)S(1)}, f32[256,128]{1,0:T(8,128)S(1)}, f32[512,128]{1,0:T(8,128)S(1)}, s32[512,128]{1,0...) custom-call(f32[768,128]{1,0:T(8,128)} %bitcast.7, f32[256,128]{1,0:T(8,128)} %bitcast.10, ...), custom_call_target="tpu_custom_call" | custom-call | tf_op jit(solution)/shard_map/send_rows/pallas_call | solution.py:204
  1.5 3.1 %collective-permute-start = (f32[4,7,16,128]{3,2,1,0:T(8,128)S(1)}, f32[4,7,16,128]{3,2,1,0:T(8,128)S(1)}, u32[]{:S(2)}, u32[]{:S(2)}) collective-permute-start(f32[4,7,16,128]{3,2,1,0:T(8,128)S(1)} %get-tuple-element.42), channel_id=1, source_target_pairs={{0,4},{4,0},{8,12},{12,8},{1,5},{5,1},{9,13},{13,9},{2,6},{6,2},{1... | collective-permute-start | bytes 688136 | tf_op jit(solution)/shard_map/ppermute | solution.py:709
  4.6 0.0 collective-permute-start.1
  4.6 3.6 %cone_steps.1 = (f32[16,12,16,128]{3,2,1,0:T(8,128)S(1)}, f32[4,16,3,16,128]{4,3,2,1,0:T(8,128)S(1)}, f32[4,16,3,16,128]{4,3,2,1,0:T(8,128)S(1)}, f32[4,16,3,16,...) custom-call(f32[3]{0:T(128)} %retard_hbm.1, ...), custom_call_target="tpu_custom_call" | custom-call | flops 10000000 | bytes 10000000 | tf_op jit(solution)/shard_map/cone_steps/pallas_call | solution.py:319
  8.2 1.9 %collective-permute-done.xa_ref = f32[4,7,16,128]{3,2,1,0:T(8,128)S(1)} collective-permute-done((f32[4,7,16,128]{3,2,1,0:T(8,128)S(1)}, f32[4,7,16,128]{3,2,1,0:T(8,128)S(1)}, u32[]{:S(2)}, u32[]{:S(2)}) %collective-permute-start) | collective-permute-done | bytes 229408 | tf_op jit(solution)/shard_map/ppermute | solution.py:709
  10.2 0.0 collective-permute-done.1.xb_ref
  10.2 0.3 edge_columns.1
  10.5 0.1 collective-permute-start.2
  10.5 1.8 %collective-permute-start.3 = (f32[12,16,128]{2,1,0:T(8,128)S(1)}, f32[12,16,128]{2,1,0:T(8,128)S(1)}, u32[]{:S(2)}, u32[]{:S(2)}) collective-permute-start(f32[12,16,128]{2,1,0:T(8,128)S(1)} %get-tuple-element.54), channel_id=1, source_target_pairs={{1,2},{2,1},{0,3},{3,0},{5,6},{6,5},{4,7},{7,4},{9,10},{10,9},{8,1... | collective-permute-start | bytes 294920 | tf_op jit(solution)/shard_map/ppermute | solution.py:715
  12.3 0.0 copy-start
  12.3 1.9 %rim_steps.1 = (f32[3,384]{1,0:T(4,128)S(1)}, f32[10,12,16,128]{3,2,1,0:T(8,128)S(1)}, f32[4,8,3,16,128]{4,3,2,1,0:T(8,128)S(1)}, f32[4,8,3,16,128]{4,3,2,1,0:T(8,128)S(1)}) custom-call(f32[8,128]{1,0:T(8,128)S(1)} %get-tuple-element.38.rate_ref, f32[4,7,16,128]{3,2,1,0:T(8,128)S(1)} %collective-permute-done.xa_ref, ...), custom_call_target="tpu_custom_call" | custom-call | flops 10000000 | bytes 10000000 | tf_op jit(solution)/shard_map/rim_steps/pallas_call | solution.py:463
  14.2 0.0 collective-permute-done.2.ea_ref
  14.2 0.9 %collective-permute-done.3.eb_ref = f32[12,16,128]{2,1,0:T(8,128)S(1)} collective-permute-done((f32[12,16,128]{2,1,0:T(8,128)S(1)}, f32[12,16,128]{2,1,0:T(8,128)S(1)}, u32[]{:S(2)}, u32[]{:S(2)}) %collective-permute-start.3) | collective-permute-done | bytes 98336 | tf_op jit(solution)/shard_map/ppermute | solution.py:715
  15.1 4.3 %strip_steps.1 = (f32[3,384]{1,0:T(4,128)S(1)}, f32[24,12,16,128]{3,2,1,0:T(8,128)S(1)}, f32[4,24,16,128]{3,2,1,0:T(8,128)S(1)}, f32[4,24,16,128]{3,2,1,0:T(8,128)S(1)}) custom-call(f32[8,128]{1,0:T(8,128)S(1)} %get-tuple-element.38.rate_ref, f32[24,16,128]{2,1,0:T(8,128)S(1)} %get-tuple-element.52.e_ref, f32[12,16,128]{2,1,0:T(8,128)S(1)} %collective-permute-done.2.ea_ref, ...), custom_call_target="tpu_custom_call" | custom-call | tf_op jit(solution)/shard_map/strip_steps/pallas_call | solution.py:554
  19.4 3.9 %collective-permute-start.6 = (f32[3,384]{1,0:T(4,128)S(1)}, f32[3,384]{1,0:T(4,128)S(1)}, u32[]{:S(2)}, u32[]{:S(2)}) collective-permute-start(f32[3,384]{1,0:T(4,128)S(1)} %get-tuple-element.60.partial_ref), channel_id=1, source_target_pairs={{0,12},{4,8},{8,4},{12,0},{1,13},{5,9},{9,5},{13,1},{2,14},{6,10},... | collective-permute-start | bytes 13832 | tf_op jit(solution)/shard_map/ppermute | solution.py:721
  23.3 0.6 %collective-permute-start.5 = (f32[3,384]{1,0:T(4,128)S(1)}, f32[3,384]{1,0:T(4,128)S(1)}, u32[]{:S(2)}, u32[]{:S(2)}) collective-permute-start(f32[3,384]{1,0:T(4,128)S(1)} %get-tuple-element.60.partial_ref), channel_id=1, source_target_pairs={{0,8},{4,12},{8,0},{12,4},{1,9},{5,13},{9,1},{13,5},{2,10},{6,14},... | collective-permute-start | bytes 13832 | tf_op jit(solution)/shard_map/ppermute | solution.py:721
  23.8 0.3 collective-permute-start.4
  24.1 0.8 %collective-permute-done.6.rest_2_ = f32[3,384]{1,0:T(4,128)S(1)} collective-permute-done((f32[3,384]{1,0:T(4,128)S(1)}, f32[3,384]{1,0:T(4,128)S(1)}, u32[]{:S(2)}, u32[]{:S(2)}) %collective-permute-start.6) | collective-permute-done | bytes 4640 | tf_op jit(solution)/shard_map/ppermute | solution.py:721
  24.9 2.9 %collective-permute-done.5.rest_1_ = f32[3,384]{1,0:T(4,128)S(1)} collective-permute-done((f32[3,384]{1,0:T(4,128)S(1)}, f32[3,384]{1,0:T(4,128)S(1)}, u32[]{:S(2)}, u32[]{:S(2)}) %collective-permute-start.5) | collective-permute-done | bytes 4640 | tf_op jit(solution)/shard_map/ppermute | solution.py:721
  27.8 0.0 collective-permute-done.4.rest_0_
  27.8 0.0 copy-done
  27.8 4.1 %adjoint_steps.1 = f32[256,128]{1,0:T(8,128)} custom-call(f32[8,128]{1,0:T(8,128)S(1)} %get-tuple-element.38.rate_ref, f32[3,384]{1,0:T(4,128)S(1)} %copy-done, s32[8,384]{1,0:T(8,128)S(1)} %get-tuple-element.39.meta_ref, bf16[384,384]{1,0:T(8,128)(2,1)S(1)} %get-tuple-element.40.mask_ref, f32[16,12,16,128]{3,2,1,0:T(8,128)S(1)} %get-tuple-element.41.coef_in, ...), custom_call_target="tpu_custom_call" | custom-call | tf_op jit(solution)/shard_map/adjoint_steps/pallas_call | solution.py:686
Async XLA Ops:
  1.5 8.7 %collective-permute-start = (f32[4,7,16,128]{3,2,1,0:T(8,128)S(1)}, f32[4,7,16,128]{3,2,1,0:T(8,128)S(1)}, u32[]{:S(2)}, u32[]{:S(2)}) collective-permute-start(f32[4,7,16,128]{3,2,1,0:T(8,128)S(1)} %get-tuple-element.42), channel_id=1, source_target_pairs={{0,4},{4,0},{8,12},{12,8},{1,5},{5,1},{9,13},{13,9},{2,6},{6,2},{1... | collective-permute-start | bytes 688136 | tf_op jit(solution)/shard_map/ppermute | solution.py:709
  4.6 5.6 %collective-permute-start.1 = (f32[4,7,16,128]{3,2,1,0:T(8,128)S(1)}, f32[4,7,16,128]{3,2,1,0:T(8,128)S(1)}, u32[]{:S(2)}, u32[]{:S(2)}) collective-permute-start(f32[4,7,16,128]{3,2,1,0:T(8,128)S(1)} %get-tuple-element.43), channel_id=1, source_target_pairs={{0,1},{1,0},{2,3},{3,2},{4,8},{5,9},{6,10},{7,11},{8,4},{9,5},{10,... | collective-permute-start | bytes 688136 | tf_op jit(solution)/shard_map/ppermute | solution.py:709
  10.5 3.7 %collective-permute-start.2 = (f32[12,16,128]{2,1,0:T(8,128)S(1)}, f32[12,16,128]{2,1,0:T(8,128)S(1)}, u32[]{:S(2)}, u32[]{:S(2)}) collective-permute-start(f32[12,16,128]{2,1,0:T(8,128)S(1)} %get-tuple-element.53), channel_id=1, source_target_pairs={{0,1},{1,0},{2,3},{3,2},{4,5},{5,4},{6,7},{7,6},{8,9},{9,8},{10,11... | collective-permute-start | bytes 294920 | tf_op jit(solution)/shard_map/ppermute | solution.py:715
  10.5 4.6 %collective-permute-start.3 = (f32[12,16,128]{2,1,0:T(8,128)S(1)}, f32[12,16,128]{2,1,0:T(8,128)S(1)}, u32[]{:S(2)}, u32[]{:S(2)}) collective-permute-start(f32[12,16,128]{2,1,0:T(8,128)S(1)} %get-tuple-element.54), channel_id=1, source_target_pairs={{1,2},{2,1},{0,3},{3,0},{5,6},{6,5},{4,7},{7,4},{9,10},{10,9},{8,1... | collective-permute-start | bytes 294920 | tf_op jit(solution)/shard_map/ppermute | solution.py:715
  12.3 15.5 %copy-start = (f32[3,384]{1,0:T(4,128)S(1)}, f32[3,384]{1,0:T(4,128)}, u32[]{:S(2)}) copy-start(f32[3,384]{1,0:T(4,128)} %weight_ref.1) | copy-start | bytes 13828
  19.4 5.5 %collective-permute-start.6 = (f32[3,384]{1,0:T(4,128)S(1)}, f32[3,384]{1,0:T(4,128)S(1)}, u32[]{:S(2)}, u32[]{:S(2)}) collective-permute-start(f32[3,384]{1,0:T(4,128)S(1)} %get-tuple-element.60.partial_ref), channel_id=1, source_target_pairs={{0,12},{4,8},{8,4},{12,0},{1,13},{5,9},{9,5},{13,1},{2,14},{6,10},... | collective-permute-start | bytes 13832 | tf_op jit(solution)/shard_map/ppermute | solution.py:721
  23.3 4.5 %collective-permute-start.5 = (f32[3,384]{1,0:T(4,128)S(1)}, f32[3,384]{1,0:T(4,128)S(1)}, u32[]{:S(2)}, u32[]{:S(2)}) collective-permute-start(f32[3,384]{1,0:T(4,128)S(1)} %get-tuple-element.60.partial_ref), channel_id=1, source_target_pairs={{0,8},{4,12},{8,0},{12,4},{1,9},{5,13},{9,1},{13,5},{2,10},{6,14},... | collective-permute-start | bytes 13832 | tf_op jit(solution)/shard_map/ppermute | solution.py:721
  23.8 4.0 %collective-permute-start.4 = (f32[3,384]{1,0:T(4,128)S(1)}, f32[3,384]{1,0:T(4,128)S(1)}, u32[]{:S(2)}, u32[]{:S(2)}) collective-permute-start(f32[3,384]{1,0:T(4,128)S(1)} %get-tuple-element.60.partial_ref), channel_id=1, source_target_pairs={{0,4},{4,0},{8,12},{12,8},{1,5},{5,1},{9,13},{13,9},{2,6},{6,2},{1... | collective-permute-start | bytes 13832 | tf_op jit(solution)/shard_map/ppermute | solution.py:721

commit v6 on v5

--- a/solution.py
+++ b/solution.py
@@ -236,7 +236,7 @@
 
 def cone_kernel(
     retard_hbm, decay_hbm, cells_hbm, count_hbm, initial_ref, logk_ref, direction_ref, speed_ref, flags_ref,
-    coef_ref, c_ref, t_ref, jy_ref, e_ref, mask_ref, hot_ref, side_hot_ref, rate_ref, meta_ref,
+    coef_ref, c_ref, t_ref, jy_ref, e_ref, mask_ref, hot_ref, side_hot_ref, spread_ref, rate_ref, meta_ref,
     retard_ref, decay_ref, cells_ref, count_ref, sem, *, layers, width, species,
 ):
     copies = [
@@ -313,6 +313,14 @@
         side_hot_ref[:, s * wells : (s + 1) * wells] = jnp.where(hit & (strip_species == s), 1.0, 0.0).astype(BF16)
 
 
+    source = lax.broadcasted_iota(I32, (2 * LANES, LANES), 0)
+    target = lax.broadcasted_iota(I32, (2 * LANES, LANES), 1)
+    target = jnp.where(target < RIGHT, 0, LANES) + target % GROUP
+    for f in range(4):
+        hit = source == target + (species + f) * GROUP
+        spread_ref[:, f * LANES : (f + 1) * LANES] = jnp.where(hit, 1.0, 0.0).astype(BF16)
+
+
 def cone(retard, decay, cells, counts, raw, layers, width, species):
     wells = counts.shape[0]
     state = jax.ShapeDtypeStruct((STEPS, width, species, layers, LANES), F32)
@@ -327,11 +335,12 @@
             jax.ShapeDtypeStruct(((width + 2 * HALO) * layers, wells), BF16),
             jax.ShapeDtypeStruct((LANES, wells), BF16),
             jax.ShapeDtypeStruct((LANES, species * wells), BF16),
+            jax.ShapeDtypeStruct((2 * LANES, 4 * LANES), BF16),
             jax.ShapeDtypeStruct((2 * species + 2, LANES), F32),
             jax.ShapeDtypeStruct((TILE, wells), I32),
         ),
         in_specs=[HBM] * 4 + [VMEM] * 5,
-        out_specs=[VMEM] * 10,
+        out_specs=[VMEM] * 11,
         scratch_shapes=[
             pltpu.SMEM(retard.shape, F32),
             pltpu.SMEM(decay.shape, F32),
@@ -478,7 +487,7 @@
 
 
 def strips_kernel(
-    rate_ref, e_ref, ea_ref, eb_ref, partial_in, mask_ref, hot_ref,
+    rate_ref, e_ref, ea_ref, eb_ref, partial_in, mask_ref, hot_ref, spread_ref,
     partial_ref, coef_ref, c_ref, jy_ref, t_ref, *, layers, width, species,
 ):
     shape = (layers, LANES)
@@ -493,24 +502,22 @@
     ).astype(F32)
     inside_low = jnp.where(gx > 0, 1.0, 0.0).astype(F32)
     inside_high = jnp.where(gx < lax.axis_size("gx") - 1, 1.0, 0.0).astype(F32)
-    group = lane % RIGHT // GROUP
-
-    def spread(first, second, third):
-        return jnp.where(group == 0, first, jnp.where(group == 1, second, third))
+    both = []
+    for r in range(rows):
+        own, outer = e_ref[r], outer_edges(r, ea_ref, eb_ref, near)
+        left_strip, right_strip = jnp.where(near, outer, own), jnp.where(near, own, outer)
+        c_ref[0, r] = jnp.where(left, left_strip, roll(right_strip, RIGHT, 1))
+        both.append(jnp.concatenate([left_strip, right_strip], axis=1))
+    rest = jnp.concatenate(both, axis=0)
+    fields = jnp.zeros((rows * layers, 4 * LANES), F32)
+    for piece in range(3):
+        coarse = rest.astype(BF16)
+        fields = fields + jnp.dot(coarse, spread_ref[...], preferred_element_type=F32)
+        rest = rest - coarse.astype(F32)
 
     kept = None
     for r in range(rows):
-        own = e_ref[r]
-        outer = outer_edges(r, ea_ref, eb_ref, near)
-        left_strip = jnp.where(near, outer, own)
-        right_strip = jnp.where(near, own, outer)
-        low = jnp.where(left, left_strip, roll(right_strip, RIGHT, 1))
-        high = jnp.where(left, roll(left_strip, RIGHT, 1), right_strip)
-        c_ref[0, r] = low
-        by_one, by_two = roll(high, GROUP, 1), roll(high, 2 * GROUP, 1)
-        back_one, back_two = roll(high, -GROUP, 1), roll(high, -2 * GROUP, 1)
-        k = spread(roll(low, -3 * GROUP, 1), roll(low, -2 * GROUP, 1), roll(low, -GROUP, 1))
-        kd, ux, uy = spread(high, by_one, by_two), spread(back_one, high, by_one), spread(back_two, back_one, high)
+        k, kd, ux, uy = [fields[r * layers : (r + 1) * layers, f * LANES : (f + 1) * LANES] for f in range(4)]
         found = y_coefs(k, kd, uy, mask)
         for kind, value in found.items():
             coef_ref[r, kind] = value
@@ -547,7 +554,7 @@
         partial_ref[s : s + 1, :] = partial_in[s : s + 1, :] + total
 
 
-def side_steps(rates, e, ea, eb, partial, mask, hot):
+def side_steps(rates, e, ea, eb, partial, mask, hot, spread):
     rows, layers, _ = e.shape
     species, wells = partial.shape
     state = (STEPS, rows, layers, LANES)
@@ -559,12 +566,12 @@
             jax.ShapeDtypeStruct(state, F32),
             jax.ShapeDtypeStruct(state, F32),
         ),
-        in_specs=[VMEM] * 7,
+        in_specs=[VMEM] * 8,
         out_specs=[VMEM] * 4,
         scratch_shapes=[pltpu.VMEM(state, F32)],
         compiler_params=pltpu.CompilerParams(vmem_limit_bytes=6 * MIB),
         name="strip_steps",
-    )(rates, e, ea, eb, partial, mask, hot)
+    )(rates, e, ea, eb, partial, mask, hot, spread)
 
 
 def adjoint_kernel(
@@ -732,13 +739,13 @@
     species, layers, width, columns = initial.shape
     raw, xa, xb = send_rows(initial, logk, direction, face_speed, face_flags)
     xa, xb = swap_x(xa, xb)
-    coef_in, c_in, t_in, jy_in, e, mask, hot, side_hot, rates, meta = cone(
+    coef_in, c_in, t_in, jy_in, e, mask, hot, side_hot, spread, rates, meta = cone(
         retard, decay, screen_cells.T, screen_count, raw, layers, width, species
     )
     e, ea, eb = all_edges(e, xa, xb)
     ea, eb = swap_y(ea, eb)
     partial, coef_out, c_out, jy_out = rim(rates, xa, xb, coef_in, c_in, t_in, mask, hot)
-    partial, *side = side_steps(rates, e, ea, eb, partial, mask, side_hot)
+    partial, *side = side_steps(rates, e, ea, eb, partial, mask, side_hot, spread)
     reach = -(-(screen_cells.shape[1] - 1 + HALO) // width)
     partials = [partial] + from_others(partial, "gx", reach)
     inner, outer = (coef_in, c_in, jy_in), (coef_out, c_out, jy_out)

time: 32.1 us -> 29.9 us (0.931)
  Pallas kernels: 15.6 us -> 13.6 us
    pallas_call x1, Pallas kernels: 4.3 us -> 2.17 us  [side_steps(): pl.pallas_call(functools.partial(strips_kernel, layers=layers, width=rows...]
  transfers between devices with their start and end apart: 7 -> 7, of which waited for: 4 -> 4; matrix products, arithmetic and copies ran while one was open for 0% -> 0% of each run, Pallas kernels for 17% -> 19%
where the time goes in v6:
time: 29.9 us; the launch traced here: 29.8 us
  Pallas kernels  13.6 us (45%)
  starting transfers between devices  9.62 us (32%)
  waiting for transfers between devices  6.5 us (22%)
    ppermute x3, starting transfers between devices, from_others(): lax.ppermute(value, axis, [(i, i ^ d) for i in range(count)])  4.7 us
    pallas_call x1, Pallas kernels, adjoint(): pl.pallas_call(functools.partial(adjoint_kernel, layers=layers, width=wid...  4.07 us
    pallas_call x1, Pallas kernels, cone(): pl.pallas_call(functools.partial(cone_kernel, layers=layers, width=width,...  3.74 us
    ppermute x3, waiting for transfers between devices, from_others(): lax.ppermute(value, axis, [(i, i ^ d) for i in range(count)])  3.69 us
    ppermute x1, starting transfers between devices, swap_x(): lax.ppermute(first, 'gx', pairs(count, 0))  3.09 us
    pallas_call x1, Pallas kernels, side_steps(): pl.pallas_call(functools.partial(strips_kernel, layers=layers, width=rows...  2.17 us
    ppermute x1, waiting for transfers between devices, swap_x(): lax.ppermute(first, 'gx', pairs(count, 0))  1.85 us
    pallas_call x1, Pallas kernels, rim(): pl.pallas_call(functools.partial(rim_kernel, layers=layers, width=width,...  1.85 us
  transfers between devices with their start and end apart: 7, of which 4 were waited for; matrix products, arithmetic and copies ran while one was open for 0% of the time, Pallas kernels for 19%

profile of v6, /device:TPU:0, one launch (start us, length us, event | category | flops | bytes accessed | tf_op | source)
XLA Modules:
  0.0 29.8 jit_solution(6744879550254840465)
XLA Ops:
  0.0 1.5 %send_rows.1 = (f32[768,128]{1,0:T(8,128)S(1)}, f32[256,128]{1,0:T(8,128)S(1)}, f32[256,128]{1,0:T(8,128)S(1)}, f32[512,128]{1,0:T(8,128)S(1)}, s32[512,128]{1,0...) custom-call(f32[768,128]{1,0:T(8,128)} %bitcast.7, f32[256,128]{1,0:T(8,128)} %bitcast.10, ...), custom_call_target="tpu_custom_call" | custom-call | tf_op jit(solution)/shard_map/send_rows/pallas_call | solution.py:204
  1.5 3.1 %collective-permute-start = (f32[4,7,16,128]{3,2,1,0:T(8,128)S(1)}, f32[4,7,16,128]{3,2,1,0:T(8,128)S(1)}, u32[]{:S(2)}, u32[]{:S(2)}) collective-permute-start(f32[4,7,16,128]{3,2,1,0:T(8,128)S(1)} %get-tuple-element.43), channel_id=1, source_target_pairs={{0,4},{4,0},{8,12},{12,8},{1,5},{5,1},{9,13},{13,9},{2,6},{6,2},{1... | collective-permute-start | bytes 688136 | tf_op jit(solution)/shard_map/ppermute | solution.py:716
  4.6 0.0 collective-permute-start.1
  4.6 3.7 %cone_steps.1 = (f32[16,12,16,128]{3,2,1,0:T(8,128)S(1)}, f32[4,16,3,16,128]{4,3,2,1,0:T(8,128)S(1)}, f32[4,16,3,16,128]{4,3,2,1,0:T(8,128)S(1)}, f32[4,16,3,16,...) custom-call(f32[3]{0:T(128)} %retard_hbm.1, ...), custom_call_target="tpu_custom_call" | custom-call | flops 10000000 | bytes 10000000 | tf_op jit(solution)/shard_map/cone_steps/pallas_call | solution.py:327
  8.3 1.9 %collective-permute-done.xa_ref = f32[4,7,16,128]{3,2,1,0:T(8,128)S(1)} collective-permute-done((f32[4,7,16,128]{3,2,1,0:T(8,128)S(1)}, f32[4,7,16,128]{3,2,1,0:T(8,128)S(1)}, u32[]{:S(2)}, u32[]{:S(2)}) %collective-permute-start) | collective-permute-done | bytes 229408 | tf_op jit(solution)/shard_map/ppermute | solution.py:716
  10.2 0.0 collective-permute-done.1.xb_ref
  10.2 0.3 edge_columns.1
  10.5 0.1 collective-permute-start.2
  10.5 1.8 %collective-permute-start.3 = (f32[12,16,128]{2,1,0:T(8,128)S(1)}, f32[12,16,128]{2,1,0:T(8,128)S(1)}, u32[]{:S(2)}, u32[]{:S(2)}) collective-permute-start(f32[12,16,128]{2,1,0:T(8,128)S(1)} %get-tuple-element.55), channel_id=1, source_target_pairs={{1,2},{2,1},{0,3},{3,0},{5,6},{6,5},{4,7},{7,4},{9,10},{10,9},{8,1... | collective-permute-start | bytes 294920 | tf_op jit(solution)/shard_map/ppermute | solution.py:722
  12.3 0.0 copy-start
  12.3 1.8 %rim_steps.1 = (f32[3,384]{1,0:T(4,128)S(1)}, f32[10,12,16,128]{3,2,1,0:T(8,128)S(1)}, f32[4,8,3,16,128]{4,3,2,1,0:T(8,128)S(1)}, f32[4,8,3,16,128]{4,3,2,1,0:T(8,128)S(1)}) custom-call(f32[8,128]{1,0:T(8,128)S(1)} %get-tuple-element.39.rate_ref, f32[4,7,16,128]{3,2,1,0:T(8,128)S(1)} %collective-permute-done.xa_ref, ...), custom_call_target="tpu_custom_call" | custom-call | flops 10000000 | bytes 10000000 | tf_op jit(solution)/shard_map/rim_steps/pallas_call | solution.py:472
  14.1 0.0 collective-permute-done.2.ea_ref
  14.2 1.0 %collective-permute-done.3.eb_ref = f32[12,16,128]{2,1,0:T(8,128)S(1)} collective-permute-done((f32[12,16,128]{2,1,0:T(8,128)S(1)}, f32[12,16,128]{2,1,0:T(8,128)S(1)}, u32[]{:S(2)}, u32[]{:S(2)}) %collective-permute-start.3) | collective-permute-done | bytes 98336 | tf_op jit(solution)/shard_map/ppermute | solution.py:722
  15.1 2.2 %strip_steps.1 = (f32[3,384]{1,0:T(4,128)S(1)}, f32[24,12,16,128]{3,2,1,0:T(8,128)S(1)}, f32[4,24,16,128]{3,2,1,0:T(8,128)S(1)}, f32[4,24,16,128]{3,2,1,0:T(8,128)S(1)}) custom-call(f32[8,128]{1,0:T(8,128)S(1)} %get-tuple-element.39.rate_ref, f32[24,16,128]{2,1,0:T(8,128)S(1)} %get-tuple-element.53.e_ref, f32[12,16,128]{2,1,0:T(8,128)S(1)} %collective-permute-done.2.ea_ref, ...), custom_call_target="tpu_custom_call" | custom-call | tf_op jit(solution)/shard_map/strip_steps/pallas_call | solution.py:561
  17.3 3.9 %collective-permute-start.6 = (f32[3,384]{1,0:T(4,128)S(1)}, f32[3,384]{1,0:T(4,128)S(1)}, u32[]{:S(2)}, u32[]{:S(2)}) collective-permute-start(f32[3,384]{1,0:T(4,128)S(1)} %get-tuple-element.62.partial_ref), channel_id=1, source_target_pairs={{0,12},{4,8},{8,4},{12,0},{1,13},{5,9},{9,5},{13,1},{2,14},{6,10},... | collective-permute-start | bytes 13832 | tf_op jit(solution)/shard_map/ppermute | solution.py:728
  21.1 0.6 %collective-permute-start.5 = (f32[3,384]{1,0:T(4,128)S(1)}, f32[3,384]{1,0:T(4,128)S(1)}, u32[]{:S(2)}, u32[]{:S(2)}) collective-permute-start(f32[3,384]{1,0:T(4,128)S(1)} %get-tuple-element.62.partial_ref), channel_id=1, source_target_pairs={{0,8},{4,12},{8,0},{12,4},{1,9},{5,13},{9,1},{13,5},{2,10},{6,14},... | collective-permute-start | bytes 13832 | tf_op jit(solution)/shard_map/ppermute | solution.py:728
  21.7 0.3 collective-permute-start.4
  22.0 0.8 %collective-permute-done.6.rest_2_ = f32[3,384]{1,0:T(4,128)S(1)} collective-permute-done((f32[3,384]{1,0:T(4,128)S(1)}, f32[3,384]{1,0:T(4,128)S(1)}, u32[]{:S(2)}, u32[]{:S(2)}) %collective-permute-start.6) | collective-permute-done | bytes 4640 | tf_op jit(solution)/shard_map/ppermute | solution.py:728
  22.8 2.9 %collective-permute-done.5.rest_1_ = f32[3,384]{1,0:T(4,128)S(1)} collective-permute-done((f32[3,384]{1,0:T(4,128)S(1)}, f32[3,384]{1,0:T(4,128)S(1)}, u32[]{:S(2)}, u32[]{:S(2)}) %collective-permute-start.5) | collective-permute-done | bytes 4640 | tf_op jit(solution)/shard_map/ppermute | solution.py:728
  25.7 0.0 collective-permute-done.4.rest_0_
  25.7 0.0 copy-done
  25.7 4.1 %adjoint_steps.1 = f32[256,128]{1,0:T(8,128)} custom-call(f32[8,128]{1,0:T(8,128)S(1)} %get-tuple-element.39.rate_ref, f32[3,384]{1,0:T(4,128)S(1)} %copy-done, s32[8,384]{1,0:T(8,128)S(1)} %get-tuple-element.40.meta_ref, bf16[384,384]{1,0:T(8,128)(2,1)S(1)} %get-tuple-element.41.mask_ref, f32[16,12,16,128]{3,2,1,0:T(8,128)S(1)} %get-tuple-element.42.coef_in, ...), custom_call_target="tpu_custom_call" | custom-call | tf_op jit(solution)/shard_map/adjoint_steps/pallas_call | solution.py:693
Async XLA Ops:
  1.5 8.7 %collective-permute-start = (f32[4,7,16,128]{3,2,1,0:T(8,128)S(1)}, f32[4,7,16,128]{3,2,1,0:T(8,128)S(1)}, u32[]{:S(2)}, u32[]{:S(2)}) collective-permute-start(f32[4,7,16,128]{3,2,1,0:T(8,128)S(1)} %get-tuple-element.43), channel_id=1, source_target_pairs={{0,4},{4,0},{8,12},{12,8},{1,5},{5,1},{9,13},{13,9},{2,6},{6,2},{1... | collective-permute-start | bytes 688136 | tf_op jit(solution)/shard_map/ppermute | solution.py:716
  4.6 5.6 %collective-permute-start.1 = (f32[4,7,16,128]{3,2,1,0:T(8,128)S(1)}, f32[4,7,16,128]{3,2,1,0:T(8,128)S(1)}, u32[]{:S(2)}, u32[]{:S(2)}) collective-permute-start(f32[4,7,16,128]{3,2,1,0:T(8,128)S(1)} %get-tuple-element.44), channel_id=1, source_target_pairs={{0,1},{1,0},{2,3},{3,2},{4,8},{5,9},{6,10},{7,11},{8,4},{9,5},{10,... | collective-permute-start | bytes 688136 | tf_op jit(solution)/shard_map/ppermute | solution.py:716
  10.5 3.7 %collective-permute-start.2 = (f32[12,16,128]{2,1,0:T(8,128)S(1)}, f32[12,16,128]{2,1,0:T(8,128)S(1)}, u32[]{:S(2)}, u32[]{:S(2)}) collective-permute-start(f32[12,16,128]{2,1,0:T(8,128)S(1)} %get-tuple-element.54), channel_id=1, source_target_pairs={{0,1},{1,0},{2,3},{3,2},{4,5},{5,4},{6,7},{7,6},{8,9},{9,8},{10,11... | collective-permute-start | bytes 294920 | tf_op jit(solution)/shard_map/ppermute | solution.py:722
  10.5 4.6 %collective-permute-start.3 = (f32[12,16,128]{2,1,0:T(8,128)S(1)}, f32[12,16,128]{2,1,0:T(8,128)S(1)}, u32[]{:S(2)}, u32[]{:S(2)}) collective-permute-start(f32[12,16,128]{2,1,0:T(8,128)S(1)} %get-tuple-element.55), channel_id=1, source_target_pairs={{1,2},{2,1},{0,3},{3,0},{5,6},{6,5},{4,7},{7,4},{9,10},{10,9},{8,1... | collective-permute-start | bytes 294920 | tf_op jit(solution)/shard_map/ppermute | solution.py:722
  12.3 13.4 %copy-start = (f32[3,384]{1,0:T(4,128)S(1)}, f32[3,384]{1,0:T(4,128)}, u32[]{:S(2)}) copy-start(f32[3,384]{1,0:T(4,128)} %weight_ref.1) | copy-start | bytes 13828
  17.3 5.5 %collective-permute-start.6 = (f32[3,384]{1,0:T(4,128)S(1)}, f32[3,384]{1,0:T(4,128)S(1)}, u32[]{:S(2)}, u32[]{:S(2)}) collective-permute-start(f32[3,384]{1,0:T(4,128)S(1)} %get-tuple-element.62.partial_ref), channel_id=1, source_target_pairs={{0,12},{4,8},{8,4},{12,0},{1,13},{5,9},{9,5},{13,1},{2,14},{6,10},... | collective-permute-start | bytes 13832 | tf_op jit(solution)/shard_map/ppermute | solution.py:728
  21.1 4.5 %collective-permute-start.5 = (f32[3,384]{1,0:T(4,128)S(1)}, f32[3,384]{1,0:T(4,128)S(1)}, u32[]{:S(2)}, u32[]{:S(2)}) collective-permute-start(f32[3,384]{1,0:T(4,128)S(1)} %get-tuple-element.62.partial_ref), channel_id=1, source_target_pairs={{0,8},{4,12},{8,0},{12,4},{1,9},{5,13},{9,1},{13,5},{2,10},{6,14},... | collective-permute-start | bytes 13832 | tf_op jit(solution)/shard_map/ppermute | solution.py:728
  21.7 4.0 %collective-permute-start.4 = (f32[3,384]{1,0:T(4,128)S(1)}, f32[3,384]{1,0:T(4,128)S(1)}, u32[]{:S(2)}, u32[]{:S(2)}) collective-permute-start(f32[3,384]{1,0:T(4,128)S(1)} %get-tuple-element.62.partial_ref), channel_id=1, source_target_pairs={{0,4},{4,0},{8,12},{12,8},{1,5},{5,1},{9,13},{13,9},{2,6},{6,2},{1... | collective-permute-start | bytes 13832 | tf_op jit(solution)/shard_map/ppermute | solution.py:728

commit v7 on v6

--- a/solution.py
+++ b/solution.py
@@ -158,6 +158,10 @@
     put_t(s, source)
 
 
+def once(load):
+    return functools.cache(load)
+
+
 def put_at(ref, m, index):
     def store(s, value):
         ref[m, index, s] = value
@@ -236,7 +240,7 @@
 
 def cone_kernel(
     retard_hbm, decay_hbm, cells_hbm, count_hbm, initial_ref, logk_ref, direction_ref, speed_ref, flags_ref,
-    coef_ref, c_ref, t_ref, jy_ref, e_ref, mask_ref, hot_ref, side_hot_ref, spread_ref, rate_ref, meta_ref,
+    coef_ref, c_ref, t_ref, jy_ref, e_ref, mask_ref, hot_ref, side_hot_ref, spread_ref, patch_ref, rate_ref, meta_ref,
     retard_ref, decay_ref, cells_ref, count_ref, sem, *, layers, width, species,
 ):
     copies = [
@@ -283,16 +287,14 @@
     rate_ref[species : species + 1, :] = strips
 
     for m in range(STEPS):
+        coef = once(lambda kind, r: coef_ref[r - HALO, kind])
+        state = once(lambda r, s: c_ref[m, r - HALO, s])
+        tangent = once(lambda r, s: t_ref[m - 1, r - HALO, s])
         for r in range(HALO + 1 + m, HALO + width - 1 - m):
             x = r - HALO
+            puts = put_at(c_ref, m + 1, x), put_at(t_ref, m, x), put_at(jy_ref, m, x)
             for s in range(species):
-                step_cell(
-                    r, m, s, rates[s],
-                    lambda kind, r: coef_ref[r - HALO, kind],
-                    lambda r, s: c_ref[m, r - HALO, s],
-                    lambda r, s: t_ref[m - 1, r - HALO, s],
-                    put_at(c_ref, m + 1, x), put_at(t_ref, m, x), put_at(jy_ref, m, x),
-                )
+                step_cell(r, m, s, rates[s], coef, state, tangent, *puts)
 
     wells = meta_ref.shape[1]
     table = well_table(cells_ref, count_ref[...].reshape(1, wells), width)
@@ -319,6 +321,11 @@
     for f in range(4):
         hit = source == target + (species + f) * GROUP
         spread_ref[:, f * LANES : (f + 1) * LANES] = jnp.where(hit, 1.0, 0.0).astype(BF16)
+    source, target = source[:LANES], lax.broadcasted_iota(I32, (LANES, LANES), 1)
+    used = (target < STEPS) | (target >= LANES - STEPS)
+    same = (source < RIGHT) == (target < STEPS)
+    hit = used & same & (source % RIGHT < species * GROUP) & (source % GROUP == (target + 8) % GROUP)
+    patch_ref[...] = jnp.where(hit, 1.0, 0.0).astype(BF16)
 
 
 def cone(retard, decay, cells, counts, raw, layers, width, species):
@@ -336,11 +343,12 @@
             jax.ShapeDtypeStruct((LANES, wells), BF16),
             jax.ShapeDtypeStruct((LANES, species * wells), BF16),
             jax.ShapeDtypeStruct((2 * LANES, 4 * LANES), BF16),
+            jax.ShapeDtypeStruct((LANES, LANES), BF16),
             jax.ShapeDtypeStruct((2 * species + 2, LANES), F32),
             jax.ShapeDtypeStruct((TILE, wells), I32),
         ),
         in_specs=[HBM] * 4 + [VMEM] * 5,
-        out_specs=[VMEM] * 11,
+        out_specs=[VMEM] * 12,
         scratch_shapes=[
             pltpu.SMEM(retard.shape, F32),
             pltpu.SMEM(decay.shape, F32),
@@ -444,15 +452,14 @@
         put_coef(D, r, value)
 
     for m in range(STEPS):
+        coef = once(get)
+        state = once(lambda r, s: read_state((c_in, c_out), m, width, r, s))
+        tangent = once(lambda r, s: tangent_row(t_in, t_out, m, width, r)[s])
         for r in list(range(1 + m, HALO + 1 + m)) + list(range(last - m, rows - 1 - m)):
             index = state_row(m + 1, width)(r)[1]
+            puts = put_at(c_out, m + 1, index), put_at(t_out, m, index), put_at(jy_out, m, index)
             for s in range(species):
-                step_cell(
-                    r, m, s, rate_ref[s : s + 1, :], get,
-                    lambda r, s: read_state((c_in, c_out), m, width, r, s),
-                    lambda r, s: tangent_row(t_in, t_out, m, width, r)[s],
-                    put_at(c_out, m + 1, index), put_at(t_out, m, index), put_at(jy_out, m, index),
-                )
+                step_cell(r, m, s, rate_ref[s : s + 1, :], coef, state, tangent, *puts)
 
     masks = mask_ref[HALO * layers : (HALO + width) * layers, :]
     for s in range(species):
@@ -530,23 +537,19 @@
             diagonal = diagonal + q
         kept = (k, kd, ux, diagonal)
 
+    def put(ref, m, r):
+        def store(s, value):
+            ref[m, r] = value
+
+        return store
+
     rate = rate_ref[species : species + 1, :]
     for m in range(STEPS):
+        coef = once(lambda kind, r: coef_ref[r, kind])
+        state = once(lambda r, s: c_ref[m, r])
+        tangent = once(lambda r, s: t_ref[m - 1, r])
         for r in range(1 + m, rows - 1 - m):
-
-            def put(ref, slot):
-                def store(s, value):
-                    ref[slot, r] = value
-
-                return store
-
-            step_cell(
-                r, m, 0, rate,
-                lambda kind, r: coef_ref[r, kind],
-                lambda r, s: c_ref[m, r],
-                lambda r, s: t_ref[m - 1, r],
-                put(c_ref, m + 1), put(t_ref, m), put(jy_ref, m),
-            )
+            step_cell(r, m, 0, rate, coef, state, tangent, put(c_ref, m + 1, r), put(t_ref, m, r), put(jy_ref, m, r))
 
     masks = mask_ref[HALO * layers : (HALO + width) * layers, :]
     block = jnp.concatenate([t_ref[STEPS - 1, r] for r in range(HALO, HALO + width)], axis=0)
@@ -576,7 +579,7 @@
 
 def adjoint_kernel(
     rate_ref, weight_ref, meta_ref, mask_ref, coef_in, coef_out, c_in, c_out, jy_in, jy_out,
-    coef_side, c_side, jy_side, partial_ref, *rest, layers, width, species, parts,
+    coef_side, c_side, jy_side, patch_ref, partial_ref, *rest, layers, width, species, parts,
 ):
     others, out_ref, lam_ref = rest[:parts], *rest[parts:]
     rows = width + 2 * HALO
@@ -622,23 +625,23 @@
     def add(key, term):
         sums[key] = sums[key] + term if key in sums else term
 
+    rates = [rate_ref[s : s + 1, :] for s in range(species + 1)]
     for m in reversed(range(STEPS)):
         now = STEPS - 1 - m
         low, high = STEPS - m, rows - 1 - (STEPS - m)
+        lam_row = once(lambda r, s: lam_ref[now, r, s])
+        main, side = once(main_coef), once(side_coef)
+        state = once(lambda r, s: c_side[m, r] if s == species else read_state((c_in, c_out), m, width, r, s))
         for r in range(min(low, first_row), max(high, last_row) + 1):
             sense, retreat = first_row <= r <= last_row, m > 0 and low <= r <= high
+            results = []
             for s in range(species + 1):
                 is_side = s == species
-                coef = side_coef if is_side else main_coef
-                value, up = lam_ref[now, r, s], lam_ref[now, r + 1, s]
+                coef = side if is_side else main
+                value, up = lam_row(r, s), lam_row(r + 1, s)
                 after = y_next(value)
                 if sense:
-                    if is_side:
-                        jump = c_side[m, r + 1] - c_side[m, r]
-                    else:
-                        states = (c_in, c_out)
-                        jump = read_state(states, m, width, r + 1, s) - read_state(states, m, width, r, s)
-                    add(("x", is_side, r), jump * (up - value))
+                    add(("x", is_side, r), (state(r + 1, s) - state(r, s)) * (up - value))
                     if r >= HALO:
                         if is_side:
                             jump = jy_side[m, r]
@@ -647,14 +650,16 @@
                             jump = (jy_in, jy_out)[which][m, index, s]
                         add(("y", is_side, r), jump * (after - value))
                 if retreat:
-                    lam_ref[now + 1, r, s] = (
-                        (rate_ref[s : s + 1, :] - coef(D, r)) * value
+                    results.append(
+                        (rates[s] - coef(D, r)) * value
                         + coef(PX, r) * up
-                        + coef(QX, r - 1) * lam_ref[now, r - 1, s]
+                        + coef(QX, r - 1) * lam_row(r - 1, s)
                         + coef(PY, r) * after
                         + coef(QYM, r) * y_previous(value)
                         + RATE * z_pair(value)
                     )
+            for s, result in enumerate(results):
+                lam_ref[now + 1, r, s] = result
 
     column, left = lane % GROUP, lane < RIGHT
     first_y, last_y = gy == 0, gy == lax.axis_size(Y) - 1
@@ -663,33 +668,45 @@
     ).astype(F32)
     inside_low = jnp.where(gx > 0, 1.0, 0.0).astype(F32)
     inside_high = jnp.where(gx < lax.axis_size("gx") - 1, 1.0, 0.0).astype(F32)
-    for x in range(width):
-        r = x + HALO
-        totals = []
-        for is_side in (False, True):
-            upper, lower = sums["x", is_side, r], sums["x", is_side, r - 1]
-            if x == 0:
-                lower = lower * inside_low
-            if x == width - 1:
+
+    sides, results = [], []
+    for is_side in (True, False):
+        lower = None
+        for r in range(HALO - 1, HALO + width):
+            upper, along_y = sums["x", is_side, r], sums.get(("y", is_side, r))
+            if r < HALO:
+                lower = upper * inside_low
+                continue
+            if r == HALO + width - 1:
                 upper = upper * inside_high
-            along_y = sums["y", is_side, r]
             if is_side:
                 along_y = along_y * side_mask
-            totals.append(upper + lower + along_y + y_previous(along_y))
-        total, side = totals
-        all_species = side
-        for s in range(1, species):
-            all_species = all_species + roll(side, -GROUP * s, 1)
-        total = jnp.where(lane < STEPS, roll(all_species, -8, 1), total)
-        total = jnp.where(lane >= LANES - STEPS, roll(all_species, 120 - RIGHT, 1), total)
-        out_ref[pl.ds(x, layers, stride=width), :] = -HALF_DT * main_coef(K, r) * total
-
-
-def adjoint(rates, weight, meta, mask, inner, outer, side, partials):
+            total = upper + lower + along_y + y_previous(along_y)
+            lower = upper
+            if is_side:
+                sides.append(total)
+                if len(sides) == width:
+                    rest = jnp.concatenate(sides, axis=0)
+                    patch = jnp.zeros_like(rest)
+                    for piece in range(3):
+                        coarse = rest.astype(BF16)
+                        patch = patch + jnp.dot(coarse, patch_ref[...], preferred_element_type=F32)
+                        rest = rest - coarse.astype(F32)
+            else:
+                x = r - HALO
+                total = jnp.where(
+                    (lane < STEPS) | (lane >= LANES - STEPS), patch[x * layers : (x + 1) * layers], total
+                )
+                results.append(-HALF_DT * main_coef(K, r) * total)
+    for x, result in enumerate(results):
+        out_ref[pl.ds(x, layers, stride=width), :] = result
+
+
+def adjoint(rates, weight, meta, mask, inner, outer, side, patch, partials):
     (coef_in, c_in, jy_in), (coef_out, c_out, jy_out) = inner, outer
     _, width, species, layers, _ = c_in.shape
     parts = len(partials) - 1
-    operands = (rates, weight, meta, mask, coef_in, coef_out, c_in, c_out, jy_in, jy_out, *side, *partials)
+    operands = (rates, weight, meta, mask, coef_in, coef_out, c_in, c_out, jy_in, jy_out, *side, patch, *partials)
     return pl.pallas_call(
         functools.partial(adjoint_kernel, layers=layers, width=width, species=species, parts=parts),
         out_shape=jax.ShapeDtypeStruct((layers * width, LANES), F32),
@@ -739,7 +756,7 @@
     species, layers, width, columns = initial.shape
     raw, xa, xb = send_rows(initial, logk, direction, face_speed, face_flags)
     xa, xb = swap_x(xa, xb)
-    coef_in, c_in, t_in, jy_in, e, mask, hot, side_hot, spread, rates, meta = cone(
+    coef_in, c_in, t_in, jy_in, e, mask, hot, side_hot, spread, patch, rates, meta = cone(
         retard, decay, screen_cells.T, screen_count, raw, layers, width, species
     )
     e, ea, eb = all_edges(e, xa, xb)
@@ -749,7 +766,7 @@
     reach = -(-(screen_cells.shape[1] - 1 + HALO) // width)
     partials = [partial] + from_others(partial, "gx", reach)
     inner, outer = (coef_in, c_in, jy_in), (coef_out, c_out, jy_out)
-    hessian = adjoint(rates, well_weight, meta, mask, inner, outer, side, partials)
+    hessian = adjoint(rates, well_weight, meta, mask, inner, outer, side, patch, partials)
     return hessian.reshape(layers, width, columns)
 
 

time: 29.9 us -> 29.4 us (0.983)
  Pallas kernels: 13.6 us -> 12.9 us
    pallas_call x1, Pallas kernels: 4.07 us -> 3.56 us  [adjoint(): pl.pallas_call(functools.partial(adjoint_kernel, layers=layers, width=wid...]
where the time goes in v7:
time: 29.4 us; the launch traced here: 29.2 us
  Pallas kernels  12.9 us (44%)
  starting transfers between devices  9.62 us (33%)
  waiting for transfers between devices  6.6 us (22%)
    ppermute x3, starting transfers between devices, from_others(): lax.ppermute(value, axis, [(i, i ^ d) for i in range(count)])  4.7 us
    pallas_call x1, Pallas kernels, cone(): pl.pallas_call(functools.partial(cone_kernel, layers=layers, width=width,...  3.7 us
    ppermute x3, waiting for transfers between devices, from_others(): lax.ppermute(value, axis, [(i, i ^ d) for i in range(count)])  3.69 us
    pallas_call x1, Pallas kernels, adjoint(): pl.pallas_call(functools.partial(adjoint_kernel, layers=layers, width=wid...  3.56 us
    ppermute x1, starting transfers between devices, swap_x(): lax.ppermute(first, 'gx', pairs(count, 0))  3.09 us
    pallas_call x1, Pallas kernels, side_steps(): pl.pallas_call(functools.partial(strips_kernel, layers=layers, width=rows...  2.11 us
    ppermute x1, waiting for transfers between devices, swap_x(): lax.ppermute(first, 'gx', pairs(count, 0))  1.9 us
    pallas_call x1, Pallas kernels, rim(): pl.pallas_call(functools.partial(rim_kernel, layers=layers, width=width,...  1.79 us
  transfers between devices with their start and end apart: 7, of which 4 were waited for; matrix products, arithmetic and copies ran while one was open for 0% of the time, Pallas kernels for 19%

profile of v7, /device:TPU:0, one launch (start us, length us, event | category | flops | bytes accessed | tf_op | source)
XLA Modules:
  0.0 29.2 jit_solution(17877848390138463473)
XLA Ops:
  0.0 1.5 %send_rows.1 = (f32[768,128]{1,0:T(8,128)S(1)}, f32[256,128]{1,0:T(8,128)S(1)}, f32[256,128]{1,0:T(8,128)S(1)}, f32[512,128]{1,0:T(8,128)S(1)}, s32[512,128]{1,0...) custom-call(f32[768,128]{1,0:T(8,128)} %bitcast.7, f32[256,128]{1,0:T(8,128)} %bitcast.10, ...), custom_call_target="tpu_custom_call" | custom-call | tf_op jit(solution)/shard_map/send_rows/pallas_call | solution.py:208
  1.5 3.1 %collective-permute-start = (f32[4,7,16,128]{3,2,1,0:T(8,128)S(1)}, f32[4,7,16,128]{3,2,1,0:T(8,128)S(1)}, u32[]{:S(2)}, u32[]{:S(2)}) collective-permute-start(f32[4,7,16,128]{3,2,1,0:T(8,128)S(1)} %get-tuple-element.44), channel_id=1, source_target_pairs={{0,4},{4,0},{8,12},{12,8},{1,5},{5,1},{9,13},{13,9},{2,6},{6,2},{1... | collective-permute-start | bytes 688136 | tf_op jit(solution)/shard_map/ppermute | solution.py:733
  4.6 0.0 collective-permute-start.1
  4.6 3.7 %cone_steps.1 = (f32[16,12,16,128]{3,2,1,0:T(8,128)S(1)}, f32[4,16,3,16,128]{4,3,2,1,0:T(8,128)S(1)}, f32[4,16,3,16,128]{4,3,2,1,0:T(8,128)S(1)}, f32[4,16,3,16,...) custom-call(f32[3]{0:T(128)} %retard_hbm.1, ...), custom_call_target="tpu_custom_call" | custom-call | flops 10000000 | bytes 10000000 | tf_op jit(solution)/shard_map/cone_steps/pallas_call | solution.py:334
  8.3 1.9 %collective-permute-done.xa_ref = f32[4,7,16,128]{3,2,1,0:T(8,128)S(1)} collective-permute-done((f32[4,7,16,128]{3,2,1,0:T(8,128)S(1)}, f32[4,7,16,128]{3,2,1,0:T(8,128)S(1)}, u32[]{:S(2)}, u32[]{:S(2)}) %collective-permute-start) | collective-permute-done | bytes 229408 | tf_op jit(solution)/shard_map/ppermute | solution.py:733
  10.2 0.0 collective-permute-done.1.xb_ref
  10.2 0.3 edge_columns.1
  10.5 0.1 collective-permute-start.2
  10.5 1.8 %collective-permute-start.3 = (f32[12,16,128]{2,1,0:T(8,128)S(1)}, f32[12,16,128]{2,1,0:T(8,128)S(1)}, u32[]{:S(2)}, u32[]{:S(2)}) collective-permute-start(f32[12,16,128]{2,1,0:T(8,128)S(1)} %get-tuple-element.56), channel_id=1, source_target_pairs={{1,2},{2,1},{0,3},{3,0},{5,6},{6,5},{4,7},{7,4},{9,10},{10,9},{8,1... | collective-permute-start | bytes 294920 | tf_op jit(solution)/shard_map/ppermute | solution.py:739
  12.3 0.0 copy-start
  12.3 1.8 %rim_steps.1 = (f32[3,384]{1,0:T(4,128)S(1)}, f32[10,12,16,128]{3,2,1,0:T(8,128)S(1)}, f32[4,8,3,16,128]{4,3,2,1,0:T(8,128)S(1)}, f32[4,8,3,16,128]{4,3,2,1,0:T(8,128)S(1)}) custom-call(f32[8,128]{1,0:T(8,128)S(1)} %get-tuple-element.40.rate_ref, f32[4,7,16,128]{3,2,1,0:T(8,128)S(1)} %collective-permute-done.xa_ref, ...), custom_call_target="tpu_custom_call" | custom-call | flops 10000000 | bytes 10000000 | tf_op jit(solution)/shard_map/rim_steps/pallas_call | solution.py:479
  14.1 0.0 collective-permute-done.2.ea_ref
  14.1 1.0 %collective-permute-done.3.eb_ref = f32[12,16,128]{2,1,0:T(8,128)S(1)} collective-permute-done((f32[12,16,128]{2,1,0:T(8,128)S(1)}, f32[12,16,128]{2,1,0:T(8,128)S(1)}, u32[]{:S(2)}, u32[]{:S(2)}) %collective-permute-start.3) | collective-permute-done | bytes 98336 | tf_op jit(solution)/shard_map/ppermute | solution.py:739
  15.1 2.1 %strip_steps.1 = (f32[3,384]{1,0:T(4,128)S(1)}, f32[24,12,16,128]{3,2,1,0:T(8,128)S(1)}, f32[4,24,16,128]{3,2,1,0:T(8,128)S(1)}, f32[4,24,16,128]{3,2,1,0:T(8,128)S(1)}) custom-call(f32[8,128]{1,0:T(8,128)S(1)} %get-tuple-element.40.rate_ref, f32[24,16,128]{2,1,0:T(8,128)S(1)} %get-tuple-element.54.e_ref, f32[12,16,128]{2,1,0:T(8,128)S(1)} %collective-permute-done.2.ea_ref, ...), custom_call_target="tpu_custom_call" | custom-call | tf_op jit(solution)/shard_map/strip_steps/pallas_call | solution.py:564
  17.2 3.9 %collective-permute-start.6 = (f32[3,384]{1,0:T(4,128)S(1)}, f32[3,384]{1,0:T(4,128)S(1)}, u32[]{:S(2)}, u32[]{:S(2)}) collective-permute-start(f32[3,384]{1,0:T(4,128)S(1)} %get-tuple-element.64.partial_ref), channel_id=1, source_target_pairs={{0,12},{4,8},{8,4},{12,0},{1,13},{5,9},{9,5},{13,1},{2,14},{6,10},... | collective-permute-start | bytes 13832 | tf_op jit(solution)/shard_map/ppermute | solution.py:745
  21.1 0.6 %collective-permute-start.5 = (f32[3,384]{1,0:T(4,128)S(1)}, f32[3,384]{1,0:T(4,128)S(1)}, u32[]{:S(2)}, u32[]{:S(2)}) collective-permute-start(f32[3,384]{1,0:T(4,128)S(1)} %get-tuple-element.64.partial_ref), channel_id=1, source_target_pairs={{0,8},{4,12},{8,0},{12,4},{1,9},{5,13},{9,1},{13,5},{2,10},{6,14},... | collective-permute-start | bytes 13832 | tf_op jit(solution)/shard_map/ppermute | solution.py:745
  21.6 0.3 collective-permute-start.4
  21.9 0.8 %collective-permute-done.6.rest_2_ = f32[3,384]{1,0:T(4,128)S(1)} collective-permute-done((f32[3,384]{1,0:T(4,128)S(1)}, f32[3,384]{1,0:T(4,128)S(1)}, u32[]{:S(2)}, u32[]{:S(2)}) %collective-permute-start.6) | collective-permute-done | bytes 4640 | tf_op jit(solution)/shard_map/ppermute | solution.py:745
  22.7 2.9 %collective-permute-done.5.rest_1_ = f32[3,384]{1,0:T(4,128)S(1)} collective-permute-done((f32[3,384]{1,0:T(4,128)S(1)}, f32[3,384]{1,0:T(4,128)S(1)}, u32[]{:S(2)}, u32[]{:S(2)}) %collective-permute-start.5) | collective-permute-done | bytes 4640 | tf_op jit(solution)/shard_map/ppermute | solution.py:745
  25.6 0.0 collective-permute-done.4.rest_0_
  25.6 0.0 copy-done
  25.6 3.6 %adjoint_steps.1 = f32[256,128]{1,0:T(8,128)} custom-call(f32[8,128]{1,0:T(8,128)S(1)} %get-tuple-element.40.rate_ref, f32[3,384]{1,0:T(4,128)S(1)} %copy-done, s32[8,384]{1,0:T(8,128)S(1)} %get-tuple-element.41.meta_ref, bf16[384,384]{1,0:T(8,128)(2,1)S(1)} %get-tuple-element.42.mask_ref, f32[16,12,16,128]{3,2,1,0:T(8,128)S(1)} %get-tuple-element.43.coef_in, ...), custom_call_target="tpu_custom_call" | custom-call | tf_op jit(solution)/shard_map/adjoint_steps/pallas_call | solution.py:710
Async XLA Ops:
  1.5 8.7 %collective-permute-start = (f32[4,7,16,128]{3,2,1,0:T(8,128)S(1)}, f32[4,7,16,128]{3,2,1,0:T(8,128)S(1)}, u32[]{:S(2)}, u32[]{:S(2)}) collective-permute-start(f32[4,7,16,128]{3,2,1,0:T(8,128)S(1)} %get-tuple-element.44), channel_id=1, source_target_pairs={{0,4},{4,0},{8,12},{12,8},{1,5},{5,1},{9,13},{13,9},{2,6},{6,2},{1... | collective-permute-start | bytes 688136 | tf_op jit(solution)/shard_map/ppermute | solution.py:733
  4.6 5.6 %collective-permute-start.1 = (f32[4,7,16,128]{3,2,1,0:T(8,128)S(1)}, f32[4,7,16,128]{3,2,1,0:T(8,128)S(1)}, u32[]{:S(2)}, u32[]{:S(2)}) collective-permute-start(f32[4,7,16,128]{3,2,1,0:T(8,128)S(1)} %get-tuple-element.45), channel_id=1, source_target_pairs={{0,1},{1,0},{2,3},{3,2},{4,8},{5,9},{6,10},{7,11},{8,4},{9,5},{10,... | collective-permute-start | bytes 688136 | tf_op jit(solution)/shard_map/ppermute | solution.py:733
  10.5 3.6 %collective-permute-start.2 = (f32[12,16,128]{2,1,0:T(8,128)S(1)}, f32[12,16,128]{2,1,0:T(8,128)S(1)}, u32[]{:S(2)}, u32[]{:S(2)}) collective-permute-start(f32[12,16,128]{2,1,0:T(8,128)S(1)} %get-tuple-element.55), channel_id=1, source_target_pairs={{0,1},{1,0},{2,3},{3,2},{4,5},{5,4},{6,7},{7,6},{8,9},{9,8},{10,11... | collective-permute-start | bytes 294920 | tf_op jit(solution)/shard_map/ppermute | solution.py:739
  10.5 4.6 %collective-permute-start.3 = (f32[12,16,128]{2,1,0:T(8,128)S(1)}, f32[12,16,128]{2,1,0:T(8,128)S(1)}, u32[]{:S(2)}, u32[]{:S(2)}) collective-permute-start(f32[12,16,128]{2,1,0:T(8,128)S(1)} %get-tuple-element.56), channel_id=1, source_target_pairs={{1,2},{2,1},{0,3},{3,0},{5,6},{6,5},{4,7},{7,4},{9,10},{10,9},{8,1... | collective-permute-start | bytes 294920 | tf_op jit(solution)/shard_map/ppermute | solution.py:739
  12.3 13.3 %copy-start = (f32[3,384]{1,0:T(4,128)S(1)}, f32[3,384]{1,0:T(4,128)}, u32[]{:S(2)}) copy-start(f32[3,384]{1,0:T(4,128)} %weight_ref.1) | copy-start | bytes 13828
  17.2 5.5 %collective-permute-start.6 = (f32[3,384]{1,0:T(4,128)S(1)}, f32[3,384]{1,0:T(4,128)S(1)}, u32[]{:S(2)}, u32[]{:S(2)}) collective-permute-start(f32[3,384]{1,0:T(4,128)S(1)} %get-tuple-element.64.partial_ref), channel_id=1, source_target_pairs={{0,12},{4,8},{8,4},{12,0},{1,13},{5,9},{9,5},{13,1},{2,14},{6,10},... | collective-permute-start | bytes 13832 | tf_op jit(solution)/shard_map/ppermute | solution.py:745
  21.1 4.5 %collective-permute-start.5 = (f32[3,384]{1,0:T(4,128)S(1)}, f32[3,384]{1,0:T(4,128)S(1)}, u32[]{:S(2)}, u32[]{:S(2)}) collective-permute-start(f32[3,384]{1,0:T(4,128)S(1)} %get-tuple-element.64.partial_ref), channel_id=1, source_target_pairs={{0,8},{4,12},{8,0},{12,4},{1,9},{5,13},{9,1},{13,5},{2,10},{6,14},... | collective-permute-start | bytes 13832 | tf_op jit(solution)/shard_map/ppermute | solution.py:745
  21.6 4.0 %collective-permute-start.4 = (f32[3,384]{1,0:T(4,128)S(1)}, f32[3,384]{1,0:T(4,128)S(1)}, u32[]{:S(2)}, u32[]{:S(2)}) collective-permute-start(f32[3,384]{1,0:T(4,128)S(1)} %get-tuple-element.64.partial_ref), channel_id=1, source_target_pairs={{0,4},{4,0},{8,12},{12,8},{1,5},{5,1},{9,13},{13,9},{2,6},{6,2},{1... | collective-permute-start | bytes 13832 | tf_op jit(solution)/shard_map/ppermute | solution.py:745

commit v8 on v7

--- a/solution.py
+++ b/solution.py
@@ -158,6 +158,14 @@
     put_t(s, source)
 
 
+def pieces_of(value, axis):
+    parts = []
+    for _ in range(3):
+        parts.append(value.astype(BF16))
+        value = value - parts[-1].astype(F32)
+    return jnp.concatenate(parts, axis=axis)
+
+
 def once(load):
     return functools.cache(load)
 
@@ -170,11 +178,7 @@
 
 
 def picked_sums(wide, hot, masks, layers):
-    picked = jnp.zeros((wide.shape[0], hot.shape[1]), F32)
-    for piece in range(3):
-        coarse = wide.astype(BF16)
-        picked = picked + jnp.dot(coarse, hot, preferred_element_type=F32)
-        wide = wide - coarse.astype(F32)
+    picked = jnp.dot(pieces_of(wide, 1), jnp.concatenate([hot] * 3, axis=0), preferred_element_type=F32)
     wells = masks.shape[1]
     totals = []
     for s in range(hot.shape[1] // wells):
@@ -515,12 +519,11 @@
         left_strip, right_strip = jnp.where(near, outer, own), jnp.where(near, own, outer)
         c_ref[0, r] = jnp.where(left, left_strip, roll(right_strip, RIGHT, 1))
         both.append(jnp.concatenate([left_strip, right_strip], axis=1))
-    rest = jnp.concatenate(both, axis=0)
-    fields = jnp.zeros((rows * layers, 4 * LANES), F32)
-    for piece in range(3):
-        coarse = rest.astype(BF16)
-        fields = fields + jnp.dot(coarse, spread_ref[...], preferred_element_type=F32)
-        rest = rest - coarse.astype(F32)
+    fields = jnp.dot(
+        pieces_of(jnp.concatenate(both, axis=0), 1),
+        jnp.concatenate([spread_ref[...]] * 3, axis=0),
+        preferred_element_type=F32,
+    )
 
     kept = None
     for r in range(rows):
@@ -600,7 +603,7 @@
         factor = rate_ref[species + 1 + s, 0:1][:, None]
         residual = weight_ref[s : s + 1, :] * (total * factor) / counts
         residuals.append(residual / counts * factor)
-    lam = jnp.zeros((rows * layers, (species + 1) * LANES), F32)
+    spreads = []
     for piece in range(3):
         coarse = [r.astype(BF16).astype(F32) for r in residuals]
         residuals = [r - q for r, q in zip(residuals, coarse)]
@@ -608,8 +611,13 @@
         side = jnp.zeros((LANES, wells), F32)
         for s in range(species):
             side = jnp.where(strip_hit & (strip_species == s), coarse[s], side)
-        spread = jnp.concatenate(blocks + [side.astype(BF16)], axis=0)
-        lam = lam + lax.dot_general(mask_ref[...], spread, (((1,), (1,)), ((), ())), preferred_element_type=F32)
+        spreads.append(jnp.concatenate(blocks + [side.astype(BF16)], axis=0))
+    lam = lax.dot_general(
+        jnp.concatenate([mask_ref[...]] * len(spreads), axis=1),
+        jnp.concatenate(spreads, axis=1),
+        (((1,), (1,)), ((), ())),
+        preferred_element_type=F32,
+    )
     for s in range(species + 1):
         lam_ref[0, :, s] = lam[:, s * LANES : (s + 1) * LANES].reshape(rows, layers, LANES)
 
@@ -686,12 +694,11 @@
             if is_side:
                 sides.append(total)
                 if len(sides) == width:
-                    rest = jnp.concatenate(sides, axis=0)
-                    patch = jnp.zeros_like(rest)
-                    for piece in range(3):
-                        coarse = rest.astype(BF16)
-                        patch = patch + jnp.dot(coarse, patch_ref[...], preferred_element_type=F32)
-                        rest = rest - coarse.astype(F32)
+                    patch = jnp.dot(
+                        pieces_of(jnp.concatenate(sides, axis=0), 1),
+                        jnp.concatenate([patch_ref[...]] * 3, axis=0),
+                        preferred_element_type=F32,
+                    )
             else:
                 x = r - HALO
                 total = jnp.where(

time: 29.4 us -> 29 us (0.986)
  Pallas kernels: 12.9 us -> 12.5 us
where the time goes in v8:
time: 29 us; the launch traced here: 28.8 us
  Pallas kernels  12.5 us (43%)
  starting transfers between devices  9.61 us (33%)
  waiting for transfers between devices  6.68 us (23%)
    ppermute x3, starting transfers between devices, from_others(): lax.ppermute(value, axis, [(i, i ^ d) for i in range(count)])  4.7 us
    pallas_call x1, Pallas kernels, cone(): pl.pallas_call(functools.partial(cone_kernel, layers=layers, width=width,...  3.7 us
    ppermute x3, waiting for transfers between devices, from_others(): lax.ppermute(value, axis, [(i, i ^ d) for i in range(count)])  3.69 us
    pallas_call x1, Pallas kernels, adjoint(): pl.pallas_call(functools.partial(adjoint_kernel, layers=layers, width=wid...  3.4 us
    ppermute x1, starting transfers between devices, swap_x(): lax.ppermute(first, 'gx', pairs(count, 0))  3.09 us
    pallas_call x1, Pallas kernels, side_steps(): pl.pallas_call(functools.partial(strips_kernel, layers=layers, width=rows...  1.91 us
    ppermute x1, waiting for transfers between devices, swap_x(): lax.ppermute(first, 'gx', pairs(count, 0))  1.9 us
    ppermute x1, starting transfers between devices, swap_y(): lax.ppermute(second, Y, odd)  1.77 us
  transfers between devices with their start and end apart: 7, of which 4 were waited for; matrix products, arithmetic and copies ran while one was open for 0% of the time, Pallas kernels for 19%

profile of v8, /device:TPU:0, one launch (start us, length us, event | category | flops | bytes accessed | tf_op | source)
XLA Modules:
  0.0 28.8 jit_solution(16432039150286975672)
XLA Ops:
  0.0 1.5 %send_rows.1 = (f32[768,128]{1,0:T(8,128)S(1)}, f32[256,128]{1,0:T(8,128)S(1)}, f32[256,128]{1,0:T(8,128)S(1)}, f32[512,128]{1,0:T(8,128)S(1)}, s32[512,128]{1,0...) custom-call(f32[768,128]{1,0:T(8,128)} %bitcast.7, f32[256,128]{1,0:T(8,128)} %bitcast.10, ...), custom_call_target="tpu_custom_call" | custom-call | tf_op jit(solution)/shard_map/send_rows/pallas_call | solution.py:212
  1.5 3.1 %collective-permute-start = (f32[4,7,16,128]{3,2,1,0:T(8,128)S(1)}, f32[4,7,16,128]{3,2,1,0:T(8,128)S(1)}, u32[]{:S(2)}, u32[]{:S(2)}) collective-permute-start(f32[4,7,16,128]{3,2,1,0:T(8,128)S(1)} %get-tuple-element.44), channel_id=1, source_target_pairs={{0,4},{4,0},{8,12},{12,8},{1,5},{5,1},{9,13},{13,9},{2,6},{6,2},{1... | collective-permute-start | bytes 688136 | tf_op jit(solution)/shard_map/ppermute | solution.py:740
  4.6 0.0 collective-permute-start.1
  4.6 3.7 %cone_steps.1 = (f32[16,12,16,128]{3,2,1,0:T(8,128)S(1)}, f32[4,16,3,16,128]{4,3,2,1,0:T(8,128)S(1)}, f32[4,16,3,16,128]{4,3,2,1,0:T(8,128)S(1)}, f32[4,16,3,16,...) custom-call(f32[3]{0:T(128)} %retard_hbm.1, ...), custom_call_target="tpu_custom_call" | custom-call | flops 10000000 | bytes 10000000 | tf_op jit(solution)/shard_map/cone_steps/pallas_call | solution.py:338
  8.3 1.9 %collective-permute-done.xa_ref = f32[4,7,16,128]{3,2,1,0:T(8,128)S(1)} collective-permute-done((f32[4,7,16,128]{3,2,1,0:T(8,128)S(1)}, f32[4,7,16,128]{3,2,1,0:T(8,128)S(1)}, u32[]{:S(2)}, u32[]{:S(2)}) %collective-permute-start) | collective-permute-done | bytes 229408 | tf_op jit(solution)/shard_map/ppermute | solution.py:740
  10.2 0.0 collective-permute-done.1.xb_ref
  10.2 0.3 edge_columns.1
  10.5 0.1 collective-permute-start.2
  10.5 1.8 %collective-permute-start.3 = (f32[12,16,128]{2,1,0:T(8,128)S(1)}, f32[12,16,128]{2,1,0:T(8,128)S(1)}, u32[]{:S(2)}, u32[]{:S(2)}) collective-permute-start(f32[12,16,128]{2,1,0:T(8,128)S(1)} %get-tuple-element.56), channel_id=1, source_target_pairs={{1,2},{2,1},{0,3},{3,0},{5,6},{6,5},{4,7},{7,4},{9,10},{10,9},{8,1... | collective-permute-start | bytes 294920 | tf_op jit(solution)/shard_map/ppermute | solution.py:746
  12.3 0.0 copy-start
  12.3 1.7 %rim_steps.1 = (f32[3,384]{1,0:T(4,128)S(1)}, f32[10,12,16,128]{3,2,1,0:T(8,128)S(1)}, f32[4,8,3,16,128]{4,3,2,1,0:T(8,128)S(1)}, f32[4,8,3,16,128]{4,3,2,1,0:T(8,128)S(1)}) custom-call(f32[8,128]{1,0:T(8,128)S(1)} %get-tuple-element.40.rate_ref, f32[4,7,16,128]{3,2,1,0:T(8,128)S(1)} %collective-permute-done.xa_ref, ...), custom_call_target="tpu_custom_call" | custom-call | flops 10000000 | bytes 10000000 | tf_op jit(solution)/shard_map/rim_steps/pallas_call | solution.py:483
  14.0 0.0 collective-permute-done.2.ea_ref
  14.0 1.1 %collective-permute-done.3.eb_ref = f32[12,16,128]{2,1,0:T(8,128)S(1)} collective-permute-done((f32[12,16,128]{2,1,0:T(8,128)S(1)}, f32[12,16,128]{2,1,0:T(8,128)S(1)}, u32[]{:S(2)}, u32[]{:S(2)}) %collective-permute-start.3) | collective-permute-done | bytes 98336 | tf_op jit(solution)/shard_map/ppermute | solution.py:746
  15.1 1.9 %strip_steps.1 = (f32[3,384]{1,0:T(4,128)S(1)}, f32[24,12,16,128]{3,2,1,0:T(8,128)S(1)}, f32[4,24,16,128]{3,2,1,0:T(8,128)S(1)}, f32[4,24,16,128]{3,2,1,0:T(8,128)S(1)}) custom-call(f32[8,128]{1,0:T(8,128)S(1)} %get-tuple-element.40.rate_ref, f32[24,16,128]{2,1,0:T(8,128)S(1)} %get-tuple-element.54.e_ref, f32[12,16,128]{2,1,0:T(8,128)S(1)} %collective-permute-done.2.ea_ref, ...), custom_call_target="tpu_custom_call" | custom-call | tf_op jit(solution)/shard_map/strip_steps/pallas_call | solution.py:567
  17.0 3.9 %collective-permute-start.6 = (f32[3,384]{1,0:T(4,128)S(1)}, f32[3,384]{1,0:T(4,128)S(1)}, u32[]{:S(2)}, u32[]{:S(2)}) collective-permute-start(f32[3,384]{1,0:T(4,128)S(1)} %get-tuple-element.64.partial_ref), channel_id=1, source_target_pairs={{0,12},{4,8},{8,4},{12,0},{1,13},{5,9},{9,5},{13,1},{2,14},{6,10},... | collective-permute-start | bytes 13832 | tf_op jit(solution)/shard_map/ppermute | solution.py:752
  20.9 0.6 %collective-permute-start.5 = (f32[3,384]{1,0:T(4,128)S(1)}, f32[3,384]{1,0:T(4,128)S(1)}, u32[]{:S(2)}, u32[]{:S(2)}) collective-permute-start(f32[3,384]{1,0:T(4,128)S(1)} %get-tuple-element.64.partial_ref), channel_id=1, source_target_pairs={{0,8},{4,12},{8,0},{12,4},{1,9},{5,13},{9,1},{13,5},{2,10},{6,14},... | collective-permute-start | bytes 13832 | tf_op jit(solution)/shard_map/ppermute | solution.py:752
  21.4 0.3 collective-permute-start.4
  21.7 0.8 %collective-permute-done.6.rest_2_ = f32[3,384]{1,0:T(4,128)S(1)} collective-permute-done((f32[3,384]{1,0:T(4,128)S(1)}, f32[3,384]{1,0:T(4,128)S(1)}, u32[]{:S(2)}, u32[]{:S(2)}) %collective-permute-start.6) | collective-permute-done | bytes 4640 | tf_op jit(solution)/shard_map/ppermute | solution.py:752
  22.5 2.9 %collective-permute-done.5.rest_1_ = f32[3,384]{1,0:T(4,128)S(1)} collective-permute-done((f32[3,384]{1,0:T(4,128)S(1)}, f32[3,384]{1,0:T(4,128)S(1)}, u32[]{:S(2)}, u32[]{:S(2)}) %collective-permute-start.5) | collective-permute-done | bytes 4640 | tf_op jit(solution)/shard_map/ppermute | solution.py:752
  25.4 0.0 collective-permute-done.4.rest_0_
  25.4 0.0 copy-done
  25.4 3.4 %adjoint_steps.1 = f32[256,128]{1,0:T(8,128)} custom-call(f32[8,128]{1,0:T(8,128)S(1)} %get-tuple-element.40.rate_ref, f32[3,384]{1,0:T(4,128)S(1)} %copy-done, s32[8,384]{1,0:T(8,128)S(1)} %get-tuple-element.41.meta_ref, bf16[384,384]{1,0:T(8,128)(2,1)S(1)} %get-tuple-element.42.mask_ref, f32[16,12,16,128]{3,2,1,0:T(8,128)S(1)} %get-tuple-element.43.coef_in, ...), custom_call_target="tpu_custom_call" | custom-call | tf_op jit(solution)/shard_map/adjoint_steps/pallas_call | solution.py:717
Async XLA Ops:
  1.5 8.7 %collective-permute-start = (f32[4,7,16,128]{3,2,1,0:T(8,128)S(1)}, f32[4,7,16,128]{3,2,1,0:T(8,128)S(1)}, u32[]{:S(2)}, u32[]{:S(2)}) collective-permute-start(f32[4,7,16,128]{3,2,1,0:T(8,128)S(1)} %get-tuple-element.44), channel_id=1, source_target_pairs={{0,4},{4,0},{8,12},{12,8},{1,5},{5,1},{9,13},{13,9},{2,6},{6,2},{1... | collective-permute-start | bytes 688136 | tf_op jit(solution)/shard_map/ppermute | solution.py:740
  4.6 5.6 %collective-permute-start.1 = (f32[4,7,16,128]{3,2,1,0:T(8,128)S(1)}, f32[4,7,16,128]{3,2,1,0:T(8,128)S(1)}, u32[]{:S(2)}, u32[]{:S(2)}) collective-permute-start(f32[4,7,16,128]{3,2,1,0:T(8,128)S(1)} %get-tuple-element.45), channel_id=1, source_target_pairs={{0,1},{1,0},{2,3},{3,2},{4,8},{5,9},{6,10},{7,11},{8,4},{9,5},{10,... | collective-permute-start | bytes 688136 | tf_op jit(solution)/shard_map/ppermute | solution.py:740
  10.5 3.6 %collective-permute-start.2 = (f32[12,16,128]{2,1,0:T(8,128)S(1)}, f32[12,16,128]{2,1,0:T(8,128)S(1)}, u32[]{:S(2)}, u32[]{:S(2)}) collective-permute-start(f32[12,16,128]{2,1,0:T(8,128)S(1)} %get-tuple-element.55), channel_id=1, source_target_pairs={{0,1},{1,0},{2,3},{3,2},{4,5},{5,4},{6,7},{7,6},{8,9},{9,8},{10,11... | collective-permute-start | bytes 294920 | tf_op jit(solution)/shard_map/ppermute | solution.py:746
  10.5 4.6 %collective-permute-start.3 = (f32[12,16,128]{2,1,0:T(8,128)S(1)}, f32[12,16,128]{2,1,0:T(8,128)S(1)}, u32[]{:S(2)}, u32[]{:S(2)}) collective-permute-start(f32[12,16,128]{2,1,0:T(8,128)S(1)} %get-tuple-element.56), channel_id=1, source_target_pairs={{1,2},{2,1},{0,3},{3,0},{5,6},{6,5},{4,7},{7,4},{9,10},{10,9},{8,1... | collective-permute-start | bytes 294920 | tf_op jit(solution)/shard_map/ppermute | solution.py:746
  12.3 13.1 %copy-start = (f32[3,384]{1,0:T(4,128)S(1)}, f32[3,384]{1,0:T(4,128)}, u32[]{:S(2)}) copy-start(f32[3,384]{1,0:T(4,128)} %weight_ref.1) | copy-start | bytes 13828
  17.0 5.5 %collective-permute-start.6 = (f32[3,384]{1,0:T(4,128)S(1)}, f32[3,384]{1,0:T(4,128)S(1)}, u32[]{:S(2)}, u32[]{:S(2)}) collective-permute-start(f32[3,384]{1,0:T(4,128)S(1)} %get-tuple-element.64.partial_ref), channel_id=1, source_target_pairs={{0,12},{4,8},{8,4},{12,0},{1,13},{5,9},{9,5},{13,1},{2,14},{6,10},... | collective-permute-start | bytes 13832 | tf_op jit(solution)/shard_map/ppermute | solution.py:752
  20.9 4.5 %collective-permute-start.5 = (f32[3,384]{1,0:T(4,128)S(1)}, f32[3,384]{1,0:T(4,128)S(1)}, u32[]{:S(2)}, u32[]{:S(2)}) collective-permute-start(f32[3,384]{1,0:T(4,128)S(1)} %get-tuple-element.64.partial_ref), channel_id=1, source_target_pairs={{0,8},{4,12},{8,0},{12,4},{1,9},{5,13},{9,1},{13,5},{2,10},{6,14},... | collective-permute-start | bytes 13832 | tf_op jit(solution)/shard_map/ppermute | solution.py:752
  21.4 4.0 %collective-permute-start.4 = (f32[3,384]{1,0:T(4,128)S(1)}, f32[3,384]{1,0:T(4,128)S(1)}, u32[]{:S(2)}, u32[]{:S(2)}) collective-permute-start(f32[3,384]{1,0:T(4,128)S(1)} %get-tuple-element.64.partial_ref), channel_id=1, source_target_pairs={{0,4},{4,0},{8,12},{12,8},{1,5},{5,1},{9,13},{13,9},{2,6},{6,2},{1... | collective-permute-start | bytes 13832 | tf_op jit(solution)/shard_map/ppermute | solution.py:752

commit v9 on v8

--- a/solution.py
+++ b/solution.py
@@ -101,19 +101,24 @@
     return refs[which][index, kind]
 
 
-def row_fields(raw, x, layers, width, species):
+def row_fields(raw, x, layers, width, species, wanted=None):
     initial_ref, logk_ref, direction_ref, speed_ref, flags_ref = raw
     plane = layers * width
 
     def take(ref, index):
         return ref[pl.ds(index * plane + x, layers, stride=width), :]
 
-    fields = [take(initial_ref, s) for s in range(species)]
-    conductance = jnp.exp(take(logk_ref, 0))
-    fields += [conductance, conductance * take(direction_ref, 0)]
-    for axis in range(2):
-        speed = take(speed_ref, axis)
-        fields.append(jnp.where(take(flags_ref, axis) == 1, speed, -speed))
+    fields = []
+    for f in range(species + 4) if wanted is None else wanted:
+        if f < species:
+            fields.append(take(initial_ref, f))
+        elif f == species:
+            fields.append(jnp.exp(take(logk_ref, 0)))
+        elif f == species + 1:
+            fields.append(jnp.exp(take(logk_ref, 0)) * take(direction_ref, 0))
+        else:
+            speed = take(speed_ref, f - species - 2)
+            fields.append(jnp.where(take(flags_ref, f - species - 2) == 1, speed, -speed))
     return fields
 
 
@@ -135,7 +140,7 @@
     return (p, q, b) if mask is None else (p * mask, q * mask, b * mask)
 
 
-def step_cell(r, m, s, rate, coef, state, tangent, put_c, put_t, put_jy):
+def step_cell(r, m, s, rate, coef, state, tangent, put_c, put_t, put_jy, put_jx):
     kept = rate - coef(D, r)
     upper, lower = coef(QX, r), coef(PX, r - 1)
     after, before = coef(QY, r), coef(PYM, r)
@@ -145,11 +150,12 @@
 
     c, up, down = state(r, s), state(r + 1, s), state(r - 1, s)
     yp, ym = y_next(c), y_previous(c)
-    jump = yp - c
+    jump, jump_x = yp - c, up - c
     source = (
-        coef(BX, r) * (up - c) - coef(BX, r - 1) * (c - down) + coef(BY, r) * jump - coef(BYM, r) * (c - ym)
+        coef(BX, r) * jump_x - coef(BX, r - 1) * (c - down) + coef(BY, r) * jump - coef(BYM, r) * (c - ym)
     )
     put_jy(s, jump)
+    put_jx(s, jump_x)
     if m + 1 < STEPS:
         put_c(s, moved(c, up, down, yp, ym))
     if m > 0:
@@ -192,17 +198,19 @@
 def send_kernel(*refs, layers, width, species):
     sources, raw, (xa_ref, xb_ref, sem) = refs[:5], refs[5:10], refs[10:]
     copies = [pltpu.make_async_copy(a, b, sem.at[i]) for i, (a, b) in enumerate(zip(sources, raw))]
-    for copy in copies:
+    order = copies[1:] + copies[:1]
+    for copy in order:
         copy.start()
-    for copy in copies:
-        copy.wait()
     even = lax.rem(lax.axis_index("gx"), 2) == 0
-    for r in range(HALO):
-        bottom = row_fields(raw, r, layers, width, species)
-        top = row_fields(raw, width - HALO + r, layers, width, species)
-        for f in range(species + 4):
-            xa_ref[r, f] = jnp.where(even, top[f], bottom[f])
-            xb_ref[r, f] = jnp.where(even, bottom[f], top[f])
+    for waits, fields in ((order[:2], (species, species + 1)), (order[2:4], (species + 2, species + 3)), (order[4:], range(species))):
+        for copy in waits:
+            copy.wait()
+        for r in range(HALO):
+            bottom = row_fields(raw, r, layers, width, species, fields)
+            top = row_fields(raw, width - HALO + r, layers, width, species, fields)
+            for f, low, high in zip(fields, bottom, top):
+                xa_ref[r, f] = jnp.where(even, high, low)
+                xb_ref[r, f] = jnp.where(even, low, high)
 
 
 def send_rows(initial, logk, direction, face_speed, face_flags):
@@ -244,7 +252,7 @@
 
 def cone_kernel(
     retard_hbm, decay_hbm, cells_hbm, count_hbm, initial_ref, logk_ref, direction_ref, speed_ref, flags_ref,
-    coef_ref, c_ref, t_ref, jy_ref, e_ref, mask_ref, hot_ref, side_hot_ref, spread_ref, patch_ref, rate_ref, meta_ref,
+    coef_ref, c_ref, t_ref, jy_ref, jx_ref, e_ref, mask_ref, hot_ref, side_hot_ref, spread_ref, patch_ref, rate_ref, meta_ref,
     retard_ref, decay_ref, cells_ref, count_ref, sem, *, layers, width, species,
 ):
     copies = [
@@ -296,7 +304,7 @@
         tangent = once(lambda r, s: t_ref[m - 1, r - HALO, s])
         for r in range(HALO + 1 + m, HALO + width - 1 - m):
             x = r - HALO
-            puts = put_at(c_ref, m + 1, x), put_at(t_ref, m, x), put_at(jy_ref, m, x)
+            puts = put_at(c_ref, m + 1, x), put_at(t_ref, m, x), put_at(jy_ref, m, x), put_at(jx_ref, m, x)
             for s in range(species):
                 step_cell(r, m, s, rates[s], coef, state, tangent, *puts)
 
@@ -342,6 +350,7 @@
             state,
             state,
             state,
+            state,
             jax.ShapeDtypeStruct((width, layers, LANES), F32),
             jax.ShapeDtypeStruct(((width + 2 * HALO) * layers, wells), BF16),
             jax.ShapeDtypeStruct((LANES, wells), BF16),
@@ -352,7 +361,7 @@
             jax.ShapeDtypeStruct((TILE, wells), I32),
         ),
         in_specs=[HBM] * 4 + [VMEM] * 5,
-        out_specs=[VMEM] * 12,
+        out_specs=[VMEM] * 13,
         scratch_shapes=[
             pltpu.SMEM(retard.shape, F32),
             pltpu.SMEM(decay.shape, F32),
@@ -418,7 +427,7 @@
 
 def rim_kernel(
     rate_ref, xa_ref, xb_ref, coef_in, c_in, t_in, mask_ref, hot_ref,
-    partial_ref, coef_out, c_out, jy_out, t_out, *, layers, width, species,
+    partial_ref, coef_out, c_out, jy_out, jx_out, t_out, *, layers, width, species,
 ):
     gx = lax.axis_index("gx")
     rows = width + 2 * HALO
@@ -461,7 +470,7 @@
         tangent = once(lambda r, s: tangent_row(t_in, t_out, m, width, r)[s])
         for r in list(range(1 + m, HALO + 1 + m)) + list(range(last - m, rows - 1 - m)):
             index = state_row(m + 1, width)(r)[1]
-            puts = put_at(c_out, m + 1, index), put_at(t_out, m, index), put_at(jy_out, m, index)
+            puts = [put_at(ref, n, index) for ref, n in ((c_out, m + 1), (t_out, m), (jy_out, m), (jx_out, m))]
             for s in range(species):
                 step_cell(r, m, s, rate_ref[s : s + 1, :], coef, state, tangent, *puts)
 
@@ -487,9 +496,10 @@
             jax.ShapeDtypeStruct((2 * HALO + 2, KINDS, layers, LANES), F32),
             jax.ShapeDtypeStruct(state, F32),
             jax.ShapeDtypeStruct(state, F32),
+            jax.ShapeDtypeStruct(state, F32),
         ),
         in_specs=[VMEM] * 8,
-        out_specs=[VMEM] * 4,
+        out_specs=[VMEM] * 5,
         scratch_shapes=[pltpu.VMEM(state, F32)],
         compiler_params=pltpu.CompilerParams(vmem_limit_bytes=6 * MIB),
         cost_estimate=pl.CostEstimate(flops=10**7, bytes_accessed=10**7, transcendentals=0),
@@ -499,7 +509,7 @@
 
 def strips_kernel(
     rate_ref, e_ref, ea_ref, eb_ref, partial_in, mask_ref, hot_ref, spread_ref,
-    partial_ref, coef_ref, c_ref, jy_ref, t_ref, *, layers, width, species,
+    partial_ref, coef_ref, c_ref, jy_ref, jx_ref, t_ref, *, layers, width, species,
 ):
     shape = (layers, LANES)
     rows = width + 2 * HALO
@@ -552,7 +562,8 @@
         state = once(lambda r, s: c_ref[m, r])
         tangent = once(lambda r, s: t_ref[m - 1, r])
         for r in range(1 + m, rows - 1 - m):
-            step_cell(r, m, 0, rate, coef, state, tangent, put(c_ref, m + 1, r), put(t_ref, m, r), put(jy_ref, m, r))
+            puts = put(c_ref, m + 1, r), put(t_ref, m, r), put(jy_ref, m, r), put(jx_ref, m, r)
+            step_cell(r, m, 0, rate, coef, state, tangent, *puts)
 
     masks = mask_ref[HALO * layers : (HALO + width) * layers, :]
     block = jnp.concatenate([t_ref[STEPS - 1, r] for r in range(HALO, HALO + width)], axis=0)
@@ -571,9 +582,10 @@
             jax.ShapeDtypeStruct((rows, KINDS, layers, LANES), F32),
             jax.ShapeDtypeStruct(state, F32),
             jax.ShapeDtypeStruct(state, F32),
+            jax.ShapeDtypeStruct(state, F32),
         ),
         in_specs=[VMEM] * 8,
-        out_specs=[VMEM] * 4,
+        out_specs=[VMEM] * 5,
         scratch_shapes=[pltpu.VMEM(state, F32)],
         compiler_params=pltpu.CompilerParams(vmem_limit_bytes=6 * MIB),
         name="strip_steps",
@@ -581,8 +593,8 @@
 
 
 def adjoint_kernel(
-    rate_ref, weight_ref, meta_ref, mask_ref, coef_in, coef_out, c_in, c_out, jy_in, jy_out,
-    coef_side, c_side, jy_side, patch_ref, partial_ref, *rest, layers, width, species, parts,
+    rate_ref, weight_ref, meta_ref, mask_ref, coef_in, coef_out, c_in, c_out, jy_in, jy_out, jx_in, jx_out,
+    coef_side, c_side, jy_side, jx_side, patch_ref, partial_ref, *rest, layers, width, species, parts,
 ):
     others, out_ref, lam_ref = rest[:parts], *rest[parts:]
     rows = width + 2 * HALO
@@ -649,13 +661,14 @@
                 value, up = lam_row(r, s), lam_row(r + 1, s)
                 after = y_next(value)
                 if sense:
-                    add(("x", is_side, r), (state(r + 1, s) - state(r, s)) * (up - value))
+                    which, index = state_row(m + 1, width)(r)
+                    if r <= m:
+                        jump = state(r + 1, s) - state(r, s)
+                    else:
+                        jump = jx_side[m, r] if is_side else (jx_in, jx_out)[which][m, index, s]
+                    add(("x", is_side, r), jump * (up - value))
                     if r >= HALO:
-                        if is_side:
-                            jump = jy_side[m, r]
-                        else:
-                            which, index = state_row(m + 1, width)(r)
-                            jump = (jy_in, jy_out)[which][m, index, s]
+                        jump = jy_side[m, r] if is_side else (jy_in, jy_out)[which][m, index, s]
                         add(("y", is_side, r), jump * (after - value))
                 if retreat:
                     results.append(
@@ -710,10 +723,10 @@
 
 
 def adjoint(rates, weight, meta, mask, inner, outer, side, patch, partials):
-    (coef_in, c_in, jy_in), (coef_out, c_out, jy_out) = inner, outer
+    (coef_in, c_in, jy_in, jx_in), (coef_out, c_out, jy_out, jx_out) = inner, outer
     _, width, species, layers, _ = c_in.shape
     parts = len(partials) - 1
-    operands = (rates, weight, meta, mask, coef_in, coef_out, c_in, c_out, jy_in, jy_out, *side, patch, *partials)
+    operands = (rates, weight, meta, mask, coef_in, coef_out, c_in, c_out, jy_in, jy_out, jx_in, jx_out, *side, patch, *partials)
     return pl.pallas_call(
         functools.partial(adjoint_kernel, layers=layers, width=width, species=species, parts=parts),
         out_shape=jax.ShapeDtypeStruct((layers * width, LANES), F32),
@@ -763,16 +776,16 @@
     species, layers, width, columns = initial.shape
     raw, xa, xb = send_rows(initial, logk, direction, face_speed, face_flags)
     xa, xb = swap_x(xa, xb)
-    coef_in, c_in, t_in, jy_in, e, mask, hot, side_hot, spread, patch, rates, meta = cone(
+    coef_in, c_in, t_in, jy_in, jx_in, e, mask, hot, side_hot, spread, patch, rates, meta = cone(
         retard, decay, screen_cells.T, screen_count, raw, layers, width, species
     )
     e, ea, eb = all_edges(e, xa, xb)
     ea, eb = swap_y(ea, eb)
-    partial, coef_out, c_out, jy_out = rim(rates, xa, xb, coef_in, c_in, t_in, mask, hot)
+    partial, coef_out, c_out, jy_out, jx_out = rim(rates, xa, xb, coef_in, c_in, t_in, mask, hot)
     partial, *side = side_steps(rates, e, ea, eb, partial, mask, side_hot, spread)
     reach = -(-(screen_cells.shape[1] - 1 + HALO) // width)
     partials = [partial] + from_others(partial, "gx", reach)
-    inner, outer = (coef_in, c_in, jy_in), (coef_out, c_out, jy_out)
+    inner, outer = (coef_in, c_in, jy_in, jx_in), (coef_out, c_out, jy_out, jx_out)
     hessian = adjoint(rates, well_weight, meta, mask, inner, outer, side, patch, partials)
     return hessian.reshape(layers, width, columns)
 

time: 29 us -> 28.8 us (level)
  no operation moved by 1% of the time
where the time goes in v9:
time: 28.8 us; the launch traced here: 28.7 us
  Pallas kernels  12.3 us (43%)
  starting transfers between devices  9.58 us (33%)
  waiting for transfers between devices  6.69 us (23%)
    ppermute x3, starting transfers between devices, from_others(): lax.ppermute(value, axis, [(i, i ^ d) for i in range(count)])  4.67 us
    ppermute x3, waiting for transfers between devices, from_others(): lax.ppermute(value, axis, [(i, i ^ d) for i in range(count)])  3.71 us
    pallas_call x1, Pallas kernels, cone(): pl.pallas_call(functools.partial(cone_kernel, layers=layers, width=width,...  3.7 us
    pallas_call x1, Pallas kernels, adjoint(): pl.pallas_call(functools.partial(adjoint_kernel, layers=layers, width=wid...  3.33 us
    ppermute x1, starting transfers between devices, swap_x(): lax.ppermute(first, 'gx', pairs(count, 0))  3.09 us
    pallas_call x1, Pallas kernels, side_steps(): pl.pallas_call(functools.partial(strips_kernel, layers=layers, width=rows...  1.92 us
    ppermute x1, waiting for transfers between devices, swap_x(): lax.ppermute(first, 'gx', pairs(count, 0))  1.89 us
    ppermute x1, starting transfers between devices, swap_y(): lax.ppermute(second, Y, odd)  1.77 us
  transfers between devices with their start and end apart: 7, of which 4 were waited for; matrix products, arithmetic and copies ran while one was open for 0% of the time, Pallas kernels for 19%

profile of v9, /device:TPU:0, one launch (start us, length us, event | category | flops | bytes accessed | tf_op | source)
XLA Modules:
  0.0 28.7 jit_solution(16829440913445263449)
XLA Ops:
  0.0 1.4 %send_rows.1 = (f32[768,128]{1,0:T(8,128)S(1)}, f32[256,128]{1,0:T(8,128)S(1)}, f32[256,128]{1,0:T(8,128)S(1)}, f32[512,128]{1,0:T(8,128)S(1)}, s32[512,128]{1,0...) custom-call(f32[768,128]{1,0:T(8,128)} %bitcast.7, f32[256,128]{1,0:T(8,128)} %bitcast.10, ...), custom_call_target="tpu_custom_call" | custom-call | tf_op jit(solution)/shard_map/send_rows/pallas_call | solution.py:220
  1.4 3.1 %collective-permute-start = (f32[4,7,16,128]{3,2,1,0:T(8,128)S(1)}, f32[4,7,16,128]{3,2,1,0:T(8,128)S(1)}, u32[]{:S(2)}, u32[]{:S(2)}) collective-permute-start(f32[4,7,16,128]{3,2,1,0:T(8,128)S(1)} %get-tuple-element.47), channel_id=1, source_target_pairs={{0,4},{4,0},{8,12},{12,8},{1,5},{5,1},{9,13},{13,9},{2,6},{6,2},{1... | collective-permute-start | bytes 688136 | tf_op jit(solution)/shard_map/ppermute | solution.py:753
  4.5 0.0 collective-permute-start.1
  4.5 3.7 %cone_steps.1 = (f32[16,12,16,128]{3,2,1,0:T(8,128)S(1)}, f32[4,16,3,16,128]{4,3,2,1,0:T(8,128)S(1)}, f32[4,16,3,16,128]{4,3,2,1,0:T(8,128)S(1)}, f32[4,16,3,16,...) custom-call(f32[3]{0:T(128)} %retard_hbm.1, ...), custom_call_target="tpu_custom_call" | custom-call | flops 10000000 | bytes 10000000 | tf_op jit(solution)/shard_map/cone_steps/pallas_call | solution.py:346
  8.2 1.9 %collective-permute-done.xa_ref = f32[4,7,16,128]{3,2,1,0:T(8,128)S(1)} collective-permute-done((f32[4,7,16,128]{3,2,1,0:T(8,128)S(1)}, f32[4,7,16,128]{3,2,1,0:T(8,128)S(1)}, u32[]{:S(2)}, u32[]{:S(2)}) %collective-permute-start) | collective-permute-done | bytes 229408 | tf_op jit(solution)/shard_map/ppermute | solution.py:753
  10.1 0.0 collective-permute-done.1.xb_ref
  10.1 0.3 edge_columns.1
  10.4 0.1 collective-permute-start.2
  10.4 1.8 %collective-permute-start.3 = (f32[12,16,128]{2,1,0:T(8,128)S(1)}, f32[12,16,128]{2,1,0:T(8,128)S(1)}, u32[]{:S(2)}, u32[]{:S(2)}) collective-permute-start(f32[12,16,128]{2,1,0:T(8,128)S(1)} %get-tuple-element.61), channel_id=1, source_target_pairs={{1,2},{2,1},{0,3},{3,0},{5,6},{6,5},{4,7},{7,4},{9,10},{10,9},{8,1... | collective-permute-start | bytes 294920 | tf_op jit(solution)/shard_map/ppermute | solution.py:759
  12.2 0.0 copy-start
  12.2 1.7 %rim_steps.1 = (f32[3,384]{1,0:T(4,128)S(1)}, f32[10,12,16,128]{3,2,1,0:T(8,128)S(1)}, f32[4,8,3,16,128]{4,3,2,1,0:T(8,128)S(1)}, f32[4,8,3,16,128]{4,3,2,1,0:T(8,128)S(1)}, f32[4,8,3,16,128]{4,3,2,1,0:T(8,128)S(1)}) custom-call(f32[8,128]{1,0:T(8,128)S(1)} %get-tuple-element.43.rate_ref, f32[4,7,16,128]{3,2,1,0:T(8,128)S(1)} %collective-permute-done.xa_ref, ...), custom_call_target="tpu_custom_call" | custom-call | flops 10000000 | bytes 10000000 | tf_op jit(solution)/shard_map/rim_steps/pallas_call | solution.py:492
  13.9 0.0 collective-permute-done.2.ea_ref
  13.9 1.1 %collective-permute-done.3.eb_ref = f32[12,16,128]{2,1,0:T(8,128)S(1)} collective-permute-done((f32[12,16,128]{2,1,0:T(8,128)S(1)}, f32[12,16,128]{2,1,0:T(8,128)S(1)}, u32[]{:S(2)}, u32[]{:S(2)}) %collective-permute-start.3) | collective-permute-done | bytes 98336 | tf_op jit(solution)/shard_map/ppermute | solution.py:759
  15.0 1.9 %strip_steps.1 = (f32[3,384]{1,0:T(4,128)S(1)}, f32[24,12,16,128]{3,2,1,0:T(8,128)S(1)}, f32[4,24,16,128]{3,2,1,0:T(8,128)S(1)}, f32[4,24,16,128]{3,2,1,0:T(8,128)S(1)}, f32[4,24,16,128]{3,2,1,0:T(8,128)S(1)}) custom-call(f32[8,128]{1,0:T(8,128)S(1)} %get-tuple-element.43.rate_ref, f32[24,16,128]{2,1,0:T(8,128)S(1)} %get-tuple-element.59.e_ref, ...), custom_call_target="tpu_custom_call" | custom-call | tf_op jit(solution)/shard_map/strip_steps/pallas_call | solution.py:578
  16.9 3.8 %collective-permute-start.6 = (f32[3,384]{1,0:T(4,128)S(1)}, f32[3,384]{1,0:T(4,128)S(1)}, u32[]{:S(2)}, u32[]{:S(2)}) collective-permute-start(f32[3,384]{1,0:T(4,128)S(1)} %get-tuple-element.70.partial_ref), channel_id=1, source_target_pairs={{0,12},{4,8},{8,4},{12,0},{1,13},{5,9},{9,5},{13,1},{2,14},{6,10},... | collective-permute-start | bytes 13832 | tf_op jit(solution)/shard_map/ppermute | solution.py:765
  20.8 0.6 %collective-permute-start.5 = (f32[3,384]{1,0:T(4,128)S(1)}, f32[3,384]{1,0:T(4,128)S(1)}, u32[]{:S(2)}, u32[]{:S(2)}) collective-permute-start(f32[3,384]{1,0:T(4,128)S(1)} %get-tuple-element.70.partial_ref), channel_id=1, source_target_pairs={{0,8},{4,12},{8,0},{12,4},{1,9},{5,13},{9,1},{13,5},{2,10},{6,14},... | collective-permute-start | bytes 13832 | tf_op jit(solution)/shard_map/ppermute | solution.py:765
  21.4 0.3 collective-permute-start.4
  21.6 0.8 %collective-permute-done.6.rest_2_ = f32[3,384]{1,0:T(4,128)S(1)} collective-permute-done((f32[3,384]{1,0:T(4,128)S(1)}, f32[3,384]{1,0:T(4,128)S(1)}, u32[]{:S(2)}, u32[]{:S(2)}) %collective-permute-start.6) | collective-permute-done | bytes 4640 | tf_op jit(solution)/shard_map/ppermute | solution.py:765
  22.5 2.9 %collective-permute-done.5.rest_1_ = f32[3,384]{1,0:T(4,128)S(1)} collective-permute-done((f32[3,384]{1,0:T(4,128)S(1)}, f32[3,384]{1,0:T(4,128)S(1)}, u32[]{:S(2)}, u32[]{:S(2)}) %collective-permute-start.5) | collective-permute-done | bytes 4640 | tf_op jit(solution)/shard_map/ppermute | solution.py:765
  25.3 0.0 collective-permute-done.4.rest_0_
  25.3 0.0 copy-done
  25.3 3.3 %adjoint_steps.1 = f32[256,128]{1,0:T(8,128)} custom-call(f32[8,128]{1,0:T(8,128)S(1)} %get-tuple-element.43.rate_ref, f32[3,384]{1,0:T(4,128)S(1)} %copy-done, s32[8,384]{1,0:T(8,128)S(1)} %get-tuple-element.44.meta_ref, bf16[384,384]{1,0:T(8,128)(2,1)S(1)} %get-tuple-element.45.mask_ref, f32[16,12,16,128]{3,2,1,0:T(8,128)S(1)} %get-tuple-element.46.coef_in, ...), custom_call_target="tpu_custom_call" | custom-call | tf_op jit(solution)/shard_map/adjoint_steps/pallas_call | solution.py:730
Async XLA Ops:
  1.4 8.7 %collective-permute-start = (f32[4,7,16,128]{3,2,1,0:T(8,128)S(1)}, f32[4,7,16,128]{3,2,1,0:T(8,128)S(1)}, u32[]{:S(2)}, u32[]{:S(2)}) collective-permute-start(f32[4,7,16,128]{3,2,1,0:T(8,128)S(1)} %get-tuple-element.47), channel_id=1, source_target_pairs={{0,4},{4,0},{8,12},{12,8},{1,5},{5,1},{9,13},{13,9},{2,6},{6,2},{1... | collective-permute-start | bytes 688136 | tf_op jit(solution)/shard_map/ppermute | solution.py:753
  4.5 5.6 %collective-permute-start.1 = (f32[4,7,16,128]{3,2,1,0:T(8,128)S(1)}, f32[4,7,16,128]{3,2,1,0:T(8,128)S(1)}, u32[]{:S(2)}, u32[]{:S(2)}) collective-permute-start(f32[4,7,16,128]{3,2,1,0:T(8,128)S(1)} %get-tuple-element.48), channel_id=1, source_target_pairs={{0,1},{1,0},{2,3},{3,2},{4,8},{5,9},{6,10},{7,11},{8,4},{9,5},{10,... | collective-permute-start | bytes 688136 | tf_op jit(solution)/shard_map/ppermute | solution.py:753
  10.4 3.6 %collective-permute-start.2 = (f32[12,16,128]{2,1,0:T(8,128)S(1)}, f32[12,16,128]{2,1,0:T(8,128)S(1)}, u32[]{:S(2)}, u32[]{:S(2)}) collective-permute-start(f32[12,16,128]{2,1,0:T(8,128)S(1)} %get-tuple-element.60), channel_id=1, source_target_pairs={{0,1},{1,0},{2,3},{3,2},{4,5},{5,4},{6,7},{7,6},{8,9},{9,8},{10,11... | collective-permute-start | bytes 294920 | tf_op jit(solution)/shard_map/ppermute | solution.py:759
  10.4 4.6 %collective-permute-start.3 = (f32[12,16,128]{2,1,0:T(8,128)S(1)}, f32[12,16,128]{2,1,0:T(8,128)S(1)}, u32[]{:S(2)}, u32[]{:S(2)}) collective-permute-start(f32[12,16,128]{2,1,0:T(8,128)S(1)} %get-tuple-element.61), channel_id=1, source_target_pairs={{1,2},{2,1},{0,3},{3,0},{5,6},{6,5},{4,7},{7,4},{9,10},{10,9},{8,1... | collective-permute-start | bytes 294920 | tf_op jit(solution)/shard_map/ppermute | solution.py:759
  12.2 13.1 %copy-start = (f32[3,384]{1,0:T(4,128)S(1)}, f32[3,384]{1,0:T(4,128)}, u32[]{:S(2)}) copy-start(f32[3,384]{1,0:T(4,128)} %weight_ref.1) | copy-start | bytes 13828
  16.9 5.5 %collective-permute-start.6 = (f32[3,384]{1,0:T(4,128)S(1)}, f32[3,384]{1,0:T(4,128)S(1)}, u32[]{:S(2)}, u32[]{:S(2)}) collective-permute-start(f32[3,384]{1,0:T(4,128)S(1)} %get-tuple-element.70.partial_ref), channel_id=1, source_target_pairs={{0,12},{4,8},{8,4},{12,0},{1,13},{5,9},{9,5},{13,1},{2,14},{6,10},... | collective-permute-start | bytes 13832 | tf_op jit(solution)/shard_map/ppermute | solution.py:765
  20.8 4.5 %collective-permute-start.5 = (f32[3,384]{1,0:T(4,128)S(1)}, f32[3,384]{1,0:T(4,128)S(1)}, u32[]{:S(2)}, u32[]{:S(2)}) collective-permute-start(f32[3,384]{1,0:T(4,128)S(1)} %get-tuple-element.70.partial_ref), channel_id=1, source_target_pairs={{0,8},{4,12},{8,0},{12,4},{1,9},{5,13},{9,1},{13,5},{2,10},{6,14},... | collective-permute-start | bytes 13832 | tf_op jit(solution)/shard_map/ppermute | solution.py:765
  21.4 4.0 %collective-permute-start.4 = (f32[3,384]{1,0:T(4,128)S(1)}, f32[3,384]{1,0:T(4,128)S(1)}, u32[]{:S(2)}, u32[]{:S(2)}) collective-permute-start(f32[3,384]{1,0:T(4,128)S(1)} %get-tuple-element.70.partial_ref), channel_id=1, source_target_pairs={{0,4},{4,0},{8,12},{12,8},{1,5},{5,1},{9,13},{13,9},{2,6},{6,2},{1... | collective-permute-start | bytes 13832 | tf_op jit(solution)/shard_map/ppermute | solution.py:765
